TPU v7x, 32 devices: a whole 2x2x4 slice. The times are simulated.
32 devices in a mesh: seq: 4 (over y, x), fsdp: 8 (over z, core).
Axes of the slice: x: 2, y: 2, z: 4, core: 2. Of those that a mesh axis runs over, the one named last changes fastest.
Arguments:
- tokens: bfloat16 [2, 3072, 2048], P(None, ('seq', 'fsdp')), may hold values from -6 to 6
- cotangent: bfloat16 [2, 3072, 2048], P(None, ('seq', 'fsdp')), may hold values from -6 to 6
- ids: int32 [2, 3072, 4], P(None, ('seq', 'fsdp')), may hold values from 0 to 7, all different within a row; in each aligned block of 96 rows (0 to 95, 96 to 191, ..., all dimensions but the last counted through in order) at most 72 rows name the same one
- deal: int32 [2, 8, 8], replicated, may hold values from 0 to 7, each once within a row
- lengths: int32 [2, 8, 4], replicated, may hold values from 1 to 337, 384 in all within a row
- w_qkv: bfloat16 [2048, 6144], P(('seq', 'fsdp')), may hold values from -0.125 to 0.125
- b_qkv: bfloat16 [6144], P(('seq', 'fsdp')), may hold values from -1.5 to 1.5
- w_out: bfloat16 [2048, 2048], P(('seq', 'fsdp')), may hold values from -0.5 to 0.5
- gain_attn: bfloat16 [2048], P(('seq', 'fsdp')), may hold values from 0.5 to 1.5
- gain_ffn: bfloat16 [2048], P(('seq', 'fsdp')), may hold values from 0.5 to 1.5
- w_router: bfloat16 [2048, 8], P(('seq', 'fsdp')), may hold values from -0.0625 to 0.0625
- w_shared_gate: bfloat16 [2048], P(('seq', 'fsdp')), may hold values from -0.125 to 0.125
- e_gate: bfloat16 [8, 2048, 1408], P('fsdp', 'seq'), may hold values from -0.125 to 0.125
- e_up: bfloat16 [8, 2048, 1408], P('fsdp', 'seq'), may hold values from -0.125 to 0.125
- e_down: bfloat16 [8, 1408, 2048], P('fsdp', None, 'seq'), may hold values from -0.875 to 0.875
- s_gate: bfloat16 [2048, 5632], P('seq', 'fsdp'), may hold values from -0.125 to 0.125
- s_up: bfloat16 [2048, 5632], P('seq', 'fsdp'), may hold values from -0.125 to 0.125
- s_down: bfloat16 [5632, 2048], P('fsdp', 'seq'), may hold values from -0.21875 to 0.21875
Outputs:
- mixed: bfloat16 [2, 3072, 2048], P(None, ('seq', 'fsdp'))
- grad_tokens: float32 [2, 3072, 2048], P(None, ('seq', 'fsdp'))
- grad_w_qkv: float32 [2048, 6144], P(('seq', 'fsdp'))
- grad_b_qkv: float32 [6144], P(('seq', 'fsdp'))
- grad_w_out: float32 [2048, 2048], P(('seq', 'fsdp'))
- grad_gain_attn: float32 [2048], P(('seq', 'fsdp'))
- grad_gain_ffn: float32 [2048], P(('seq', 'fsdp'))
- grad_w_router: float32 [2048, 8], P(('seq', 'fsdp'))
- grad_w_shared_gate: float32 [2048], P(('seq', 'fsdp'))
- grad_e_gate: float32 [8, 2048, 1408], P('fsdp', 'seq')
- grad_e_up: float32 [8, 2048, 1408], P('fsdp', 'seq')
- grad_e_down: float32 [8, 1408, 2048], P('fsdp', None, 'seq')
- grad_s_gate: float32 [2048, 5632], P('seq', 'fsdp')
- grad_s_up: float32 [2048, 5632], P('seq', 'fsdp')
- grad_s_down: float32 [5632, 2048], P('fsdp', 'seq')
Inputs may be any that keep to these rules, and one draw needn't show every extreme that they name: `ids`: within the rows of one device in one micro-batch (aligned blocks of 96 rows) no expert is named by more than 72 rows, a bound that some block reaches; a token names 4 different experts. Each row deal[m, j, :] holds every data group once. Each lengths[m, g, :] sums to 384 and its largest entry is exactly 337.
All inputs are finite; a program needn't handle non-finite values.
Results may differ from a plain program's by a relative error of at most 0.028.
Values may be sent and summed in bfloat16 or wider, within the bound.
A program may use at most 576 MiB of HBM per device.

v0:
```python
import jax
import jax.numpy as jnp
from jax import lax
from jax.sharding import PartitionSpec as P

H = 16
HD = 128
TOP = 4


eps = 1e-06
theta = 1000000.0
masked_score = -1e30


def sigmoid_linear(values):
    return values * jax.nn.sigmoid(values)


def rotary(position, head_size):
    frequency = theta ** (-jnp.arange(0, head_size, 2, dtype=jnp.float32) / head_size)
    angle = position.astype(jnp.float32)[:, None] * frequency[None, :]
    angle = jnp.concatenate([angle, angle], axis=1)
    return (jnp.cos(angle), jnp.sin(angle))


def turn(values):
    half = values.shape[-1] // 2
    return jnp.concatenate([-values[..., half:], values[..., :half]], axis=-1)


def turn_back(values):
    half = values.shape[-1] // 2
    return jnp.concatenate([values[..., half:], -values[..., :half]], axis=-1)


def rms_forward(values):
    inverse = lax.rsqrt(jnp.mean(values * values, axis=-1, keepdims=True) + eps)
    return (values * inverse, inverse)


def rms_backward(grad_normed, unit, inverse, gain):
    scaled = grad_normed * gain
    grad_gain = jnp.sum(grad_normed * unit, axis=0)
    grad_values = inverse * (scaled - unit * jnp.mean(scaled * unit, axis=-1, keepdims=True))
    return (grad_values, grad_gain)


def allowed_mask(segment, first, count):
    rows = first + jnp.arange(count, dtype=jnp.int32)
    columns = jnp.arange(segment.shape[0], dtype=jnp.int32)
    return (segment[:, None] == segment[None, :]) & (columns[None, :] <= rows[:, None])


def attend_forward(query, key, value, segment, block):
    scale = query.shape[-1] ** (-0.5)

    def one_block(first):
        raw = jnp.einsum("qhd,khd->hqk", query, key, preferred_element_type=jnp.float32)
        scores = jnp.where(allowed_mask(segment, first, block)[None], raw * scale, masked_score)
        top = jnp.max(scores, axis=-1, keepdims=True)
        weights = jnp.exp(scores - top)
        total = jnp.sum(weights, axis=-1, keepdims=True)
        chance = (weights / total).astype(jnp.bfloat16)
        context = jnp.einsum("hqk,khd->qhd", chance, value, preferred_element_type=jnp.float32)
        return (context.astype(jnp.bfloat16), (top + jnp.log(total))[..., 0])

    firsts = jnp.arange(0, query.shape[0], block, dtype=jnp.int32)
    context, logsum = lax.map(one_block, firsts)
    return (context.reshape(query.shape), logsum, firsts)


def attend_backward(query, key, value, segment, logsum, firsts, grad_context, block):
    scale = query.shape[-1] ** (-0.5)

    def one_block(carry, inputs):
        grad_key, grad_value = carry
        first, block_logsum = inputs
        raw = jnp.einsum("qhd,khd->hqk", query, key, preferred_element_type=jnp.float32)
        scores = jnp.where(allowed_mask(segment, first, block)[None], raw * scale, masked_score)
        chance = jnp.exp(scores - block_logsum[..., None])
        chance_low = chance.astype(jnp.bfloat16)
        grad_chance = jnp.einsum(
            "qhd,khd->hqk", grad_context, value, preferred_element_type=jnp.float32
        )
        delta = jnp.sum(chance * grad_chance, axis=-1, keepdims=True)
        grad_raw = (chance * (grad_chance - delta) * scale).astype(jnp.bfloat16)
        grad_query = jnp.einsum("hqk,khd->qhd", grad_raw, key, preferred_element_type=jnp.float32)
        grad_key = grad_key + jnp.einsum(
            "hqk,qhd->khd", grad_raw, query, preferred_element_type=jnp.float32
        )
        grad_value = grad_value + jnp.einsum(
            "hqk,qhd->khd", chance_low, grad_context, preferred_element_type=jnp.float32
        )
        return ((grad_key, grad_value), grad_query)

    zero_filled = jnp.zeros(key.shape, jnp.float32)
    (grad_key, grad_value), grad_query = lax.scan(
        one_block, (zero_filled, zero_filled), (firsts, logsum)
    )
    return (grad_query.reshape(query.shape), grad_key, grad_value)


def swiglu_grads(grad_act, gate_pre, up_pre):
    gate_sig = jax.nn.sigmoid(gate_pre)
    grad_gate = (grad_act * up_pre * gate_sig * (1.0 + gate_pre * (1.0 - gate_sig))).astype(
        jnp.bfloat16
    )
    grad_up = (grad_act * gate_pre * gate_sig).astype(jnp.bfloat16)
    return (grad_gate, grad_up)


def shards(
    tokens,
    cotangent,
    ids,
    deal,
    lengths,
    w_qkv,
    b_qkv,
    w_out,
    gain_attn,
    gain_ffn,
    w_router,
    w_shared_gate,
    e_gate,
    e_up,
    e_down,
    s_gate,
    s_up,
    s_down,
):
    seq_size = lax.axis_size("seq")
    shard_count = lax.axis_size("fsdp")
    seq_index = lax.axis_index("seq")
    shard_index = lax.axis_index("fsdp")
    micro_count, tok_rows, width = tokens.shape
    piece_rows = tok_rows // shard_count
    pack_rows = tok_rows * seq_size
    block = min(pack_rows, 512)
    local_heads = H // seq_size
    expert_count = w_router.shape[1]
    local_experts = e_gate.shape[0]
    capacity = min(tok_rows, 3 * tok_rows * TOP // (2 * expert_count))
    slot_count = expert_count * capacity
    single_precision = jnp.float32
    bf16 = jnp.bfloat16
    qkv_full, bias_full, out_full, gain_first, gain_second, router_full, shared_vec = (
        lax.all_gather(w_qkv, ("seq", "fsdp"), axis=0, tiled=True),
        lax.all_gather(b_qkv, ("seq", "fsdp"), axis=0, tiled=True),
        lax.all_gather(w_out, ("seq", "fsdp"), axis=0, tiled=True),
        lax.all_gather(gain_attn, ("seq", "fsdp"), axis=0, tiled=True),
        lax.all_gather(gain_ffn, ("seq", "fsdp"), axis=0, tiled=True),
        lax.all_gather(w_router, ("seq", "fsdp"), axis=0, tiled=True),
        lax.all_gather(w_shared_gate, ("seq", "fsdp"), axis=0, tiled=True),
    )
    gate_full, complete_up_weight, down_full, sgate_full, sup_full, sdown_full = (
        lax.all_gather(e_gate, "seq", axis=1, tiled=True),
        lax.all_gather(e_up, "seq", axis=1, tiled=True),
        lax.all_gather(e_down, "seq", axis=2, tiled=True),
        lax.all_gather(s_gate, "seq", axis=0, tiled=True),
        lax.all_gather(s_up, "seq", axis=0, tiled=True),
        lax.all_gather(s_down, "seq", axis=1, tiled=True),
    )
    acc_qkv = jnp.zeros((width, 3 * width), single_precision)
    acc_bias = jnp.zeros((3 * width,), single_precision)
    acc_out = jnp.zeros((width, width), single_precision)
    acc_gain_attn = jnp.zeros((width,), single_precision)
    acc_gain_ffn = jnp.zeros((width,), single_precision)
    acc_router = jnp.zeros((width, expert_count), single_precision)
    acc_shared_vec = jnp.zeros((width,), single_precision)
    acc_egate = jnp.zeros(gate_full.shape, single_precision)
    expert_up_accumulator = jnp.zeros(complete_up_weight.shape, single_precision)
    acc_edown = jnp.zeros(down_full.shape, single_precision)
    acc_sgate = jnp.zeros(sgate_full.shape, single_precision)
    acc_sup = jnp.zeros(sup_full.shape, single_precision)
    acc_sdown = jnp.zeros(sdown_full.shape, single_precision)
    gain_before = gain_first.astype(single_precision)
    gain_after = gain_second.astype(single_precision)
    rows_local = jnp.arange(tok_rows, dtype=jnp.int32)
    start_shift = rows_local // shard_count
    piece = rows_local % shard_count
    spots = jnp.arange(pack_rows, dtype=jnp.int32)
    assign_index = jnp.arange(tok_rows * TOP, dtype=jnp.int32)
    slot_index = jnp.arange(slot_count, dtype=jnp.int32)
    expert_index = jnp.arange(expert_count, dtype=jnp.int32)
    mixed_parts = []
    input_grads = []
    for micro in range(micro_count):
        deal_row = deal[micro, shard_index]
        inverse_deal = jnp.argsort(deal_row)
        length_table = lengths[micro]
        ends = jnp.cumsum(length_table, axis=1)
        group = deal_row[piece]
        place = (seq_index * piece_rows + start_shift) * shard_count + shard_index
        row_ends = ends[group]
        row_lengths = length_table[group]
        start = jnp.sum(jnp.where(row_ends <= place[:, None], row_lengths, 0), axis=1)
        cosine, sine = rotary(place - start, HD)
        cos_rows = cosine[:, None, :]
        sin_rows = sine[:, None, :]
        own_ends = ends[shard_index]
        segment = jnp.sum((own_ends[None, :] <= spots[:, None]).astype(jnp.int32), axis=1)
        input_rows = tokens[micro].astype(single_precision)
        unit_first, inverse_first = rms_forward(input_rows)
        normed = (unit_first * gain_before).astype(bf16)
        projected = jnp.dot(
            normed, qkv_full, preferred_element_type=single_precision
        ) + bias_full.astype(single_precision)
        projected = projected.reshape(tok_rows, 3, H, HD)
        rotated_query = projected[:, 0] * cos_rows + turn(projected[:, 0]) * sin_rows
        turned_key = projected[:, 1] * cos_rows + turn(projected[:, 1]) * sin_rows
        moved = jnp.stack([rotated_query, turned_key, projected[:, 2]], axis=1).astype(bf16)
        send_heads = jnp.take(
            moved.reshape(piece_rows, shard_count, 3, H, HD), inverse_deal, axis=1
        )
        heads = lax.all_to_all(
            lax.all_to_all(send_heads, "seq", split_axis=3, concat_axis=0, tiled=True),
            "fsdp",
            split_axis=1,
            concat_axis=1,
            tiled=True,
        )
        heads = heads.reshape(pack_rows, 3, local_heads, HD)
        query = heads[:, 0]
        key = heads[:, 1]
        value = heads[:, 2]
        context, logsum, firsts = attend_forward(query, key, value, segment, block)
        returned = lax.all_to_all(
            lax.all_to_all(
                context.reshape(seq_size * piece_rows, shard_count, local_heads, HD),
                "seq",
                split_axis=0,
                concat_axis=2,
                tiled=True,
            ),
            "fsdp",
            split_axis=1,
            concat_axis=1,
            tiled=True,
        )
        context_rows = jnp.take(returned, deal_row, axis=1).reshape(tok_rows, width)
        hidden = input_rows + jnp.dot(
            context_rows, out_full, preferred_element_type=single_precision
        )
        unit_second, inverse_second = rms_forward(hidden)
        normed2 = (unit_second * gain_after).astype(bf16)
        logits = jnp.dot(normed2, router_full, preferred_element_type=single_precision)
        shifted = jnp.exp(logits - jnp.max(logits, axis=-1, keepdims=True))
        router = shifted / jnp.sum(shifted, axis=-1, keepdims=True)
        chosen = ids[micro]
        onehot = (chosen[:, :, None] == expert_index[None, None, :]).astype(single_precision)
        gates = jnp.sum(router[:, None, :] * onehot, axis=2)
        sigma = jax.nn.sigmoid(
            jnp.dot(normed2, shared_vec, preferred_element_type=single_precision)
        )
        grad_out = cotangent[micro].astype(single_precision)
        grad_shared_out = (sigma[:, None] * grad_out).astype(bf16)
        flat_onehot = onehot.reshape(tok_rows * TOP, expert_count).astype(jnp.int32)
        before = jnp.cumsum(flat_onehot, axis=0) - flat_onehot
        slot = jnp.sum(before * flat_onehot, axis=1)
        target = chosen.reshape(-1) * capacity + slot
        match = target[None, :] == slot_index[:, None]
        owner = jnp.sum(jnp.where(match, assign_index[None, :] + 1, 0), axis=1) - 1
        filled = owner >= 0
        owner_row = jnp.maximum(owner, 0)
        source_token = owner_row // TOP
        routed_send = jnp.where(
            filled[:, None], jnp.take(normed2, source_token, axis=0), jnp.zeros((), bf16)
        )
        routed_send = routed_send.reshape(shard_count, local_experts * capacity, width)
        grad_picked = (
            (gates[:, :, None] * grad_out[:, None, :]).astype(bf16).reshape(tok_rows * TOP, width)
        )
        routed_grad_send = jnp.where(
            filled[:, None], jnp.take(grad_picked, owner_row, axis=0), jnp.zeros((), bf16)
        )
        routed_grad_send = routed_grad_send.reshape(shard_count, local_experts * capacity, width)
        routed_in, routed_grad_in = (
            lax.all_to_all(routed_send, "fsdp", split_axis=0, concat_axis=0, tiled=True),
            lax.all_to_all(routed_grad_send, "fsdp", split_axis=0, concat_axis=0, tiled=True),
        )
        rows_per_expert = jnp.swapaxes(
            routed_in.reshape(shard_count, local_experts, capacity, width), 0, 1
        ).reshape(local_experts, shard_count * capacity, width)
        grad_rows = jnp.swapaxes(
            routed_grad_in.reshape(shard_count, local_experts, capacity, width), 0, 1
        ).reshape(local_experts, shard_count * capacity, width)
        gate_pre = jnp.einsum(
            "erd,edf->erf", rows_per_expert, gate_full, preferred_element_type=single_precision
        )
        up_pre = jnp.einsum(
            "erd,edf->erf",
            rows_per_expert,
            complete_up_weight,
            preferred_element_type=single_precision,
        )
        activation = (sigmoid_linear(gate_pre) * up_pre).astype(bf16)
        expert_out = jnp.einsum(
            "erf,efd->erd", activation, down_full, preferred_element_type=single_precision
        ).astype(bf16)
        grad_act = jnp.einsum(
            "erd,efd->erf", grad_rows, down_full, preferred_element_type=single_precision
        )
        grad_gate, grad_up = swiglu_grads(grad_act, gate_pre, up_pre)
        acc_egate = acc_egate + jnp.einsum(
            "erd,erf->edf", rows_per_expert, grad_gate, preferred_element_type=single_precision
        )
        expert_up_accumulator = expert_up_accumulator + jnp.einsum(
            "erd,erf->edf", rows_per_expert, grad_up, preferred_element_type=single_precision
        )
        acc_edown = acc_edown + jnp.einsum(
            "erf,erd->efd", activation, grad_rows, preferred_element_type=single_precision
        )
        grad_expert_in = (
            jnp.einsum(
                "erf,edf->erd", grad_gate, gate_full, preferred_element_type=single_precision
            )
            + jnp.einsum(
                "erf,edf->erd", grad_up, complete_up_weight, preferred_element_type=single_precision
            )
        ).astype(bf16)
        expert_return_rows = jnp.swapaxes(
            expert_out.reshape(local_experts, shard_count, capacity, width), 0, 1
        ).reshape(shard_count, local_experts * capacity, width)
        routed_grad_reply = jnp.swapaxes(
            grad_expert_in.reshape(local_experts, shard_count, capacity, width), 0, 1
        ).reshape(shard_count, local_experts * capacity, width)
        routed_back, routed_dx = (
            lax.all_to_all(expert_return_rows, "fsdp", split_axis=0, concat_axis=0, tiled=True),
            lax.all_to_all(routed_grad_reply, "fsdp", split_axis=0, concat_axis=0, tiled=True),
        )
        picked = (
            jnp.take(routed_back.reshape(slot_count, width), target, axis=0)
            .reshape(tok_rows, TOP, width)
            .astype(single_precision)
        )
        routed = jnp.sum(gates[:, :, None] * picked, axis=1)
        routed_grad_in_rows = (
            jnp.take(routed_dx.reshape(slot_count, width), target, axis=0)
            .reshape(tok_rows, TOP, width)
            .astype(single_precision)
        )
        shared_rows, shared_grad_rows = (
            lax.all_gather(normed2, "fsdp", axis=0, tiled=True),
            lax.all_gather(grad_shared_out, "fsdp", axis=0, tiled=True),
        )
        sgate_pre = jnp.dot(shared_rows, sgate_full, preferred_element_type=single_precision)
        sup_pre = jnp.dot(shared_rows, sup_full, preferred_element_type=single_precision)
        shared_act = (sigmoid_linear(sgate_pre) * sup_pre).astype(bf16)
        shared_reply = jnp.dot(shared_act, sdown_full, preferred_element_type=single_precision)
        grad_shared_act = jnp.einsum(
            "rd,fd->rf", shared_grad_rows, sdown_full, preferred_element_type=single_precision
        )
        grad_sgate, grad_sup = swiglu_grads(grad_shared_act, sgate_pre, sup_pre)
        acc_sgate = acc_sgate + jnp.einsum(
            "rd,rf->df", shared_rows, grad_sgate, preferred_element_type=single_precision
        )
        acc_sup = acc_sup + jnp.einsum(
            "rd,rf->df", shared_rows, grad_sup, preferred_element_type=single_precision
        )
        acc_sdown = acc_sdown + jnp.einsum(
            "rf,rd->fd", shared_act, shared_grad_rows, preferred_element_type=single_precision
        )
        shared_grad_reply = jnp.einsum(
            "rf,df->rd", grad_sgate, sgate_full, preferred_element_type=single_precision
        ) + jnp.einsum("rf,df->rd", grad_sup, sup_full, preferred_element_type=single_precision)
        shared_out, shared_dx = (
            lax.psum_scatter(shared_reply, "fsdp", scatter_dimension=0, tiled=True),
            lax.psum_scatter(shared_grad_reply, "fsdp", scatter_dimension=0, tiled=True),
        )
        result = hidden + routed + sigma[:, None] * shared_out
        mixed_parts.append(result.astype(bf16))
        grad_normed2 = shared_dx + jnp.sum(routed_grad_in_rows, axis=1)
        grad_gates = jnp.sum(grad_out[:, None, :] * picked, axis=2)
        grad_router = jnp.sum(grad_gates[:, :, None] * onehot, axis=1)
        grad_logits = (
            router * (grad_router - jnp.sum(router * grad_router, axis=-1, keepdims=True))
        ).astype(bf16)
        acc_router = acc_router + jnp.einsum(
            "rd,re->de", normed2, grad_logits, preferred_element_type=single_precision
        )
        grad_normed2 = grad_normed2 + jnp.einsum(
            "re,de->rd", grad_logits, router_full, preferred_element_type=single_precision
        )
        grad_sigma = jnp.sum(grad_out * shared_out, axis=1)
        grad_gate_logit = grad_sigma * sigma * (1.0 - sigma)
        acc_shared_vec = acc_shared_vec + jnp.dot(
            grad_gate_logit, normed2.astype(single_precision), precision=lax.Precision.HIGHEST
        )
        grad_normed2 = (
            grad_normed2 + grad_gate_logit[:, None] * shared_vec.astype(single_precision)[None, :]
        )
        grad_from_norm, grad_gain_second = rms_backward(
            grad_normed2, unit_second, inverse_second, gain_after
        )
        acc_gain_ffn = acc_gain_ffn + grad_gain_second
        grad_hidden = grad_out + grad_from_norm
        grad_attn = grad_hidden.astype(bf16)
        acc_out = acc_out + jnp.einsum(
            "rc,rd->cd", context_rows, grad_attn, preferred_element_type=single_precision
        )
        grad_context = jnp.einsum(
            "rd,cd->rc", grad_attn, out_full, preferred_element_type=single_precision
        ).astype(bf16)
        grad_send = jnp.take(
            grad_context.reshape(piece_rows, shard_count, H, HD), inverse_deal, axis=1
        )
        grad_heads = lax.all_to_all(
            lax.all_to_all(grad_send, "seq", split_axis=2, concat_axis=0, tiled=True),
            "fsdp",
            split_axis=1,
            concat_axis=1,
            tiled=True,
        )
        grad_heads = grad_heads.reshape(pack_rows, local_heads, HD)
        grad_query, grad_key, grad_value = attend_backward(
            query, key, value, segment, logsum, firsts, grad_heads, block
        )
        grad_moved = jnp.stack([grad_query, grad_key, grad_value], axis=1).astype(bf16)
        grad_returned = lax.all_to_all(
            lax.all_to_all(
                grad_moved.reshape(seq_size * piece_rows, shard_count, 3, local_heads, HD),
                "seq",
                split_axis=0,
                concat_axis=3,
                tiled=True,
            ),
            "fsdp",
            split_axis=1,
            concat_axis=1,
            tiled=True,
        )
        grad_moved_rows = (
            jnp.take(grad_returned, deal_row, axis=1)
            .reshape(tok_rows, 3, H, HD)
            .astype(single_precision)
        )
        grad_turned_query = grad_moved_rows[:, 0] * cos_rows + turn_back(
            grad_moved_rows[:, 0] * sin_rows
        )
        grad_turned_key = grad_moved_rows[:, 1] * cos_rows + turn_back(
            grad_moved_rows[:, 1] * sin_rows
        )
        grad_qkv = (
            jnp.stack([grad_turned_query, grad_turned_key, grad_moved_rows[:, 2]], axis=1)
            .reshape(tok_rows, 3 * width)
            .astype(bf16)
        )
        acc_bias = acc_bias + jnp.sum(grad_qkv.astype(single_precision), axis=0)
        acc_qkv = acc_qkv + jnp.einsum(
            "rd,rc->dc", normed, grad_qkv, preferred_element_type=single_precision
        )
        grad_normed = jnp.einsum(
            "rc,dc->rd", grad_qkv, qkv_full, preferred_element_type=single_precision
        )
        grad_from_first, grad_gain_first = rms_backward(
            grad_normed, unit_first, inverse_first, gain_before
        )
        acc_gain_attn = acc_gain_attn + grad_gain_first
        input_grads.append(grad_hidden + grad_from_first)
    dense_grads = (
        lax.psum_scatter(acc_qkv, ("seq", "fsdp"), scatter_dimension=0, tiled=True),
        lax.psum_scatter(acc_bias, ("seq", "fsdp"), scatter_dimension=0, tiled=True),
        lax.psum_scatter(acc_out, ("seq", "fsdp"), scatter_dimension=0, tiled=True),
        lax.psum_scatter(acc_gain_attn, ("seq", "fsdp"), scatter_dimension=0, tiled=True),
        lax.psum_scatter(acc_gain_ffn, ("seq", "fsdp"), scatter_dimension=0, tiled=True),
        lax.psum_scatter(acc_router, ("seq", "fsdp"), scatter_dimension=0, tiled=True),
        lax.psum_scatter(acc_shared_vec, ("seq", "fsdp"), scatter_dimension=0, tiled=True),
    )
    expert_grads = (
        lax.psum_scatter(
            acc_egate.astype(jnp.bfloat16), "seq", scatter_dimension=1, tiled=True
        ).astype(jnp.float32),
        lax.psum_scatter(
            expert_up_accumulator.astype(jnp.bfloat16), "seq", scatter_dimension=1, tiled=True
        ).astype(jnp.float32),
        lax.psum_scatter(
            acc_edown.astype(jnp.bfloat16), "seq", scatter_dimension=2, tiled=True
        ).astype(jnp.float32),
        lax.psum_scatter(
            acc_sgate.astype(jnp.bfloat16), "seq", scatter_dimension=0, tiled=True
        ).astype(jnp.float32),
        lax.psum_scatter(
            acc_sup.astype(jnp.bfloat16), "seq", scatter_dimension=0, tiled=True
        ).astype(jnp.float32),
        lax.psum_scatter(
            acc_sdown.astype(jnp.bfloat16), "seq", scatter_dimension=1, tiled=True
        ).astype(jnp.float32),
    )
    return (
        jnp.stack(mixed_parts),
        jnp.stack(input_grads),
        dense_grads[0],
        dense_grads[1],
        dense_grads[2],
        dense_grads[3],
        dense_grads[4],
        dense_grads[5],
        dense_grads[6],
        expert_grads[0],
        expert_grads[1],
        expert_grads[2],
        expert_grads[3],
        expert_grads[4],
        expert_grads[5],
    )


def solution(mesh):
    in_specs = (
        P(None, ("seq", "fsdp"), None),
        P(None, ("seq", "fsdp"), None),
        P(None, ("seq", "fsdp"), None),
        P(),
        P(),
        P(("seq", "fsdp"), None),
        P(("seq", "fsdp")),
        P(("seq", "fsdp"), None),
        P(("seq", "fsdp")),
        P(("seq", "fsdp")),
        P(("seq", "fsdp"), None),
        P(("seq", "fsdp")),
        P("fsdp", "seq", None),
        P("fsdp", "seq", None),
        P("fsdp", None, "seq"),
        P("seq", "fsdp"),
        P("seq", "fsdp"),
        P("fsdp", "seq"),
    )
    out_specs = (
        P(None, ("seq", "fsdp"), None),
        P(None, ("seq", "fsdp"), None),
        P(("seq", "fsdp"), None),
        P(("seq", "fsdp")),
        P(("seq", "fsdp"), None),
        P(("seq", "fsdp")),
        P(("seq", "fsdp")),
        P(("seq", "fsdp"), None),
        P(("seq", "fsdp")),
        P("fsdp", "seq", None),
        P("fsdp", "seq", None),
        P("fsdp", None, "seq"),
        P("seq", "fsdp"),
        P("seq", "fsdp"),
        P("fsdp", "seq"),
    )
    return jax.shard_map(shards, mesh=mesh, in_specs=in_specs, out_specs=out_specs, check_vma=False)
```

profile of v0, /device:TPU:0, one launch (start us, length us, event | category | flops | bytes accessed | tf_op | source)
XLA Modules:
  0.0 2414.9 jit_solution(833450879040653396)
XLA Ops:
  25.8 43.1 %all-reduce.9 = (bf16[6144]{0:T(1024)(128)(2,1)S(1)}, bf16[2048]{0:T(1024)(128)(2,1)S(1)}, bf16[2048]{0:T(1024)(128)(2,1)S(1)}, bf16[2048]{0:T(1024)(128)(2,1)S(1)}) all-reduce(bf16[6144]{0:T(1024)(128)(2,1)S(1)} %dynamic-update-slice.1, bf16[2048]{0:T(1024)(128)(2,1)S(1)} %dynamic-update-slice, ...), channel_id=1, replica_groups=mesh['seq'=4,'fsdp'=8] {'seq','fsdp'}, use_global_device_ids=true, to_apply=%add.1 | all-reduce | flops 12288 | bytes 49152
  72.1 97.1 %all-gather.14.cloned.1.call-done = bf16[2048,6144]{1,0:T(8,128)(2,1)} async-done(((bf16[64,6144]{1,0:T(8,128)(2,1)}), bf16[2048,6144]{1,0:T(8,128)(2,1)}) %all-gather.14.cloned.1.call-update) | async-done | bytes 25165840 | tf_op jit(solution)/shard_map/all_gather | solution.py:149
  217.0 16.5 all-to-all-done
  238.7 36.4 %all-to-all-done.7 = bf16[48,8,3,4,128]{4,0,3,2,1:T(8,128)(2,1)S(1)} async-done(((bf16[48,8,3,4,128]{4,0,3,2,1:T(8,128)(2,1)}), bf16[48,8,3,4,128]{4,0,3,2,1:T(8,128)(2,1)S(1)}, u32[]{:S(2)}, u32[]{:S(2)}) %all-to-all-start.7) | async-done | bytes 1179680 | tf_op jit(solution)/shard_map/all_to_all | solution.py:217
  284.9 23.1 all-to-all-done.1
  337.1 11.7 all-to-all-done.9
  381.9 28.8 %all-gather.24.cloned.1.call-done = bf16[768,2048]{1,0:T(8,128)(2,1)} async-done(((bf16[96,2048]{1,0:T(8,128)(2,1)}), bf16[768,2048]{1,0:T(8,128)(2,1)}) %all-gather.24.cloned.1.call-update) | async-done | bytes 3145744 | tf_op jit(solution)/shard_map/all_gather | solution.py:345
  417.4 35.5 %all-gather.28.cloned.1.call-done = bf16[2048,704]{0,1:T(8,128)(2,1)} async-done(((bf16[512,704]{0,1:T(8,128)(2,1)}), bf16[2048,704]{0,1:T(8,128)(2,1)}) %all-gather.28.cloned.1.call-update) | async-done | bytes 2883600 | tf_op jit(solution)/shard_map/all_gather | solution.py:162
  458.5 37.8 %all-gather.30.cloned.1.call-done = bf16[704,2048]{1,0:T(8,128)(2,1)} async-done(((bf16[704,512]{1,0:T(8,128)(2,1)}), bf16[704,2048]{1,0:T(8,128)(2,1)}) %all-gather.30.cloned.1.call-update) | async-done | bytes 2883600 | tf_op jit(solution)/shard_map/all_gather | solution.py:163
  496.3 40.5 %all-gather.34.cloned.1.call-done = bf16[768,2048]{1,0:T(8,128)(2,1)} async-done(((bf16[96,2048]{1,0:T(8,128)(2,1)}), bf16[768,2048]{1,0:T(8,128)(2,1)}) %all-gather.34.cloned.1.call-update) | async-done | bytes 3145744 | tf_op jit(solution)/shard_map/all_gather | solution.py:346
  551.2 24.5 %all-gather.32.cloned.1.call-done = bf16[768,2048]{1,0:T(8,128)(2,1)} async-done(((bf16[96,2048]{1,0:T(8,128)(2,1)}), bf16[768,2048]{1,0:T(8,128)(2,1)}) %all-gather.32.cloned.1.call-update) | async-done | bytes 3145744 | tf_op jit(solution)/shard_map/all_gather | solution.py:345
  585.3 29.8 %all-gather.36.cloned.1.call-done = bf16[768,2048]{1,0:T(8,128)(2,1)} async-done(((bf16[96,2048]{1,0:T(8,128)(2,1)}), bf16[768,2048]{1,0:T(8,128)(2,1)}) %all-gather.36.cloned.1.call-update) | async-done | bytes 3145744 | tf_op jit(solution)/shard_map/all_gather | solution.py:346
  657.8 49.5 %all-to-all-done.4 = bf16[8,72,2048]{2,1,0:T(8,128)(2,1)} async-done(((bf16[8,72,2048]{2,1,0:T(8,128)(2,1)}), bf16[8,72,2048]{2,1,0:T(8,128)(2,1)}, u32[]{:S(2)}, u32[]{:S(2)}) %all-to-all-start.4) | async-done | bytes 2359328 | tf_op jit(solution)/shard_map/all_to_all | solution.py:280
  729.7 19.5 all-gather.20.cloned.1.call-done
  759.7 56.9 %all-gather.22.cloned.1.call-done = bf16[1,1408,2048]{2,1,0:T(8,128)(2,1)} async-done(((bf16[1,1408,512]{2,1,0:T(8,128)(2,1)}), bf16[1,1408,2048]{2,1,0:T(8,128)(2,1)}) %all-gather.22.cloned.1.call-update) | async-done | bytes 5767184 | tf_op jit(solution)/shard_map/all_gather | solution.py:160
  826.4 16.4 all-to-all-start.5
  866.0 64.5 %all-to-all-done.5 = bf16[8,72,2048]{2,1,0:T(8,128)(2,1)S(1)} async-done(((bf16[8,72,2048]{2,1,0:T(8,128)(2,1)}), bf16[8,72,2048]{2,1,0:T(8,128)(2,1)S(1)}, u32[]{:S(2)}, u32[]{:S(2)}) %all-to-all-start.5) | async-done | bytes 2359328 | tf_op jit(solution)/shard_map/all_to_all | solution.py:330
  935.1 119.2 %all-gather = bf16[32,64,8]{1,2,0:T(8,128)(2,1)S(1)} all-gather(bf16[1,64,8]{1,2,0:T(8,128)(2,1)S(1)} %bitcast.732), channel_id=1, replica_groups=mesh['seq'=4,'fsdp'=8] {'seq','fsdp'}, dimensions={0}, use_global_device_ids=true | all-gather | bytes 33792 | tf_op jit(solution)/shard_map/all_gather | solution.py:154
  1149.8 74.5 %all-to-all-done.12 = bf16[8,72,2048]{2,1,0:T(8,128)(2,1)} async-done(((bf16[8,72,2048]{2,1,0:T(8,128)(2,1)}), bf16[8,72,2048]{2,1,0:T(8,128)(2,1)}, u32[]{:S(2)}, u32[]{:S(2)}) %all-to-all-start.12) | async-done | bytes 2359328 | tf_op jit(solution)/shard_map/all_to_all | solution.py:281
  1239.5 50.4 %all-to-all-done.18 = bf16[8,72,2048]{2,1,0:T(8,128)(2,1)S(1)} async-done(((bf16[8,72,2048]{2,1,0:T(8,128)(2,1)}), bf16[8,72,2048]{2,1,0:T(8,128)(2,1)S(1)}, u32[]{:S(2)}, u32[]{:S(2)}) %all-to-all-start.18) | async-done | bytes 2359328 | tf_op jit(solution)/shard_map/all_to_all | solution.py:281
  1381.8 29.9 %all-to-all-done.13 = bf16[8,72,2048]{2,1,0:T(8,128)(2,1)S(1)} async-done(((bf16[8,72,2048]{2,1,0:T(8,128)(2,1)}), bf16[8,72,2048]{2,1,0:T(8,128)(2,1)S(1)}, u32[]{:S(2)}, u32[]{:S(2)}) %all-to-all-start.13) | async-done | bytes 2359328 | tf_op jit(solution)/shard_map/all_to_all | solution.py:331
  1431.0 39.9 %all-to-all-done.19 = bf16[8,72,2048]{2,1,0:T(8,128)(2,1)} async-done(((bf16[8,72,2048]{2,1,0:T(8,128)(2,1)}), bf16[8,72,2048]{2,1,0:T(8,128)(2,1)}, u32[]{:S(2)}, u32[]{:S(2)}) %all-to-all-start.19) | async-done | bytes 2359328 | tf_op jit(solution)/shard_map/all_to_all | solution.py:331
  1641.3 14.0 all-to-all-done.22
  1661.3 27.9 %all-to-all-done.17 = bf16[12,8,3,16,128]{4,3,2,0,1:T(8,128)(2,1)S(1)} async-done(((bf16[12,8,3,16,128]{4,3,2,0,1:T(8,128)(2,1)}), bf16[12,8,3,16,128]{4,3,2,0,1:T(8,128)(2,1)S(1)}, u32[]{:S(2)}, u32[]{:S(2)}) %all-to-all-start.17) | async-done | bytes 1179680 | tf_op jit(solution)/shard_map/all_to_all | solution.py:421
  1695.3 27.7 %all-to-all-done.23 = bf16[12,8,3,16,128]{4,3,2,0,1:T(8,128)(2,1)} async-done(((bf16[12,8,3,16,128]{4,3,2,0,1:T(8,128)(2,1)}), bf16[12,8,3,16,128]{4,3,2,0,1:T(8,128)(2,1)}, u32[]{:S(2)}, u32[]{:S(2)}) %all-to-all-start.23) | async-done | bytes 1179680 | tf_op jit(solution)/shard_map/all_to_all | solution.py:421
  1737.7 21.4 fusion.100
  1759.1 33.0 %convolution_add_fusion = f32[2048,6144]{1,0:T(8,128)} fusion(f32[2048,6144]{1,0:T(8,128)} %fusion.100, bf16[12,8,48,128]{3,2,1,0:T(8,128)(2,1)S(1)} %bitcast.661, f32[96]{0:T(128)S(1)} %copy-done.81, f32[2048]{0:T(1024)S(1)} %copy-done.50, bf16[2,96,2048]{2,1,0:T(8,128)(2,1)S(1)} %copy-done.7), kind=kOutput, calls=%fused_computation.22 | convolution fusion | flops 2429288448 | bytes 102244864 | tf_op jit(solution)/shard_map/rd,rc->dc/dot_general | solution.py:451
  1805.0 13.7 fusion.98
  1818.8 14.5 fusion.148
  1833.4 43.1 %all-reduce.8 = (f32[6144]{0:T(1024)S(1)}, f32[2048]{0:T(1024)S(1)}, f32[2048]{0:T(1024)S(1)}, f32[2048]{0:T(1024)S(1)}) all-reduce(f32[6144]{0:T(1024)S(1)} %bitcast.725, f32[2048]{0:T(1024)S(1)} %add.537, f32[2048]{0:T(1024)S(1)} %copy-done.79, f32[2048]{0:T(1024)S(1)} %copy-done.78), channel_id=7, replica_groups=mesh['seq'=4,'fsdp'=8] {'seq','fsdp'}, use_global_device_ids=true, to_apply=%region_55.61.clone | all-reduce | flops 12288 | bytes 98304
  1891.4 79.4 %reduce-scatter.26.cloned.1.call-done = f32[64,2048]{1,0:T(8,128)} async-done(((f32[2048,2048]{1,0:T(8,128)}), f32[64,2048]{1,0:T(8,128)}) %reduce-scatter.26.cloned.1.call-update) | async-done | bytes 524304 | tf_op jit(solution)/shard_map/reduce_scatter | solution.py:465
  1970.8 437.3 %reduce-scatter.24.cloned.1.call-done = f32[64,6144]{1,0:T(8,128)} async-done(((f32[2048,6144]{1,0:T(8,128)}), f32[64,6144]{1,0:T(8,128)}) %reduce-scatter.24.cloned.1.call-update) | async-done | bytes 1572880 | tf_op jit(solution)/shard_map/reduce_scatter | solution.py:463
  (743 shorter events, 740.1 us)
Async XLA Ops:
  7.2 162.0 %all-gather.14.cloned.1.call-start = ((), (), s32[]{:S(2)}) async-start(), calls=%async_computation.37 | async-start | bytes 25952256 | tf_op jit(solution)/shard_map/all_gather | solution.py:149
  8.0 357.6 %all-gather.16.cloned.1.call-start = ((), (), s32[]{:S(2)}) async-start(), calls=%async_computation.38 | async-start | bytes 8650752 | tf_op jit(solution)/shard_map/all_gather | solution.py:151
  278.7 103.3 %all-gather.26.cloned.1.call-start = ((), (), s32[]{:S(2)}) async-start(), calls=%async_computation.43 | async-start | bytes 3604480 | tf_op jit(solution)/shard_map/all_gather | solution.py:161
  374.2 78.8 %all-gather.28.cloned.1.call-start = ((), (), s32[]{:S(2)}) async-start(), calls=%async_computation.44 | async-start | bytes 3604480 | tf_op jit(solution)/shard_map/all_gather | solution.py:162
  374.8 121.6 %all-gather.30.cloned.1.call-start = ((), (), s32[]{:S(2)}) async-start(), calls=%async_computation.45 | async-start | bytes 3604480 | tf_op jit(solution)/shard_map/all_gather | solution.py:163
  375.4 161.5 %all-gather.34.cloned.1.call-start = ((), (), s32[]{:S(2)}) async-start(), calls=%async_computation.49 | async-start | bytes 3538944 | tf_op jit(solution)/shard_map/all_gather | solution.py:346
  378.0 197.7 %all-gather.32.cloned.1.call-start = ((), (), s32[]{:S(2)}) async-start(), calls=%async_computation.47 | async-start | bytes 3538944 | tf_op jit(solution)/shard_map/all_gather | solution.py:345
  378.8 236.3 %all-gather.36.cloned.1.call-start = ((), (), s32[]{:S(2)}) async-start(), calls=%async_computation.51 | async-start | bytes 3538944 | tf_op jit(solution)/shard_map/all_gather | solution.py:346
  379.5 341.3 %all-gather.18.cloned.1.call-start = ((), (), s32[]{:S(2)}) async-start(), calls=%async_computation.39 | async-start | bytes 7208960 | tf_op jit(solution)/shard_map/all_gather | solution.py:158
  380.1 369.1 %all-gather.20.cloned.1.call-start = ((), (), s32[]{:S(2)}) async-start(), calls=%async_computation.40 | async-start | bytes 7208960 | tf_op jit(solution)/shard_map/all_gather | solution.py:159
  380.8 435.7 %all-gather.22.cloned.1.call-start = ((), (), s32[]{:S(2)}) async-start(), calls=%async_computation.41 | async-start | bytes 7208960 | tf_op jit(solution)/shard_map/all_gather | solution.py:160
  381.4 1123.8 %reduce-scatter.16.cloned.1.call-start = ((), (), s32[]{:S(2)}) async-start(), calls=%async_computation.46 | async-start | bytes 7077888 | tf_op jit(solution)/shard_map/reduce_scatter | solution.py:369
  551.0 954.3 %reduce-scatter.18.cloned.1.call-start = ((), (), s32[]{:S(2)}) async-start(), calls=%async_computation.48 | async-start | bytes 7077888 | tf_op jit(solution)/shard_map/reduce_scatter | solution.py:369
  629.3 877.9 %reduce-scatter.22.cloned.1.call-start = ((), (), s32[]{:S(2)}) async-start(), calls=%async_computation.52 | async-start | bytes 7077888 | tf_op jit(solution)/shard_map/reduce_scatter | solution.py:370
  648.0 59.2 %all-to-all-start.4 = ((bf16[8,72,2048]{2,1,0:T(8,128)(2,1)}), bf16[8,72,2048]{2,1,0:T(8,128)(2,1)}, u32[]{:S(2)}, u32[]{:S(2)}) async-start(bf16[8,72,2048]{2,1,0:T(8,128)(2,1)} %bitcast.44), calls=%async_computation.4 | async-start | bytes 4718592 | tf_op jit(solution)/shard_map/all_to_all | solution.py:280
  707.2 117.7 %all-to-all-start.10 = ((bf16[8,72,2048]{2,1,0:T(8,128)(2,1)}), bf16[8,72,2048]{2,1,0:T(8,128)(2,1)S(1)}, u32[]{:S(2)}, u32[]{:S(2)}) async-start(bf16[8,72,2048]{2,1,0:T(8,128)(2,1)} %bitcast.95), calls=%async_computation.11 | async-start | bytes 4718592 | tf_op jit(solution)/shard_map/all_to_all | solution.py:280
  710.9 797.8 %reduce-scatter.20.cloned.1.call-start = ((), (), s32[]{:S(2)}) async-start(), calls=%async_computation.50 | async-start | bytes 7077888 | tf_op jit(solution)/shard_map/reduce_scatter | solution.py:370
  826.4 104.2 %all-to-all-start.5 = ((bf16[8,72,2048]{2,1,0:T(8,128)(2,1)}), bf16[8,72,2048]{2,1,0:T(8,128)(2,1)S(1)}, u32[]{:S(2)}, u32[]{:S(2)}) async-start(bf16[8,72,2048]{2,1,0:T(8,128)(2,1)} %bitcast.692), calls=%async_computation.5 | async-start | bytes 4718592 | tf_op jit(solution)/shard_map/all_to_all | solution.py:330
  930.5 156.1 %all-to-all-start.11 = ((bf16[8,72,2048]{2,1,0:T(8,128)(2,1)}), bf16[8,72,2048]{2,1,0:T(8,128)(2,1)}, u32[]{:S(2)}, u32[]{:S(2)}) async-start(bf16[8,72,2048]{2,1,0:T(8,128)(2,1)} %bitcast.687), calls=%async_computation.12 | async-start | bytes 4718592 | tf_op jit(solution)/shard_map/all_to_all | solution.py:330
  935.0 857.1 %reduce-scatter.40.cloned.1.call-start = ((), (), s32[]{:S(2)}) async-start(), calls=%async_computation.61 | async-start | bytes 1081344
  1098.2 695.4 %reduce-scatter.38.cloned.1.call-start = ((), (), s32[]{:S(2)}) async-start(), calls=%async_computation.60 | async-start | bytes 3604480 | tf_op jit(solution)/shard_map/reduce_scatter | solution.py:487
  1106.0 690.0 %reduce-scatter.34.cloned.1.call-start = ((), (), s32[]{:S(2)}) async-start(), calls=%async_computation.58 | async-start | bytes 3604480 | tf_op jit(solution)/shard_map/reduce_scatter | solution.py:481
  1126.2 98.1 %all-to-all-start.12 = ((bf16[8,72,2048]{2,1,0:T(8,128)(2,1)}), bf16[8,72,2048]{2,1,0:T(8,128)(2,1)}, u32[]{:S(2)}, u32[]{:S(2)}) async-start(bf16[8,72,2048]{2,1,0:T(8,128)(2,1)} %bitcast.103), calls=%async_computation.15 | async-start | bytes 4718592 | tf_op jit(solution)/shard_map/all_to_all | solution.py:281
  1130.7 667.8 %reduce-scatter.36.cloned.1.call-start = ((), (), s32[]{:S(2)}) async-start(), calls=%async_computation.59 | async-start | bytes 3604480 | tf_op jit(solution)/shard_map/reduce_scatter | solution.py:484
  1224.3 65.7 %all-to-all-start.18 = ((bf16[8,72,2048]{2,1,0:T(8,128)(2,1)}), bf16[8,72,2048]{2,1,0:T(8,128)(2,1)S(1)}, u32[]{:S(2)}, u32[]{:S(2)}) async-start(bf16[8,72,2048]{2,1,0:T(8,128)(2,1)} %bitcast.137), calls=%async_computation.22 | async-start | bytes 4718592 | tf_op jit(solution)/shard_map/all_to_all | solution.py:281
  1227.9 653.8 %reduce-scatter.32.cloned.1.call-start = ((), (), s32[]{:S(2)}) async-start(), calls=%async_computation.57 | async-start | bytes 7208960 | tf_op jit(solution)/shard_map/reduce_scatter | solution.py:478
  1299.7 585.4 %reduce-scatter.30.cloned.1.call-start = ((), (), s32[]{:S(2)}) async-start(), calls=%async_computation.56 | async-start | bytes 7208960 | tf_op jit(solution)/shard_map/reduce_scatter | solution.py:475
  1348.8 62.8 %all-to-all-start.13 = ((bf16[8,72,2048]{2,1,0:T(8,128)(2,1)}), bf16[8,72,2048]{2,1,0:T(8,128)(2,1)S(1)}, u32[]{:S(2)}, u32[]{:S(2)}) async-start(bf16[8,72,2048]{2,1,0:T(8,128)(2,1)} %bitcast.691), calls=%async_computation.16 | async-start | bytes 4718592 | tf_op jit(solution)/shard_map/all_to_all | solution.py:331
  1352.5 535.8 %reduce-scatter.28.cloned.1.call-start = ((), (), s32[]{:S(2)}) async-start(), calls=%async_computation.55 | async-start | bytes 7208960 | tf_op jit(solution)/shard_map/reduce_scatter | solution.py:472
  1411.7 59.2 %all-to-all-start.19 = ((bf16[8,72,2048]{2,1,0:T(8,128)(2,1)}), bf16[8,72,2048]{2,1,0:T(8,128)(2,1)}, u32[]{:S(2)}, u32[]{:S(2)}) async-start(bf16[8,72,2048]{2,1,0:T(8,128)(2,1)} %bitcast.690), calls=%async_computation.23 | async-start | bytes 4718592 | tf_op jit(solution)/shard_map/all_to_all | solution.py:331
  1416.2 554.6 %reduce-scatter.26.cloned.1.call-start = ((), (), s32[]{:S(2)}) async-start(), calls=%async_computation.54 | async-start | bytes 17301504 | tf_op jit(solution)/shard_map/reduce_scatter | solution.py:465
  1693.6 714.5 %reduce-scatter.24.cloned.1.call-start = ((), (), s32[]{:S(2)}) async-start(), calls=%async_computation.53 | async-start | bytes 51904512 | tf_op jit(solution)/shard_map/reduce_scatter | solution.py:463
  (177 other events, 4859.9 us)
Sparse Core Ops, SparseCore 0:
  11.1 158.0 all-gather.13
  172.2 89.1 all-gather.15
  281.4 46.2 all-gather.25
  374.3 36.3 all-gather.23
  412.4 40.5 all-gather.27
  454.6 41.6 all-gather.29
  498.5 38.2 all-gather.33
  538.5 37.1 all-gather.31
  577.9 37.1 all-gather.35
  616.8 64.6 all-gather.17
  683.3 65.7 all-gather.19
  750.9 65.6 all-gather.21
  818.8 104.5 reduce-scatter.15
  925.6 116.7 reduce-scatter.17
  1044.5 75.4 reduce-scatter.21
  1122.1 111.0 reduce-scatter.19
  1235.3 187.5 reduce-scatter.39
  1426.7 37.8 reduce-scatter.37
  1468.5 41.7 reduce-scatter.33
  1514.0 46.7 reduce-scatter.35
  1564.1 76.8 reduce-scatter.31
  1644.3 66.7 reduce-scatter.29
  1714.4 65.7 reduce-scatter.27
  1783.0 187.6 reduce-scatter.25
  1978.9 429.1 reduce-scatter.23
where the time goes:
time: 2430 us; the launch traced here: 2410 us
  waiting for transfers between devices  1420 us (58%)
  matrix products  418 us (17%)
  blocking collectives  205 us (8%)
  local copies, waits for them, and re-layouts  143 us (6%)
  starting transfers between devices  111 us (5%)
  other arithmetic  105 us (4%)
    reduce_scatter x1, waiting for transfers between devices, shards(): lax.psum_scatter(acc_qkv, ('seq', 'fsdp'), scatter_dimension=0, tiled=True)  437 us
    all_to_all x2, waiting for transfers between devices, shards(): lax.all_to_all(routed_grad_send, 'fsdp', split_axis=0, concat_axis=0, til...  125 us
    all_gather x1, blocking collectives, shards(): lax.all_gather(w_router, ('seq', 'fsdp'), axis=0, tiled=True)  119 us
    all_gather x1, waiting for transfers between devices, shards(): lax.all_gather(w_qkv, ('seq', 'fsdp'), axis=0, tiled=True)  97.1 us
    unnamed x2, blocking collectives  86.3 us
    reduce_scatter x1, waiting for transfers between devices, shards(): lax.psum_scatter(acc_out, ('seq', 'fsdp'), scatter_dimension=0, tiled=True)  79.4 us
    all_gather x2, waiting for transfers between devices, shards(): lax.all_gather(grad_shared_out, 'fsdp', axis=0, tiled=True)  70.3 us
    all_to_all x2, waiting for transfers between devices, shards(): lax.all_to_all(routed_grad_reply, 'fsdp', split_axis=0, concat_axis=0, ti...  69.8 us
  transfers between devices with their start and end apart: 49, of which 31 were waited for; matrix products, arithmetic and copies ran while one was open for 27% of the time, Pallas kernels for 0%

commit v1 on v0

v1 whole, which is shorter than its diff:
```python
import jax
import jax.numpy as jnp
from jax import lax
from jax.sharding import PartitionSpec as P

H = 16
HD = 128
TOP = 4
EPS = 1e-06
THETA = 1000000.0
MASKED = -1e30
F32 = jnp.float32
BF16 = jnp.bfloat16

ORDER = ((0, 0), (0, 1), (2, 0), (1, 1), (1, 0), (3, 0), (2, 1), (3, 1))


def dot(a, b):
    return jnp.dot(a, b, preferred_element_type=F32)


def dot_t(a, b):
    return lax.dot_general(a, b, (((0,), (0,)), ((), ())), preferred_element_type=F32)


def dot_nt(a, b):
    return lax.dot_general(a, b, (((1,), (1,)), ((), ())), preferred_element_type=F32)


def turn(u):
    half = u.shape[-1] // 2
    return jnp.concatenate([-u[..., half:], u[..., :half]], axis=-1)


def turn_back(u):
    half = u.shape[-1] // 2
    return jnp.concatenate([u[..., half:], -u[..., :half]], axis=-1)


def rms_forward(values):
    inverse = lax.rsqrt(jnp.mean(values * values, axis=-1, keepdims=True) + EPS)
    return values * inverse, inverse


def rms_backward(grad, unit, inverse, gain):
    scaled = grad * gain
    grad_gain = jnp.sum(grad * unit, axis=tuple(range(grad.ndim - 1)))
    return inverse * (scaled - unit * jnp.mean(scaled * unit, axis=-1, keepdims=True)), grad_gain


def across(a, which):
    return lax.ppermute(a, "seq", [(i, i ^ which) for i in range(4)])


def split3(v):
    hi = lax.reduce_precision(v, 8, 7)
    mid = lax.reduce_precision(v - hi, 8, 7)
    low = lax.reduce_precision(v - hi - mid, 8, 7)
    return hi, mid, low


def swiglu_back(grad_act, gate, up):
    sig = jax.nn.sigmoid(gate)
    grad_gate = (grad_act * up * sig * (1.0 + gate * (1.0 - sig))).astype(BF16)
    grad_up = (grad_act * gate * sig).astype(BF16)
    return grad_gate, grad_up


def gather_in(a, b):
    half = a.shape[0] // 2
    ax, ay = across(a, 1), across(a, 2)
    ad0, ad1 = across(ax[:half], 2), across(ay[half:], 1)
    full_a = jnp.concatenate([a, ay[:half], ax[half:], ax[:half], ad0, ay[half:], ad1], axis=0)
    bx, by = across(b, 1), across(b, 2)
    bd0, bd1 = across(bx[:, :half], 2), across(by[:, half:], 1)
    full_b = jnp.concatenate(
        [b, by[:, :half], bx[:, half:], bx[:, :half], bd0, by[:, half:], bd1], axis=1
    )
    return full_a, full_b


def shards(
    tokens, cotangent, ids, deal, lengths, w_qkv, b_qkv, w_out, gain_attn, gain_ffn, w_router,
    w_shared_gate, e_gate, e_up, e_down, s_gate, s_up, s_down,
):
    S, N = lax.axis_size("seq"), lax.axis_size("fsdp")
    s, f = lax.axis_index("seq"), lax.axis_index("fsdp")
    MB, T, D = tokens.shape
    E = w_router.shape[1]
    assert S == 4 and e_gate.shape[0] == 1 and E == N
    FE, FS = e_gate.shape[2], s_gate.shape[1]
    piece = T // N
    pack = T * S
    heads = H // S
    width = heads * HD
    rows = N * MB * T
    own = w_out.shape[0]

    stack_a = jnp.concatenate([e_gate[0], e_up[0], s_gate, s_up], axis=1)
    stack_b = jnp.concatenate([e_down[0], s_down], axis=0)
    full_a, full_b = gather_in(stack_a, stack_b)

    small = jnp.concatenate([gain_attn, gain_ffn, w_router.reshape(-1), w_shared_gate, b_qkv])
    small = lax.all_gather(small, ("seq", "fsdp"), axis=0)
    cuts = (own, 2 * own, 2 * own + own * E, 3 * own + own * E)
    gain_1 = small[:, : cuts[0]].reshape(D).astype(F32)
    gain_2 = small[:, cuts[0] : cuts[1]].reshape(D).astype(F32)
    router_w = small[:, cuts[1] : cuts[2]].reshape(D, E)
    shared_w = small[:, cuts[2] : cuts[3]].reshape(D)
    bias = lax.dynamic_slice_in_dim(small[:, cuts[3] :].reshape(3, S, width), s, 1, 1)
    bias = bias.reshape(3 * width).astype(F32)

    w = lax.all_to_all(w_qkv.reshape(own, 3, S, width), "seq", split_axis=2, concat_axis=0, tiled=True)
    w = lax.all_gather(w.reshape(S, own, 3 * width), "fsdp", axis=1, tiled=True)
    w_in = w.reshape(D, 3 * width)
    w_back = lax.all_gather(w_out, "fsdp", axis=0, tiled=True)

    pad = 128
    extra = jnp.pad(ids.astype(BF16), ((0, 0), (0, 0), (0, pad - TOP)))
    send = jnp.concatenate([tokens, cotangent, extra], axis=2).reshape(MB, piece, N, 2 * D + pad)
    inverse_deal = jnp.argsort(deal[:, f], axis=1)
    send = jnp.stack([jnp.take(send[m], inverse_deal[m], axis=1) for m in range(MB)])
    dealt = lax.all_to_all(send, "fsdp", split_axis=2, concat_axis=2, tiled=True)
    dealt = dealt.reshape(MB, T, 2 * D + pad)
    x0 = dealt[..., :D].astype(F32)
    cot = dealt[..., D : 2 * D]
    tags = dealt[..., 2 * D :]

    order = jnp.stack([jnp.bitwise_xor(s, rel) * 2 + half for rel, half in ORDER])
    inverse_order = jnp.argsort(order)

    def arrange(u, by):
        return jnp.take(u.reshape(u.shape[:-1] + (8, D // 8)), by, axis=u.ndim - 1).reshape(u.shape)

    g_all = lax.all_gather(
        jnp.concatenate([arrange(cot, order), tags], axis=2).reshape(MB * T, D + pad), "fsdp", axis=0, tiled=True
    )
    g_rows = g_all[:, :D]
    chosen = g_all[:, D : D + TOP].astype(jnp.int32)

    ends = jnp.cumsum(lengths[:, f], axis=1)
    spots = jnp.arange(pack, dtype=jnp.int32)
    past = ends[:, None, :] <= spots[None, :, None]
    segment = jnp.sum(past.astype(jnp.int32), axis=2)
    start = jnp.sum(jnp.where(past, lengths[:, f][:, None, :], 0), axis=2)
    frequency = THETA ** (-jnp.arange(0, HD, 2, dtype=F32) / HD)
    angle = (spots[None] - start).astype(F32)[..., None] * frequency
    angle = jnp.concatenate([angle, angle], axis=2)
    cosine, sine = jnp.cos(angle)[:, None, None], jnp.sin(angle)[:, None, None]
    allowed = (segment[:, :, None] == segment[:, None, :]) & (spots[None, None, :] <= spots[None, :, None])
    allowed = allowed[:, None]

    unit_1, inverse_1 = rms_forward(x0)
    normed = (unit_1 * gain_1).astype(BF16)
    normed_all = lax.all_gather(normed, "seq", axis=1, tiled=True)
    flat = normed_all.reshape(MB * pack, D)
    qkv = (dot(flat, w_in) + bias).reshape(MB, pack, 3, heads, HD).transpose(0, 2, 3, 1, 4)
    qk = qkv[:, :2]
    qk = (qk * cosine + turn(qk) * sine).astype(BF16)
    q, k, v = qk[:, 0], qk[:, 1], qkv[:, 2].astype(BF16)
    scale = HD ** -0.5
    raw = jnp.einsum("mhqd,mhkd->mhqk", q, k, preferred_element_type=F32)
    scores = jnp.where(allowed, raw * scale, MASKED)
    weights = jnp.exp(scores - jnp.max(scores, axis=-1, keepdims=True))
    chance = weights / jnp.sum(weights, axis=-1, keepdims=True)
    chance_low = chance.astype(BF16)
    context = jnp.einsum("mhqk,mhkd->mqhd", chance_low, v, preferred_element_type=F32).astype(BF16)
    context = context.reshape(MB * pack, width)
    partial = dot(context, w_back).astype(BF16).reshape(MB, S, T, D)
    partial = lax.all_to_all(partial, "seq", split_axis=1, concat_axis=1, tiled=True)
    hidden = x0 + jnp.sum(partial.astype(F32), axis=1)
    unit_2, inverse_2 = rms_forward(hidden)
    normed2 = (unit_2 * gain_2).astype(BF16)

    x = lax.all_gather(arrange(normed2, order).reshape(MB * T, D), "fsdp", axis=0, tiled=True)
    lead = jnp.concatenate([router_w, shared_w[:, None]], axis=1)
    lead_order = jnp.take(lead.reshape(8, D // 8, E + 1), order, axis=0).reshape(D, E + 1)
    logits = dot(x, lead_order)
    shifted = jnp.exp(logits[:, :E] - jnp.max(logits[:, :E], axis=-1, keepdims=True))
    router_f = jnp.sum(jnp.where(jnp.arange(E) == f, shifted, 0.0), axis=1) / jnp.sum(shifted, axis=1)
    gate_f = jnp.where(jnp.any(chosen == f, axis=1), router_f, 0.0)[:, None]
    sigma_rows = jax.nn.sigmoid(logits[:, E])[:, None]
    g32 = g_rows.astype(F32)
    geo = (gate_f * g32).astype(BF16)
    gso = (sigma_rows * g32).astype(BF16)

    eg, eu, sg, su = jnp.split(full_a, (FE, 2 * FE, 2 * FE + FS), axis=1)
    ed, sd = full_b[:FE], full_b[FE:]
    gate, up = dot(x, eg), dot(x, eu)
    act = (jax.nn.silu(gate) * up).astype(BF16)
    out_e = dot(act, ed).astype(BF16).astype(F32)
    sgate, sup = dot(x, sg), dot(x, su)
    sact = (jax.nn.silu(sgate) * sup).astype(BF16)
    out_s = dot(sact, sd)
    y = (gate_f * out_e + sigma_rows * out_s).astype(BF16)
    y = lax.psum_scatter(y, "fsdp", scatter_dimension=0, tiled=True)
    gg = jnp.sum(g32 * out_e, axis=1)
    gs = jnp.sum(g32 * out_s, axis=1)

    grad_gate, grad_up = swiglu_back(dot_nt(geo, ed), gate, up)
    grad_sgate, grad_sup = swiglu_back(dot_nt(gso, sd), sgate, sup)
    dx_e = (dot_nt(grad_gate, eg) + dot_nt(grad_up, eu)).astype(BF16).astype(F32)
    dx = dx_e + dot_nt(grad_sgate, sg) + dot_nt(grad_sup, su)
    mine = (jnp.arange(N) == f).astype(F32)
    notes = [part[:, None] * mine for value in (gg, gs) for part in split3(value)]
    note_pad = -(6 * N) % 128
    payload = jnp.concatenate([dx] + notes + [jnp.zeros((rows, note_pad), F32)], axis=1).astype(BF16)
    dx = lax.psum_scatter(payload, "fsdp", scatter_dimension=0, tiled=True).astype(F32)

    cat_grad = jnp.concatenate([grad_gate, grad_up, grad_sgate, grad_sup], axis=1)
    half = D // 8
    send_x = dot_t(x[:, 4 * half : 6 * half], cat_grad).astype(BF16)
    send_y = dot_t(x[:, 6 * half :], cat_grad).astype(BF16)
    from_x, from_y = across(send_x, 1), across(send_y, 2)

    def down_grad(lo, hi):
        return jnp.concatenate([dot_t(act, geo[:, lo:hi]), dot_t(sact, gso[:, lo:hi])], axis=0)

    bsend_x = down_grad(4 * half, 6 * half).astype(BF16)
    bsend_y = down_grad(6 * half, 8 * half).astype(BF16)
    bfrom_x, bfrom_y = across(bsend_x, 1), across(bsend_y, 2)
    keep = dot_t(x[:, : 4 * half], cat_grad)
    bkeep = down_grad(0, 4 * half)
    to_y = (keep[2 * half : 3 * half] + from_x[half:].astype(F32)).astype(BF16)
    to_x = (keep[3 * half :] + from_y[half:].astype(F32)).astype(BF16)
    last_y, last_x = across(to_y, 2), across(to_x, 1)
    bto_y = (bkeep[:, 2 * half : 3 * half] + bfrom_x[:, half:].astype(F32)).astype(BF16)
    bto_x = (bkeep[:, 3 * half :] + bfrom_y[:, half:].astype(F32)).astype(BF16)
    blast_y, blast_x = across(bto_y, 2), across(bto_x, 1)
    grad_a = jnp.concatenate(
        [
            keep[:half] + from_x[:half].astype(F32) + last_y.astype(F32),
            keep[half : 2 * half] + from_y[:half].astype(F32) + last_x.astype(F32),
        ],
        axis=0,
    )
    grad_b = jnp.concatenate(
        [
            bkeep[:, :half] + bfrom_x[:, :half].astype(F32) + blast_y.astype(F32),
            bkeep[:, half : 2 * half] + bfrom_y[:, :half].astype(F32) + blast_x.astype(F32),
        ],
        axis=1,
    )
    g_eg, g_eu, g_sg, g_su = jnp.split(grad_a, (FE, 2 * FE, 2 * FE + FS), axis=1)

    y = arrange(y.astype(F32).reshape(MB, T, D), inverse_order)
    mixed = (hidden + y).astype(BF16)
    base = D
    gg_own = sum(dx[:, base + i * N : base + (i + 1) * N] for i in range(3))
    gs_own = jnp.sum(dx[:, base + 3 * N : base + 6 * N], axis=1)
    grad_normed2 = arrange(dx[:, :D], inverse_order)
    flat2 = normed2.reshape(MB * T, D)
    logits = dot(flat2, lead)
    shifted = jnp.exp(logits[:, :E] - jnp.max(logits[:, :E], axis=-1, keepdims=True))
    router = shifted / jnp.sum(shifted, axis=-1, keepdims=True)
    sigma = jax.nn.sigmoid(logits[:, E])
    own_ids = tags[..., :TOP].reshape(MB * T, TOP).astype(jnp.int32)
    picked = jnp.any(own_ids[:, :, None] == jnp.arange(E)[None, None, :], axis=1)
    grad_router = jnp.where(picked, gg_own, 0.0)
    grad_logits = (router * (grad_router - jnp.sum(router * grad_router, axis=-1, keepdims=True))).astype(BF16)
    grad_sigma = gs_own * sigma * (1.0 - sigma)
    grad_normed2 = grad_normed2 + dot_nt(grad_logits, router_w) + grad_sigma[:, None] * shared_w.astype(F32)[None, :]
    g_router = dot_t(flat2, grad_logits)
    g_shared = jnp.sum(grad_sigma[:, None] * flat2.astype(F32), axis=0)
    from_norm, g_gain_2 = rms_backward(grad_normed2.reshape(MB, T, D), unit_2, inverse_2, gain_2)
    grad_hidden = cot.astype(F32) + from_norm

    grad_attn = lax.all_gather(grad_hidden.astype(BF16), "seq", axis=1, tiled=True).reshape(MB * pack, D)
    g_out = dot_t(context, grad_attn)
    gc = dot_nt(grad_attn, w_back).astype(BF16).reshape(MB, pack, heads, HD).transpose(0, 2, 1, 3)
    grad_chance = jnp.einsum("mhqd,mhkd->mhqk", gc, v, preferred_element_type=F32)
    delta = jnp.sum(chance * grad_chance, axis=-1, keepdims=True)
    grad_raw = (chance * (grad_chance - delta) * scale).astype(BF16)
    gq = jnp.einsum("mhqk,mhkd->mhqd", grad_raw, k, preferred_element_type=F32)
    gk = jnp.einsum("mhqk,mhqd->mhkd", grad_raw, q, preferred_element_type=F32)
    gv = jnp.einsum("mhqk,mhqd->mhkd", chance_low, gc, preferred_element_type=F32)
    gqk = jnp.stack([gq, gk], axis=1).astype(BF16).astype(F32)
    gqk = (gqk * cosine + turn_back(gqk * sine)).astype(BF16)
    grad_qkv = jnp.concatenate([gqk, gv.astype(BF16)[:, None]], axis=1).transpose(0, 3, 1, 2, 4)
    grad_qkv = grad_qkv.reshape(MB * pack, 3 * width)
    g_bias = jnp.sum(grad_qkv.astype(F32), axis=0)
    g_in = dot_t(flat, grad_qkv)
    partial = dot_nt(grad_qkv, w_in).astype(BF16).reshape(MB, S, T, D)
    partial = lax.all_to_all(partial, "seq", split_axis=1, concat_axis=1, tiled=True)
    grad_normed = jnp.sum(partial.astype(F32), axis=1)
    from_first, g_gain_1 = rms_backward(grad_normed, unit_1, inverse_1, gain_1)
    grad_x = (grad_hidden + from_first).astype(BF16)

    back = jnp.concatenate([mixed, grad_x], axis=2).reshape(MB, piece, N, 2 * D)
    back = lax.all_to_all(back, "fsdp", split_axis=2, concat_axis=2, tiled=True)
    back = jnp.stack([jnp.take(back[m], deal[m, f], axis=1) for m in range(MB)]).reshape(MB, T, 2 * D)
    mixed, grad_tokens = back[..., :D], back[..., D:].astype(F32)

    g_in = lax.psum_scatter(g_in.astype(BF16).reshape(S, N * own, 3 * width), "fsdp", scatter_dimension=1, tiled=True)
    g_in = lax.all_to_all(g_in, "seq", split_axis=0, concat_axis=0, tiled=True)
    g_in = g_in.reshape(S, own, 3, width).transpose(1, 2, 0, 3).reshape(own, 3 * D).astype(F32)
    g_out = lax.psum_scatter(g_out.astype(BF16), "fsdp", scatter_dimension=0, tiled=True).astype(F32)
    g_bias = jnp.where(jnp.arange(S)[None, :, None] == s, g_bias.reshape(3, 1, width), 0.0)
    count = S * N
    small = jnp.concatenate(
        [
            g_gain_1.reshape(count, own), g_gain_2.reshape(count, own), g_router.reshape(count, own * E),
            g_shared.reshape(count, own), g_bias.reshape(count, 3 * own),
        ],
        axis=1,
    )
    small = lax.psum_scatter(small, ("seq", "fsdp"), scatter_dimension=0, tiled=True)[0]
    return (
        mixed, grad_tokens, g_in, small[cuts[3] :], g_out, small[: cuts[0]], small[cuts[0] : cuts[1]],
        small[cuts[1] : cuts[2]].reshape(own, E), small[cuts[2] : cuts[3]],
        g_eg[None], g_eu[None], grad_b[:FE][None], g_sg, g_su, grad_b[FE:],
    )


def solution(mesh):
    both = ("seq", "fsdp")
    in_specs = (
        P(None, both, None), P(None, both, None), P(None, both, None), P(), P(), P(both, None), P(both), P(both, None),
        P(both), P(both), P(both, None), P(both), P("fsdp", "seq", None), P("fsdp", "seq", None),
        P("fsdp", None, "seq"), P("seq", "fsdp"), P("seq", "fsdp"), P("fsdp", "seq"),
    )
    out_specs = (
        P(None, both, None), P(None, both, None), P(both, None), P(both), P(both, None), P(both), P(both),
        P(both, None), P(both), P("fsdp", "seq", None), P("fsdp", "seq", None), P("fsdp", None, "seq"),
        P("seq", "fsdp"), P("seq", "fsdp"), P("fsdp", "seq"),
    )
    return jax.shard_map(shards, mesh=mesh, in_specs=in_specs, out_specs=out_specs, check_vma=False)
```

time: 2430 us -> 1370 us (0.56)
  waiting for transfers between devices: 1420 us -> 655 us
  blocking collectives: 205 us -> 90.4 us
  matrix products: 418 us -> 323 us
  starting transfers between devices: 111 us -> 39.8 us
    all_to_all x24 -> x5, waiting for transfers between devices: 522 us -> 51.1 us  [the longest x2 45.8 us: shards(): lax.all_to_all(partial, 'seq', split_axis=1, concat_axis=1, tiled=True)]
    reduce_scatter x12 -> x4, waiting for transfers between devices: 517 us -> 66.5 us  [the longest x1 66.5 us: shards(): lax.psum_scatter(payload, 'fsdp', scatter_dimension=0, tiled=True)]
    ppermute x0 -> x16, waiting for transfers between devices: none -> 410 us  [across(): return lax.ppermute(a, 'seq', [(i, i ^ which) for i in range(4)])]
    all_gather x12 -> x6, waiting for transfers between devices: 370 us -> 126 us  [the longest x1 66.9 us: shards(): w = lax.all_gather(w.reshape(S, own, 3 * width), 'fsdp', axis=1, tiled=True)]
    dot_general x70 -> x37, matrix products: 418 us -> 323 us  [the longest x10 104 us: dot(): return jnp.dot(a, b, preferred_element_type=F32)]
    unnamed x2 -> x0, blocking collectives: 86.3 us -> none
    all_to_all x24 -> x5, starting transfers between devices: 108 us -> 24 us  [the longest x2 9.33 us: shards(): lax.all_to_all(partial, 'seq', split_axis=1, concat_axis=1, tiled=True)]
    all_gather x1, blocking collectives: 119 us -> 68.1 us  [shards(): small = lax.all_gather(small, ('seq', 'fsdp'), axis=0)]
  transfers between devices with their start and end apart: 49 -> 32, of which waited for: 31 -> 18; matrix products, arithmetic and copies ran while one was open for 27% -> 26% of each run, Pallas kernels for 0% -> 0%
where the time goes in v1:
time: 1370 us; the launch traced here: 1360 us
  waiting for transfers between devices  655 us (48%)
  matrix products  323 us (24%)
  local copies, waits for them, and re-layouts  149 us (11%)
  blocking collectives  90.4 us (7%)
  other arithmetic  89.2 us (7%)
  starting transfers between devices  39.8 us (3%)
  between operations  15.8 us (1%)
    ppermute x16, waiting for transfers between devices, across(): return lax.ppermute(a, 'seq', [(i, i ^ which) for i in range(4)])  410 us
    dot_general x10, matrix products, dot(): return jnp.dot(a, b, preferred_element_type=F32)  104 us
    dot_general x12, matrix products, dot_t(): lax.dot_general(a, b, (((0,), (0,)), ((), ())), preferred_element_type=F32)  98.6 us
    dot_general x9, matrix products, dot_nt(): lax.dot_general(a, b, (((1,), (1,)), ((), ())), preferred_element_type=F32)  92.1 us
    all_gather x1, blocking collectives, shards(): small = lax.all_gather(small, ('seq', 'fsdp'), axis=0)  68.1 us
    all_gather x1, waiting for transfers between devices, shards(): w = lax.all_gather(w.reshape(S, own, 3 * width), 'fsdp', axis=1, tiled=True)  66.9 us
    reduce_scatter x1, waiting for transfers between devices, shards(): lax.psum_scatter(payload, 'fsdp', scatter_dimension=0, tiled=True)  66.5 us
    all_to_all x2, waiting for transfers between devices, shards(): lax.all_to_all(partial, 'seq', split_axis=1, concat_axis=1, tiled=True)  45.8 us
  transfers between devices with their start and end apart: 32, of which 18 were waited for; matrix products, arithmetic and copies ran while one was open for 26% of the time, Pallas kernels for 0%

profile of v1, /device:TPU:0, one launch (start us, length us, event | category | flops | bytes accessed | tf_op | source)
XLA Modules:
  0.0 1361.9 jit_solution(6551151081218275772)
XLA Ops:
  23.5 68.1 %all-gather.1 = bf16[32,1,896]{2,1,0:T(2,128)(2,1)S(1)} all-gather(bf16[1,1,896]{2,1,0:T(2,128)(2,1)S(1)} %reshape.822), channel_id=2, replica_groups=mesh['seq'=4,'fsdp'=8] {'seq','fsdp'}, dimensions={0}, use_global_device_ids=true | all-gather | bytes 59136 | tf_op jit(solution)/shard_map/all_gather | solution.py:104
  96.5 22.3 %all_to_all.40 = bf16[64,3,4,512]{3,0,1,2:T(8,128)(2,1)S(1)} all-to-all(bf16[64,3,4,512]{3,0,1,2:T(8,128)(2,1)S(1)} %copy.367), channel_id=1, replica_groups=mesh['seq'=4,'fsdp'=8] {'seq'}, dimensions={2} | all-to-all | bytes 1572864 | tf_op jit(solution)/shard_map/all_to_all | solution.py:113
  125.0 15.9 %all-gather.9.cloned.1.call-done = bf16[2,384,2048]{2,1,0:T(8,128)(2,1)} async-done(((bf16[2,96,2048]{2,1,0:T(8,128)(2,1)}), bf16[2,384,2048]{2,1,0:T(8,128)(2,1)}) %all-gather.9.cloned.1.call-update) | async-done | bytes 3145744 | tf_op jit(solution)/shard_map/all_gather | solution.py:155
  140.9 66.9 %all-gather.11.cloned.1.call-done = bf16[4,512,1536]{2,1,0:T(8,128)(2,1)} async-done(((bf16[4,64,1536]{2,1,0:T(8,128)(2,1)}), bf16[4,512,1536]{2,1,0:T(8,128)(2,1)}) %all-gather.11.cloned.1.call-update) | async-done | bytes 6291472 | tf_op jit(solution)/shard_map/all_gather | solution.py:114
  207.9 9.6 convolution_add_fusion
  250.3 34.2 %all-to-all-done.2 = bf16[2,4,96,2048]{3,2,0,1:T(8,128)(2,1)} async-done(((bf16[2,4,96,2048]{3,2,0,1:T(8,128)(2,1)}), bf16[2,4,96,2048]{3,2,0,1:T(8,128)(2,1)}, u32[]{:S(2)}, u32[]{:S(2)}) %all-to-all-start.2) | async-done | bytes 3145760 | tf_op jit(solution)/shard_map/all_to_all | solution.py:170
  314.3 131.5 %collective-permute-done.4 = bf16[2112,512]{1,0:T(8,128)(2,1)S(1)} collective-permute-done((bf16[2112,512]{1,0:T(8,128)(2,1)S(1)}, bf16[2112,512]{1,0:T(8,128)(2,1)S(1)}, u32[]{:S(2)}, u32[]{:S(2)}) %collective-permute-start.4) | collective-permute-done | bytes 2162720 | tf_op jit(solution)/shard_map/ppermute | solution.py:52
  464.1 66.8 %collective-permute-done.6 = bf16[2112,256]{1,0:T(8,128)(2,1)S(1)} collective-permute-done((bf16[2112,256]{1,0:T(8,128)(2,1)S(1)}, bf16[2112,256]{1,0:T(8,128)(2,1)S(1)}, u32[]{:S(2)}, u32[]{:S(2)}) %collective-permute-start.6) | collective-permute-done | bytes 1081376 | tf_op jit(solution)/shard_map/ppermute | solution.py:52
  542.2 62.2 %collective-permute-done.7 = bf16[2112,256]{1,0:T(8,128)(2,1)} collective-permute-done((bf16[2112,256]{1,0:T(8,128)(2,1)}, bf16[2112,256]{1,0:T(8,128)(2,1)}, u32[]{:S(2)}, u32[]{:S(2)}) %collective-permute-start.7) | collective-permute-done | bytes 1081376 | tf_op jit(solution)/shard_map/ppermute | solution.py:52
  623.5 14.4 %fusion.16 = f32[1536,1408]{0,1:T(8,128)} fusion(bf16[1536,2048]{1,0:T(8,128)(2,1)S(1)} %copy-done.19, bf16[2048,4224]{1,0:T(8,128)(2,1)} %constant_dynamic-update-slice_fusion), kind=kOutput, calls=%fused_computation.55 | convolution fusion | flops 8858370048 | bytes 20709376 | tf_op jit(solution)/shard_map/dot_general | solution.py:19
  649.6 13.5 fusion.8
  663.1 20.2 %multiply_convert_fusion.2 = (bf16[1536,1408]{0,1:T(8,128)(2,1)}, bf16[1536,1408]{0,1:T(8,128)(2,1)}, bf16[1536,1408]{0,1:T(8,128)(2,1)}) fusion(f32[1536,1408]{0,1:T(8,128)} %fusion.16, f32[1536,1408]{0,1:T(8,128)} %fusion.8, bf16[1536,2048]{1,0:T(8,128)(2,1)S(1)} %bitcast.243, bf16[2048,4224]{1,0:T(8,128)(2,1)} %constant_dynamic-update-slice_fusion), kind=kOutput, calls=%fused_computation.39 | convolution fusion | flops 8892973056 | bytes 42336256 | tf_op jit(solution)/shard_map/dot_general | solution.py:19
  683.3 15.8 %convolution_convert_fusion.1 = bf16[1536,2048]{1,0:T(8,128)(2,1)} fusion(bf16[1536,1408]{0,1:T(8,128)(2,1)} %get-tuple-element.182, bf16[2112,2048]{1,0:T(8,128)(2,1)} %constant_dynamic-update-slice_fusion.5), kind=kOutput, calls=%fused_computation.42 | convolution fusion | flops 8861515776 | bytes 16384000 | tf_op jit(solution)/shard_map/dot_general | solution.py:19
  707.5 13.3 multiply_convert_fusion.6
  720.8 13.4 fusion.7
  735.8 10.4 fusion.49
  746.2 16.1 %fusion.11 = f32[1536,2048]{1,0:T(8,128)} fusion(bf16[1536,1408]{0,1:T(8,128)(2,1)} %get-tuple-element.184, bf16[2048,4224]{1,0:T(8,128)(2,1)} %constant_dynamic-update-slice_fusion), kind=kOutput, calls=%fused_computation.50 | convolution fusion | flops 8858370048 | bytes 22675456 | tf_op jit(solution)/shard_map/dot_general | solution.py:27
  762.3 15.4 %add_convert_fusion.1 = bf16[1536,2048]{1,0:T(8,128)(2,1)S(1)} fusion(f32[1536,2048]{1,0:T(8,128)} %fusion.11, bf16[1536,1408]{0,1:T(8,128)(2,1)} %get-tuple-element.183, bf16[2048,4224]{1,0:T(8,128)(2,1)} %constant_dynamic-update-slice_fusion), kind=kOutput, calls=%fused_computation.27 | convolution fusion | flops 8864661504 | bytes 28966912 | tf_op jit(solution)/shard_map/dot_general | solution.py:27
  777.7 13.0 add_convert_fusion
  790.7 11.7 concatenate.122
  811.8 66.5 %reduce-scatter.7.cloned.1.call-done = bf16[192,2176]{1,0:T(8,128)(2,1)} async-done(((bf16[1536,2176]{1,0:T(8,128)(2,1)}), bf16[192,2176]{1,0:T(8,128)(2,1)}) %reduce-scatter.7.cloned.1.call-update) | async-done | bytes 835600 | tf_op jit(solution)/shard_map/reduce_scatter | solution.py:208
  894.2 41.2 %all-gather.19.cloned.1.call-done = bf16[2,384,2048]{2,1,0:T(8,128)(2,1)} async-done(((bf16[2,96,2048]{2,1,0:T(8,128)(2,1)}), bf16[2,384,2048]{2,1,0:T(8,128)(2,1)}) %all-gather.19.cloned.1.call-update) | async-done | bytes 3145744 | tf_op jit(solution)/shard_map/all_gather | solution.py:268
  961.5 9.4 fusion.119
  999.7 16.7 %convolution_convert_fusion.2 = bf16[512,4224]{1,0:T(8,128)(2,1)} fusion(bf16[1536,2048]{1,0:T(8,128)(2,1)} %all-gather.17.cloned.1.call-done, bf16[1536,704]{0,1:T(8,128)(2,1)} %get-tuple-element.195, bf16[1536,704]{0,1:T(8,128)(2,1)} %get-tuple-element.194, bf16[1536,1408]{0,1:T(8,128)(2,1)} %get-tuple-element.184, bf16[1536,1408]{0,1:T(8,128)(2,1)} %get-tuple-element.183), kind=kOutput, calls=%fused_computation.43 | convolution fusion | flops 6697844736 | bytes 18874368 | tf_op jit(solution)/shard_map/dot_general | solution.py:23
  1025.5 11.6 all-to-all-done.3
  1047.7 17.1 %convolution_convert_fusion.3 = bf16[512,4224]{1,0:T(8,128)(2,1)} fusion(bf16[1536,2048]{1,0:T(8,128)(2,1)} %all-gather.17.cloned.1.call-done, bf16[1536,704]{0,1:T(8,128)(2,1)} %get-tuple-element.195, bf16[1536,704]{0,1:T(8,128)(2,1)} %get-tuple-element.194, bf16[1536,1408]{0,1:T(8,128)(2,1)} %get-tuple-element.184, bf16[1536,1408]{0,1:T(8,128)(2,1)} %get-tuple-element.183), kind=kOutput, calls=%fused_computation.44 | convolution fusion | flops 6697844736 | bytes 18874368 | tf_op jit(solution)/shard_map/dot_general | solution.py:23
  1092.1 22.8 %fusion.33 = f32[1024,4224]{1,0:T(8,128)} fusion(bf16[1536,2048]{1,0:T(8,128)(2,1)} %all-gather.17.cloned.1.call-done, bf16[1536,704]{0,1:T(8,128)(2,1)} %get-tuple-element.195, bf16[1536,704]{0,1:T(8,128)(2,1)} %get-tuple-element.194, bf16[1536,1408]{0,1:T(8,128)(2,1)} %get-tuple-element.184, bf16[1536,1408]{0,1:T(8,128)(2,1)} %get-tuple-element.183), kind=kOutput, calls=%fused_computation.92 | convolution fusion | flops 13339459584 | bytes 33423360 | tf_op jit(solution)/shard_map/dot_general | solution.py:23
  1115.0 15.6 %collective-permute-done.10 = bf16[512,4224]{1,0:T(8,128)(2,1)} collective-permute-done((bf16[512,4224]{1,0:T(8,128)(2,1)}, bf16[512,4224]{1,0:T(8,128)(2,1)}, u32[]{:S(2)}, u32[]{:S(2)}) %collective-permute-start.10) | collective-permute-done | bytes 4325408 | tf_op jit(solution)/shard_map/ppermute | solution.py:52
  1147.2 28.9 %collective-permute-done.14 = bf16[2112,512]{1,0:T(8,128)(2,1)} collective-permute-done((bf16[2112,512]{1,0:T(8,128)(2,1)}, bf16[2112,512]{1,0:T(8,128)(2,1)}, u32[]{:S(2)}, u32[]{:S(2)}) %collective-permute-start.14) | collective-permute-done | bytes 2162720 | tf_op jit(solution)/shard_map/ppermute | solution.py:52
  1176.1 32.4 %collective-permute-done.12 = bf16[2112,512]{1,0:T(8,128)(2,1)} collective-permute-done((bf16[2112,512]{1,0:T(8,128)(2,1)}, bf16[2112,512]{1,0:T(8,128)(2,1)}, u32[]{:S(2)}, u32[]{:S(2)}) %collective-permute-start.12) | collective-permute-done | bytes 2162720 | tf_op jit(solution)/shard_map/ppermute | solution.py:52
  1213.2 41.7 %collective-permute-done.11 = bf16[256,4224]{1,0:T(8,128)(2,1)} collective-permute-done((bf16[256,4224]{1,0:T(8,128)(2,1)S(1)}, bf16[256,4224]{1,0:T(8,128)(2,1)}, u32[]{:S(2)}, u32[]{:S(2)}) %collective-permute-start.11) | collective-permute-done | bytes 2162720 | tf_op jit(solution)/shard_map/ppermute | solution.py:52
  1282.3 22.2 %collective-permute-done.9 = bf16[256,4224]{1,0:T(8,128)(2,1)} collective-permute-done((bf16[256,4224]{1,0:T(8,128)(2,1)}, bf16[256,4224]{1,0:T(8,128)(2,1)}, u32[]{:S(2)}, u32[]{:S(2)}) %collective-permute-start.9) | collective-permute-done | bytes 2162720 | tf_op jit(solution)/shard_map/ppermute | solution.py:52
  (498 shorter events, 384.9 us)
Async XLA Ops:
  16.7 75.6 %all-to-all-start = ((bf16[2,12,8,4224]{3,0,1,2:T(2,128)(2,1)}), bf16[2,12,8,4224]{3,0,1,2:T(2,128)(2,1)S(1)}, u32[]{:S(2)}, u32[]{:S(2)}) async-start(bf16[2,12,8,4224]{3,0,1,2:T(2,128)(2,1)} %copy.364), calls=%async_computation | async-start | bytes 3244032 | tf_op jit(solution)/shard_map/all_to_all | solution.py:123
  23.1 117.9 %all-gather.9.cloned.1.call-start = ((), (), s32[]{:S(2)}) async-start(), calls=%async_computation.10 | async-start | bytes 3932160 | tf_op jit(solution)/shard_map/all_gather | solution.py:155
  93.9 113.9 %all-gather.11.cloned.1.call-start = ((), (), s32[]{:S(2)}) async-start(), calls=%async_computation.11 | async-start | bytes 7077888 | tf_op jit(solution)/shard_map/all_gather | solution.py:114
  121.3 116.0 %all-gather.13.cloned.1.call-start = ((), (), s32[]{:S(2)}) async-start(), calls=%async_computation.12 | async-start | bytes 2359296 | tf_op jit(solution)/shard_map/all_gather | solution.py:116
  242.9 41.5 %all-to-all-start.2 = ((bf16[2,4,96,2048]{3,2,0,1:T(8,128)(2,1)}), bf16[2,4,96,2048]{3,2,0,1:T(8,128)(2,1)}, u32[]{:S(2)}, u32[]{:S(2)}) async-start(bf16[2,4,96,2048]{3,2,0,1:T(8,128)(2,1)} %copy.373), calls=%async_computation.2 | async-start | bytes 6291456 | tf_op jit(solution)/shard_map/all_to_all | solution.py:170
  247.6 362.3 %all-gather.17.cloned.1.call-start = ((), (), s32[]{:S(2)}) async-start(), calls=%async_computation.14 | async-start | bytes 7077888 | tf_op jit(solution)/shard_map/all_gather | solution.py:175
  295.1 342.8 %all-gather.15.cloned.1.call-start = ((), (), s32[]{:S(2)}) async-start(), calls=%async_computation.13 | async-start | bytes 7520256 | tf_op jit(solution)/shard_map/all_gather | solution.py:135
  304.6 147.1 %collective-permute-start = (bf16[512,4224]{1,0:T(8,128)(2,1)}, bf16[512,4224]{1,0:T(8,128)(2,1)S(1)}, u32[]{:S(2)}, u32[]{:S(2)}) collective-permute-start(bf16[512,4224]{1,0:T(8,128)(2,1)} %concatenate.118), channel_id=1, source_target_pairs={{0,16},{8,24},{16,0},{24,8},{1,17},{9,25},{17,1},{25,9},{2,18},{10... | collective-permute-start | bytes 12976136 | tf_op jit(solution)/shard_map/ppermute | solution.py:52
  309.4 136.4 %collective-permute-start.4 = (bf16[2112,512]{1,0:T(8,128)(2,1)S(1)}, bf16[2112,512]{1,0:T(8,128)(2,1)S(1)}, u32[]{:S(2)}, u32[]{:S(2)}) collective-permute-start(bf16[2112,512]{1,0:T(8,128)(2,1)S(1)} %get-tuple-element.210), channel_id=1, source_target_pairs={{0,16},{8,24},{16,0},{24,8},{1,17},{9,25},{17,1},{25,9},{2,18},{10... | collective-permute-start | bytes 6488072 | tf_op jit(solution)/shard_map/ppermute | solution.py:52
  310.0 143.3 %collective-permute-start.1 = (bf16[512,4224]{1,0:T(8,128)(2,1)S(1)}, bf16[512,4224]{1,0:T(8,128)(2,1)S(1)}, u32[]{:S(2)}, u32[]{:S(2)}) collective-permute-start(bf16[512,4224]{1,0:T(8,128)(2,1)S(1)} %copy-done.11), channel_id=1, source_target_pairs={{0,8},{8,0},{16,24},{24,16},{1,9},{9,1},{17,25},{25,17},{2,10},{10... | collective-permute-start | bytes 12976136 | tf_op jit(solution)/shard_map/ppermute | solution.py:52
  311.4 139.0 %collective-permute-start.5 = (bf16[2112,512]{1,0:T(8,128)(2,1)S(1)}, bf16[2112,512]{1,0:T(8,128)(2,1)S(1)}, u32[]{:S(2)}, u32[]{:S(2)}) collective-permute-start(bf16[2112,512]{1,0:T(8,128)(2,1)S(1)} %get-tuple-element.210), channel_id=1, source_target_pairs={{0,8},{8,0},{16,24},{24,16},{1,9},{9,1},{17,25},{25,17},{2,10},{10... | collective-permute-start | bytes 6488072 | tf_op jit(solution)/shard_map/ppermute | solution.py:52
  457.4 347.9 %reduce-scatter.5.cloned.1.call-start = ((), (), s32[]{:S(2)}) async-start(), calls=%async_computation.15 | async-start | bytes 7077888 | tf_op jit(solution)/shard_map/reduce_scatter | solution.py:196
  460.9 71.2 %collective-permute-start.2 = (bf16[256,4224]{1,0:T(8,128)(2,1)S(1)}, bf16[256,4224]{1,0:T(8,128)(2,1)S(1)}, u32[]{:S(2)}, u32[]{:S(2)}) collective-permute-start(bf16[256,4224]{1,0:T(8,128)(2,1)S(1)} %get-tuple-element.202), channel_id=1, source_target_pairs={{0,16},{8,24},{16,0},{24,8},{1,17},{9,25},{17,1},{25,9},{2,18},{10... | collective-permute-start | bytes 6488072 | tf_op jit(solution)/shard_map/ppermute | solution.py:52
  463.5 67.4 %collective-permute-start.6 = (bf16[2112,256]{1,0:T(8,128)(2,1)S(1)}, bf16[2112,256]{1,0:T(8,128)(2,1)S(1)}, u32[]{:S(2)}, u32[]{:S(2)}) collective-permute-start(bf16[2112,256]{1,0:T(8,128)(2,1)S(1)} %get-tuple-element.208), channel_id=1, source_target_pairs={{0,16},{8,24},{16,0},{24,8},{1,17},{9,25},{17,1},{25,9},{2,18},{10... | collective-permute-start | bytes 3244040 | tf_op jit(solution)/shard_map/ppermute | solution.py:52
  535.3 71.6 %collective-permute-start.3 = (bf16[256,4224]{1,0:T(8,128)(2,1)S(1)}, bf16[256,4224]{1,0:T(8,128)(2,1)}, u32[]{:S(2)}, u32[]{:S(2)}) collective-permute-start(bf16[256,4224]{1,0:T(8,128)(2,1)S(1)} %get-tuple-element.200), channel_id=1, source_target_pairs={{0,8},{8,0},{16,24},{24,16},{1,9},{9,1},{17,25},{25,17},{2,10},{10... | collective-permute-start | bytes 6488072 | tf_op jit(solution)/shard_map/ppermute | solution.py:52
  538.1 66.3 %collective-permute-start.7 = (bf16[2112,256]{1,0:T(8,128)(2,1)}, bf16[2112,256]{1,0:T(8,128)(2,1)}, u32[]{:S(2)}, u32[]{:S(2)}) collective-permute-start(bf16[2112,256]{1,0:T(8,128)(2,1)} %get-tuple-element.206), channel_id=1, source_target_pairs={{0,8},{8,0},{16,24},{24,16},{1,9},{9,1},{17,25},{25,17},{2,10},{10... | collective-permute-start | bytes 3244040 | tf_op jit(solution)/shard_map/ppermute | solution.py:52
  734.3 144.0 %reduce-scatter.7.cloned.1.call-start = ((), (), s32[]{:S(2)}) async-start(), calls=%async_computation.16 | async-start | bytes 7520256 | tf_op jit(solution)/shard_map/reduce_scatter | solution.py:208
  802.5 132.9 %all-gather.19.cloned.1.call-start = ((), (), s32[]{:S(2)}) async-start(), calls=%async_computation.17 | async-start | bytes 3932160 | tf_op jit(solution)/shard_map/all_gather | solution.py:268
  995.0 42.1 %all-to-all-start.3 = ((bf16[2,4,96,2048]{3,2,0,1:T(8,128)(2,1)}), bf16[2,4,96,2048]{3,2,0,1:T(8,128)(2,1)}, u32[]{:S(2)}, u32[]{:S(2)}) async-start(bf16[2,4,96,2048]{3,2,0,1:T(8,128)(2,1)} %copy.405), calls=%async_computation.5 | async-start | bytes 6291456 | tf_op jit(solution)/shard_map/all_to_all | solution.py:284
  999.7 321.6 %all-reduce.4.cloned.1.call-start = ((), (), s32[]{:S(2)}) async-start(), calls=%async_computation.20 | async-start | bytes 229376
  1016.4 114.1 %collective-permute-start.10 = (bf16[512,4224]{1,0:T(8,128)(2,1)}, bf16[512,4224]{1,0:T(8,128)(2,1)}, u32[]{:S(2)}, u32[]{:S(2)}) collective-permute-start(bf16[512,4224]{1,0:T(8,128)(2,1)} %convolution_convert_fusion.2), channel_id=1, source_target_pairs={{0,16},{8,24},{16,0},{24,8},{1,17},{9,25},{17,1},{25,9},{2,18},{10... | collective-permute-start | bytes 12976136 | tf_op jit(solution)/shard_map/ppermute | solution.py:52
  1042.3 283.3 %reduce-scatter.11.cloned.1.call-start = ((), (), s32[]{:S(2)}) async-start(), calls=%async_computation.19 | async-start | bytes 2359296 | tf_op jit(solution)/shard_map/reduce_scatter | solution.py:297
  1047.6 289.0 %reduce-scatter.9.cloned.1.call-start = ((), (), s32[]{:S(2)}) async-start(), calls=%async_computation.18 | async-start | bytes 7077888 | tf_op jit(solution)/shard_map/reduce_scatter | solution.py:294
  1064.8 148.4 %collective-permute-start.8 = (bf16[512,4224]{1,0:T(8,128)(2,1)}, bf16[512,4224]{1,0:T(8,128)(2,1)}, u32[]{:S(2)}, u32[]{:S(2)}) collective-permute-start(bf16[512,4224]{1,0:T(8,128)(2,1)} %convolution_convert_fusion.3), channel_id=1, source_target_pairs={{0,8},{8,0},{16,24},{24,16},{1,9},{9,1},{17,25},{25,17},{2,10},{10... | collective-permute-start | bytes 12976136 | tf_op jit(solution)/shard_map/ppermute | solution.py:52
  1075.1 101.0 %collective-permute-start.14 = (bf16[2112,512]{1,0:T(8,128)(2,1)}, bf16[2112,512]{1,0:T(8,128)(2,1)}, u32[]{:S(2)}, u32[]{:S(2)}) collective-permute-start(bf16[2112,512]{1,0:T(8,128)(2,1)} %pad_maximum_fusion.5), channel_id=1, source_target_pairs={{0,16},{8,24},{16,0},{24,8},{1,17},{9,25},{17,1},{25,9},{2,18},{10... | collective-permute-start | bytes 6488072 | tf_op jit(solution)/shard_map/ppermute | solution.py:52
  1084.0 124.6 %collective-permute-start.12 = (bf16[2112,512]{1,0:T(8,128)(2,1)}, bf16[2112,512]{1,0:T(8,128)(2,1)}, u32[]{:S(2)}, u32[]{:S(2)}) collective-permute-start(bf16[2112,512]{1,0:T(8,128)(2,1)} %pad_maximum_fusion.4), channel_id=1, source_target_pairs={{0,8},{8,0},{16,24},{24,16},{1,9},{9,1},{17,25},{25,17},{2,10},{10... | collective-permute-start | bytes 6488072 | tf_op jit(solution)/shard_map/ppermute | solution.py:52
  1134.0 120.9 %collective-permute-start.11 = (bf16[256,4224]{1,0:T(8,128)(2,1)S(1)}, bf16[256,4224]{1,0:T(8,128)(2,1)}, u32[]{:S(2)}, u32[]{:S(2)}) collective-permute-start(bf16[256,4224]{1,0:T(8,128)(2,1)S(1)} %fusion.19), channel_id=1, source_target_pairs={{0,8},{8,0},{16,24},{24,16},{1,9},{9,1},{17,25},{25,17},{2,10},{10... | collective-permute-start | bytes 6488072 | tf_op jit(solution)/shard_map/ppermute | solution.py:52
  1212.4 62.8 %collective-permute-start.15 = (bf16[2112,256]{1,0:T(8,128)(2,1)}, bf16[2112,256]{1,0:T(8,128)(2,1)}, u32[]{:S(2)}, u32[]{:S(2)}) collective-permute-start(bf16[2112,256]{1,0:T(8,128)(2,1)} %get-tuple-element.189), channel_id=1, source_target_pairs={{0,8},{8,0},{16,24},{24,16},{1,9},{9,1},{17,25},{25,17},{2,10},{10... | collective-permute-start | bytes 3244040 | tf_op jit(solution)/shard_map/ppermute | solution.py:52
  1213.0 62.1 %collective-permute-start.13 = (bf16[2112,256]{1,0:T(8,128)(2,1)}, bf16[2112,256]{1,0:T(8,128)(2,1)}, u32[]{:S(2)}, u32[]{:S(2)}) collective-permute-start(bf16[2112,256]{1,0:T(8,128)(2,1)} %get-tuple-element.190), channel_id=1, source_target_pairs={{0,16},{8,24},{16,0},{24,8},{1,17},{9,25},{17,1},{25,9},{2,18},{10... | collective-permute-start | bytes 3244040 | tf_op jit(solution)/shard_map/ppermute | solution.py:52
  1260.4 44.1 %collective-permute-start.9 = (bf16[256,4224]{1,0:T(8,128)(2,1)}, bf16[256,4224]{1,0:T(8,128)(2,1)}, u32[]{:S(2)}, u32[]{:S(2)}) collective-permute-start(bf16[256,4224]{1,0:T(8,128)(2,1)} %get-tuple-element.181), channel_id=1, source_target_pairs={{0,16},{8,24},{16,0},{24,8},{1,17},{9,25},{17,1},{25,9},{2,18},{10... | collective-permute-start | bytes 6488072 | tf_op jit(solution)/shard_map/ppermute | solution.py:52
  1265.0 62.3 %all-to-all-start.4 = ((bf16[2,12,8,4096]{3,0,1,2:T(2,128)(2,1)}), bf16[2,12,8,4096]{3,0,1,2:T(2,128)(2,1)S(1)}, u32[]{:S(2)}, u32[]{:S(2)}) async-start(bf16[2,12,8,4096]{3,0,1,2:T(2,128)(2,1)} %copy.406), calls=%async_computation.6 | async-start | bytes 3145728 | tf_op jit(solution)/shard_map/all_to_all | solution.py:290
  1336.6 11.7 all-to-all-start.5
  (94 other events, 2695.9 us)
Sparse Core Ops, SparseCore 0:
  94.0 46.8 all-gather.8
  143.1 64.7 all-gather.10
  209.5 27.7 all-gather.12
  295.2 63.3 all-gather.16
  457.6 66.9 all-gather.14
  734.4 69.5 reduce-scatter.4
  806.3 71.8 reduce-scatter.6
  893.1 42.2 all-gather.18
  1042.4 120.8 all-reduce.3
  1165.5 36.2 reduce-scatter.10
  1204.3 68.7 reduce-scatter.8

commit v2 on v1

--- a/solution.py
+++ b/solution.py
@@ -1,6 +1,10 @@
+import functools
+
 import jax
 import jax.numpy as jnp
 from jax import lax
+from jax.experimental import pallas as pl
+from jax.experimental.pallas import tpu as pltpu
 from jax.sharding import PartitionSpec as P
 
 H = 16
@@ -11,6 +15,8 @@
 MASKED = -1e30
 F32 = jnp.float32
 BF16 = jnp.bfloat16
+MESH = pl.DeviceIdType.MESH
+VMEM_LIMIT = 56 * 2**20
 
 ORDER = ((0, 0), (0, 1), (2, 0), (1, 1), (1, 0), (3, 0), (2, 1), (3, 1))
 
@@ -66,17 +72,241 @@
     return grad_gate, grad_up
 
 
-def gather_in(a, b):
-    half = a.shape[0] // 2
-    ax, ay = across(a, 1), across(a, 2)
-    ad0, ad1 = across(ax[:half], 2), across(ay[half:], 1)
-    full_a = jnp.concatenate([a, ay[:half], ax[half:], ax[:half], ad0, ay[half:], ad1], axis=0)
-    bx, by = across(b, 1), across(b, 2)
-    bd0, bd1 = across(bx[:, :half], 2), across(by[:, half:], 1)
-    full_b = jnp.concatenate(
-        [b, by[:, :half], bx[:, half:], bx[:, :half], bd0, by[:, half:], bd1], axis=1
-    )
-    return full_a, full_b
+def partners(s):
+    return s + 1 - 2 * lax.rem(s, 2), lax.rem(s + 2, 4), 3 - s
+
+
+def greet(s, f, S, N):
+    barrier = pltpu.get_barrier_semaphore()
+    for other in partners(s):
+        pl.semaphore_signal(barrier, inc=1, device_id=(other, f), device_id_type=MESH)
+    for step in range(1, N):
+        pl.semaphore_signal(barrier, inc=1, device_id=(s, lax.rem(f + step, N)), device_id_type=MESH)
+    pl.semaphore_wait(barrier, S - 1 + N - 1)
+
+
+class Line:
+    def __init__(self, s, f, N, block, move_send, move_recv, side_send, side_recv):
+        self.s, self.chip, self.core, self.n = s, f // 2, lax.rem(f, 2), N // 2
+        self.block = block
+        self.move_send, self.move_recv = move_send, move_recv
+        self.side_send, self.side_recv = side_send, side_recv
+
+    def move(self, way, step, origin, to):
+        ref = self.block(2 * origin + self.core)
+        return pltpu.make_async_remote_copy(
+            ref, ref, self.move_send.at[way, step], self.move_recv.at[way, step],
+            device_id=(self.s, 2 * to + self.core), device_id_type=MESH,
+        )
+
+    def side(self, origin, core):
+        ref = self.block(2 * origin + core)
+        return pltpu.make_async_remote_copy(
+            ref, ref, self.side_send.at[origin], self.side_recv.at[origin],
+            device_id=(self.s, 2 * self.chip + 1 - self.core), device_id_type=MESH,
+        )
+
+    def send(self, step, act):
+        q, n = self.chip, self.n
+
+        @pl.when((q - step >= 0) & (q + 1 < n))
+        def _():
+            act(self.move(0, step, jnp.maximum(q - step, 0), jnp.minimum(q + 1, n - 1)))
+
+        @pl.when((q + step < n) & (q >= 1))
+        def _():
+            act(self.move(1, step, jnp.minimum(q + step, n - 1), jnp.maximum(q - 1, 0)))
+
+    def begin(self):
+        self.send(0, lambda copy: copy.start())
+        self.side(self.chip, self.core).start()
+
+    def step(self, step):
+        q, n = self.chip, self.n
+
+        @pl.when(q - 1 - step >= 0)
+        def _():
+            origin = jnp.maximum(q - 1 - step, 0)
+            self.move(0, step, origin, jnp.maximum(q - 1, 0)).wait_recv()
+            if step + 1 < n - 1:
+
+                @pl.when(q + 1 < n)
+                def _():
+                    self.move(0, step + 1, origin, jnp.minimum(q + 1, n - 1)).start()
+
+            self.side(origin, self.core).start()
+
+        @pl.when(q + 1 + step < n)
+        def _():
+            origin = jnp.minimum(q + 1 + step, n - 1)
+            self.move(1, step, origin, jnp.minimum(q + 1, n - 1)).wait_recv()
+            if step + 1 < n - 1:
+
+                @pl.when(q >= 1)
+                def _():
+                    self.move(1, step + 1, origin, jnp.maximum(q - 1, 0)).start()
+
+            self.side(origin, self.core).start()
+
+    def finish(self):
+        for step in range(self.n - 1):
+            self.send(step, lambda copy: copy.wait_send())
+        for origin in range(self.n):
+            self.side(origin, self.core).wait_send()
+            self.side(origin, 1 - self.core).wait_recv()
+
+
+PLACE = {key: i for i, key in enumerate(ORDER)}
+
+
+def prologue_kernel(
+    S, N, shapes, tok, cot, wq, wo, small, *rest,
+):
+    shards_in, rest = rest[:6], rest[6:]
+    d_tok, g_all, w_in, w_back, small_all, *rest = rest
+    fulls, rest = rest[:6], rest[6:]
+    bounce, rest = rest[:11], rest[11:]
+    local_sem, deal_send, deal_recv, seq_send, seq_recv, small_send, small_recv, half_send, half_recv, *line_sems = rest
+    s, f = lax.axis_index("seq"), lax.axis_index("fsdp")
+    px, py, pd = partners(s)
+    eighth = shapes[0]
+
+    def spot(full, i, place):
+        cut = pl.ds(place * eighth, eighth)
+        return full.at[cut] if i < 4 else full.at[:, cut]
+
+    def own_half(shard, i, half):
+        cut = pl.ds(half * eighth, eighth)
+        return shard.at[cut] if i < 4 else shard.at[:, cut]
+
+    places = [small_all.at[f, s], w_in.at[s, f], w_back.at[f], d_tok.at[f], g_all.at[f, f]]
+    for i in range(6):
+        cut = pl.ds(0, 2 * eighth)
+        places.append(fulls[i].at[cut] if i < 4 else fulls[i].at[:, cut])
+    sources = [small, wq.at[s], wo, tok.at[f], cot.at[f], *shards_in]
+    take = [pltpu.make_async_copy(src, by, local_sem.at[i]) for i, (src, by) in enumerate(zip(sources, bounce))]
+    put = [pltpu.make_async_copy(by, dst, local_sem.at[i]) for i, (by, dst) in enumerate(zip(bounce, places))]
+    for copy in take:
+        copy.start()
+    greet(s, f, S, N)
+
+    def remote(src, dst, send, recv, device):
+        return pltpu.make_async_remote_copy(src, dst, send, recv, device_id=device, device_id_type=MESH)
+
+    over_seq = []
+    for k, other in enumerate((px, py, pd)):
+        over_seq.append(remote(small, small_all.at[f, s], seq_send.at[0, k], seq_recv.at[0, k], (other, f)))
+        over_seq.append(remote(wq.at[other], w_in.at[s, f], seq_send.at[1, k], seq_recv.at[1, k], (other, f)))
+    for copy in over_seq:
+        copy.start()
+    dealt = []
+    for k in range(1, N):
+        to = lax.rem(f + k, N)
+        dealt.append(remote(tok.at[to], d_tok.at[f], deal_send.at[0, k - 1], deal_recv.at[0, k - 1], (s, to)))
+    for k in range(1, N):
+        to = lax.rem(f + k, N)
+        dealt.append(remote(cot.at[to], g_all.at[to, f], deal_send.at[1, k - 1], deal_recv.at[1, k - 1], (s, to)))
+    for copy in dealt:
+        copy.start()
+
+    def half_copy(i, k):
+        where, rel, half = ((px, 1, 0), (py, 2, 1), (py, 2, 0), (px, 1, 1))[k]
+        return remote(
+            own_half(shards_in[i], i, half), spot(fulls[i], i, PLACE[rel, half]), half_send.at[i, k], half_recv.at[i, k],
+            (where, f),
+        )
+
+    def pass_on(i, k):
+        where, rel, half = ((py, 1, 0), (px, 2, 1))[k]
+        return remote(
+            spot(fulls[i], i, PLACE[rel, half]), spot(fulls[i], i, PLACE[3, half]), half_send.at[i, 4 + k],
+            half_recv.at[i, 4 + k], (where, f),
+        )
+
+    for i in range(6):
+        for k in range(4):
+            half_copy(i, k).start()
+
+    for copy, after in zip(take, put):
+        copy.wait()
+        after.start()
+    for copy in put:
+        copy.wait()
+    for copy in over_seq:
+        copy.wait_recv()
+    to_all = []
+    for k in range(1, N):
+        to = lax.rem(f + k, N)
+        to_all.append(remote(small_all.at[f], small_all.at[f], small_send.at[k - 1], small_recv.at[k - 1], (s, to)))
+    for copy in to_all:
+        copy.start()
+    lines = [
+        Line(s, f, N, lambda j: w_in.at[:, j], *line_sems[0:4]),
+        Line(s, f, N, lambda j: w_back.at[j], *line_sems[4:8]),
+        Line(s, f, N, lambda j: g_all.at[j], *line_sems[8:12]),
+    ]
+    lines[0].begin()
+    lines[1].begin()
+    for copy in dealt:
+        copy.wait_recv()
+    for step in range(N // 2 - 1):
+        lines[0].step(step)
+        lines[1].step(step)
+    lines[2].begin()
+    for step in range(N // 2 - 1):
+        lines[2].step(step)
+    for i in range(6):
+        for k in range(2):
+            half_copy(i, k).wait_recv()
+            pass_on(i, k).start()
+    for i in range(6):
+        for k in range(2, 4):
+            half_copy(i, k).wait_recv()
+        for k in range(2):
+            pass_on(i, k).wait_recv()
+    for i in range(6):
+        for k in range(4):
+            half_copy(i, k).wait_send()
+        for k in range(2):
+            pass_on(i, k).wait_send()
+    for line in lines:
+        line.finish()
+    for copy in over_seq + dealt:
+        copy.wait_send()
+    for copy in to_all:
+        copy.wait()
+
+
+def prologue(S, N, tok, cot, wq, wo, small, shards_in):
+    D = wo.shape[1]
+    own = wo.shape[0]
+    chips = N // 2
+    dma = pltpu.SemaphoreType.DMA
+    line = [dma((2, chips - 1)), dma((2, chips - 1)), dma((chips,)), dma((chips,))]
+    out = [
+        jax.ShapeDtypeStruct(tok.shape, BF16),
+        jax.ShapeDtypeStruct((N,) + cot.shape, BF16),
+        jax.ShapeDtypeStruct((S, N) + wq.shape[1:], BF16),
+        jax.ShapeDtypeStruct((N,) + wo.shape, BF16),
+        jax.ShapeDtypeStruct((N, S) + small.shape, F32),
+    ]
+    for i, shard in enumerate(shards_in):
+        rows, columns = shard.shape
+        out.append(jax.ShapeDtypeStruct((4 * rows, columns) if i < 4 else (rows, 4 * columns), BF16))
+    anywhere = pl.BlockSpec(memory_space=pl.ANY)
+    return pl.pallas_call(
+        functools.partial(prologue_kernel, S, N, (D // 8,)),
+        out_shape=out,
+        in_specs=[anywhere] * 11,
+        out_specs=[anywhere] * 11,
+        scratch_shapes=[pltpu.VMEM(u.shape, u.dtype) for u in (small, wq[0], wo, tok[0], cot[0], *shards_in)]
+        + [
+            dma((11,)), dma((2, N - 1)), dma((2, N - 1)), dma((2, 3)), dma((2, 3)), dma((N - 1,)), dma((N - 1,)),
+            dma((6, 6)), dma((6, 6)),
+        ] + line * 3,
+        compiler_params=pltpu.CompilerParams(collective_id=0, has_side_effects=True, vmem_limit_bytes=VMEM_LIMIT),
+        name="prologue",
+    )(tok, cot, wq, wo, small, *shards_in)
 
 
 def shards(
@@ -96,47 +326,56 @@
     rows = N * MB * T
     own = w_out.shape[0]
 
-    stack_a = jnp.concatenate([e_gate[0], e_up[0], s_gate, s_up], axis=1)
-    stack_b = jnp.concatenate([e_down[0], s_down], axis=0)
-    full_a, full_b = gather_in(stack_a, stack_b)
-
-    small = jnp.concatenate([gain_attn, gain_ffn, w_router.reshape(-1), w_shared_gate, b_qkv])
-    small = lax.all_gather(small, ("seq", "fsdp"), axis=0)
-    cuts = (own, 2 * own, 2 * own + own * E, 3 * own + own * E)
-    gain_1 = small[:, : cuts[0]].reshape(D).astype(F32)
-    gain_2 = small[:, cuts[0] : cuts[1]].reshape(D).astype(F32)
-    router_w = small[:, cuts[1] : cuts[2]].reshape(D, E)
-    shared_w = small[:, cuts[2] : cuts[3]].reshape(D)
-    bias = lax.dynamic_slice_in_dim(small[:, cuts[3] :].reshape(3, S, width), s, 1, 1)
-    bias = bias.reshape(3 * width).astype(F32)
-
-    w = lax.all_to_all(w_qkv.reshape(own, 3, S, width), "seq", split_axis=2, concat_axis=0, tiled=True)
-    w = lax.all_gather(w.reshape(S, own, 3 * width), "fsdp", axis=1, tiled=True)
-    w_in = w.reshape(D, 3 * width)
-    w_back = lax.all_gather(w_out, "fsdp", axis=0, tiled=True)
-
-    pad = 128
-    extra = jnp.pad(ids.astype(BF16), ((0, 0), (0, 0), (0, pad - TOP)))
-    send = jnp.concatenate([tokens, cotangent, extra], axis=2).reshape(MB, piece, N, 2 * D + pad)
-    inverse_deal = jnp.argsort(deal[:, f], axis=1)
-    send = jnp.stack([jnp.take(send[m], inverse_deal[m], axis=1) for m in range(MB)])
-    dealt = lax.all_to_all(send, "fsdp", split_axis=2, concat_axis=2, tiled=True)
-    dealt = dealt.reshape(MB, T, 2 * D + pad)
-    x0 = dealt[..., :D].astype(F32)
-    cot = dealt[..., D : 2 * D]
-    tags = dealt[..., 2 * D :]
-
     order = jnp.stack([jnp.bitwise_xor(s, rel) * 2 + half for rel, half in ORDER])
     inverse_order = jnp.argsort(order)
 
     def arrange(u, by):
         return jnp.take(u.reshape(u.shape[:-1] + (8, D // 8)), by, axis=u.ndim - 1).reshape(u.shape)
 
-    g_all = lax.all_gather(
-        jnp.concatenate([arrange(cot, order), tags], axis=2).reshape(MB * T, D + pad), "fsdp", axis=0, tiled=True
-    )
-    g_rows = g_all[:, :D]
-    chosen = g_all[:, D : D + TOP].astype(jnp.int32)
+    inverse_deal = jnp.argsort(deal, axis=2)
+
+    def deal_out(u):
+        u = u.reshape(MB, piece, N, D)
+        u = jnp.stack([jnp.take(u[m], inverse_deal[m, f], axis=1) for m in range(MB)])
+        return u.transpose(2, 0, 1, 3).reshape(N, MB * piece, D)
+
+    small = jnp.concatenate([gain_attn, gain_ffn, w_router.reshape(-1), w_shared_gate, b_qkv]).astype(F32)
+    small = jnp.concatenate([small, ids.reshape(-1).astype(F32)])
+    n_small = small.shape[0]
+    small = jnp.pad(small, (0, -n_small % 1024)).reshape(-1, 128)
+    wq = w_qkv.reshape(own, 3, S, width).transpose(2, 0, 1, 3).reshape(S, own, 3 * width)
+    d_tok, g_all, w_in, w_back, small, *fulls = prologue(
+        S, N, deal_out(tokens), deal_out(arrange(cotangent, order)), wq, w_out, small,
+        (e_gate[0], e_up[0], s_gate, s_up, e_down[0], s_down),
+    )
+    small = small.reshape(N, S, -1)[:, :, :n_small]
+    cuts = (own, 2 * own, 2 * own + own * E, 3 * own + own * E, 6 * own + own * E)
+    small, all_ids = small[:, :, : cuts[4]].swapaxes(0, 1).reshape(S * N, cuts[4]), small[:, :, cuts[4] :]
+    gain_1 = small[:, : cuts[0]].reshape(D)
+    gain_2 = small[:, cuts[0] : cuts[1]].reshape(D)
+    router_w = small[:, cuts[1] : cuts[2]].reshape(D, E).astype(BF16)
+    shared_w = small[:, cuts[2] : cuts[3]].reshape(D).astype(BF16)
+    bias = lax.dynamic_slice_in_dim(small[:, cuts[3] :].reshape(3, S, width), s, 1, 1).reshape(3 * width)
+    w_in, w_back = w_in.reshape(D, 3 * width), w_back.reshape(width, D)
+    eg, eu, sg, su, ed, sd = fulls
+    x0 = d_tok.reshape(N, MB, piece, D).transpose(1, 2, 0, 3).reshape(MB, T, D).astype(F32)
+    d_cot = lax.dynamic_index_in_dim(g_all, f, 0, keepdims=False)
+    cot = arrange(d_cot.reshape(N, MB, piece, D).transpose(1, 2, 0, 3).reshape(MB, T, D), inverse_order)
+    g_rows = g_all.reshape(rows, D)
+    all_ids = lax.dynamic_index_in_dim(all_ids, s, 1, keepdims=False).reshape(N, MB, piece, N, TOP)
+    where = inverse_deal.transpose(2, 1, 0)
+    chosen = jnp.take_along_axis(
+        all_ids[None], where[:, :, :, None, None, None], axis=4
+    ).reshape(N, MB * T, TOP).astype(jnp.int32)
+    own_ids = lax.dynamic_index_in_dim(chosen, f, 0, keepdims=False)
+    own_ids = own_ids.reshape(N, MB, piece, TOP).transpose(1, 2, 0, 3).reshape(MB * T, TOP)
+    chosen = chosen.reshape(rows, TOP)
+
+    def to_rows(u):
+        return u.reshape(MB, piece, N, -1).transpose(2, 0, 1, 3).reshape(MB * T, -1)
+
+    def to_pack(u):
+        return u.reshape(N, MB, piece, -1).transpose(1, 2, 0, 3).reshape(MB * T, -1)
 
     ends = jnp.cumsum(lengths[:, f], axis=1)
     spots = jnp.arange(pack, dtype=jnp.int32)
@@ -172,7 +411,7 @@
     unit_2, inverse_2 = rms_forward(hidden)
     normed2 = (unit_2 * gain_2).astype(BF16)
 
-    x = lax.all_gather(arrange(normed2, order).reshape(MB * T, D), "fsdp", axis=0, tiled=True)
+    x = lax.all_gather(to_rows(arrange(normed2, order)), "fsdp", axis=0, tiled=True)
     lead = jnp.concatenate([router_w, shared_w[:, None]], axis=1)
     lead_order = jnp.take(lead.reshape(8, D // 8, E + 1), order, axis=0).reshape(D, E + 1)
     logits = dot(x, lead_order)
@@ -184,8 +423,6 @@
     geo = (gate_f * g32).astype(BF16)
     gso = (sigma_rows * g32).astype(BF16)
 
-    eg, eu, sg, su = jnp.split(full_a, (FE, 2 * FE, 2 * FE + FS), axis=1)
-    ed, sd = full_b[:FE], full_b[FE:]
     gate, up = dot(x, eg), dot(x, eu)
     act = (jax.nn.silu(gate) * up).astype(BF16)
     out_e = dot(act, ed).astype(BF16).astype(F32)
@@ -243,7 +480,8 @@
     )
     g_eg, g_eu, g_sg, g_su = jnp.split(grad_a, (FE, 2 * FE, 2 * FE + FS), axis=1)
 
-    y = arrange(y.astype(F32).reshape(MB, T, D), inverse_order)
+    y = arrange(to_pack(y).astype(F32).reshape(MB, T, D), inverse_order)
+    dx = to_pack(dx)
     mixed = (hidden + y).astype(BF16)
     base = D
     gg_own = sum(dx[:, base + i * N : base + (i + 1) * N] for i in range(3))
@@ -254,7 +492,6 @@
     shifted = jnp.exp(logits[:, :E] - jnp.max(logits[:, :E], axis=-1, keepdims=True))
     router = shifted / jnp.sum(shifted, axis=-1, keepdims=True)
     sigma = jax.nn.sigmoid(logits[:, E])
-    own_ids = tags[..., :TOP].reshape(MB * T, TOP).astype(jnp.int32)
     picked = jnp.any(own_ids[:, :, None] == jnp.arange(E)[None, None, :], axis=1)
     grad_router = jnp.where(picked, gg_own, 0.0)
     grad_logits = (router * (grad_router - jnp.sum(router * grad_router, axis=-1, keepdims=True))).astype(BF16)

time: 1370 us -> 1200 us (0.88)
  waiting for transfers between devices: 655 us -> 352 us
  Pallas kernels: 0 us -> 233 us
  blocking collectives: 90.4 us -> 0 us
    ppermute x16 -> x8, waiting for transfers between devices: 410 us -> 119 us  [across(): return lax.ppermute(a, 'seq', [(i, i ^ which) for i in range(4)])]
    pallas_call x0 -> x1, Pallas kernels: none -> 233 us  [prologue(): pl.pallas_call(functools.partial(prologue_kernel, S, N, (D // 8,)), out_s...]
    all_gather x1 -> x0, blocking collectives: 68.1 us -> none  [shards(): small = lax.all_gather(small, ('seq', 'fsdp'), axis=0)]
    all_gather x1, waiting for transfers between devices: 15.9 us -> 41.3 us  [shards(): normed_all = lax.all_gather(normed, 'seq', axis=1, tiled=True)]
    all_to_all x1 -> x0, blocking collectives: 22.3 us -> none  [shards(): lax.all_to_all(w_qkv.reshape(own, 3, S, width), 'seq', split_axis=2, conc...]
    all_gather x1, waiting for transfers between devices: 41.2 us -> 26.9 us  [shards(): lax.all_gather(grad_hidden.astype(BF16), 'seq', axis=1, tiled=True)]
    convert_element_type x4 -> x15, local copies, waits for them, and re-layouts: 0.22 us -> 14 us  [the longest x3 5.41 us: shards(): y = arrange(to_pack(y).astype(F32).reshape(MB, T, D), inverse_order)]
    unnamed x213 -> x223, local copies, waits for them, and re-layouts: 36.8 us -> 24 us
  transfers between devices with their start and end apart: 32 -> 20, of which waited for: 18 -> 11; matrix products, arithmetic and copies ran while one was open for 26% -> 23% of each run, Pallas kernels for 0% -> 0%
where the time goes in v2:
time: 1200 us; the launch traced here: 1190 us
  waiting for transfers between devices  352 us (29%)
  matrix products  318 us (26%)
  Pallas kernels  233 us (19%)
  local copies, waits for them, and re-layouts  146 us (12%)
  other arithmetic  93.9 us (8%)
  starting transfers between devices  27.6 us (2%)
  between operations  16.4 us (1%)
    pallas_call x1, Pallas kernels, prologue(): pl.pallas_call(functools.partial(prologue_kernel, S, N, (D // 8,)), out_s...  233 us
    ppermute x8, waiting for transfers between devices, across(): return lax.ppermute(a, 'seq', [(i, i ^ which) for i in range(4)])  119 us
    dot_general x12, matrix products, dot_t(): lax.dot_general(a, b, (((0,), (0,)), ((), ())), preferred_element_type=F32)  101 us
    dot_general x10, matrix products, dot(): return jnp.dot(a, b, preferred_element_type=F32)  97.2 us
    dot_general x9, matrix products, dot_nt(): lax.dot_general(a, b, (((1,), (1,)), ((), ())), preferred_element_type=F32)  90.7 us
    all_gather x1, waiting for transfers between devices, shards(): lax.all_gather(to_rows(arrange(normed2, order)), 'fsdp', axis=0, tiled=True)  60.2 us
    reduce_scatter x1, waiting for transfers between devices, shards(): lax.psum_scatter(payload, 'fsdp', scatter_dimension=0, tiled=True)  59.2 us
    all_gather x1, waiting for transfers between devices, shards(): normed_all = lax.all_gather(normed, 'seq', axis=1, tiled=True)  41.3 us
  transfers between devices with their start and end apart: 20, of which 11 were waited for; matrix products, arithmetic and copies ran while one was open for 23% of the time, Pallas kernels for 0%

profile of v2, /device:TPU:0, one launch (start us, length us, event | category | flops | bytes accessed | tf_op | source)
XLA Modules:
  0.0 1187.8 jit_solution(7031734325924153200)
XLA Ops:
  36.6 233.2 %prologue.1 = (bf16[8,24,2048]{2,1,0:T(8,128)(2,1)}, bf16[8,8,24,2048]{3,2,1,0:T(8,128)(2,1)}, bf16[4,8,64,1536]{3,2,1,0:T(8,128)(2,1)}, bf16[8,64,2048]{2,1,0:T...) custom-call(bf16[8,24,2048]{2,1,0:T(8,128)(2,1)} %copy.679.tok, ...), custom_call_target="tpu_custom_call" | custom-call | tf_op jit(solution)/shard_map/prologue/pallas_call | solution.py:297
  277.3 41.3 %all-gather.4.cloned.1.call-done = bf16[2,384,2048]{2,1,0:T(8,128)(2,1)} async-done(((bf16[2,96,2048]{2,1,0:T(8,128)(2,1)}), bf16[2,384,2048]{2,1,0:T(8,128)(2,1)}) %all-gather.4.cloned.1.call-update) | async-done | bytes 3145744 | tf_op jit(solution)/shard_map/all_gather | solution.py:394
  318.6 9.5 convolution_add_fusion
  359.1 34.0 %all-to-all-done = bf16[2,4,96,2048]{3,2,0,1:T(8,128)(2,1)} async-done(((bf16[2,4,96,2048]{3,2,0,1:T(8,128)(2,1)}), bf16[2,4,96,2048]{3,2,0,1:T(8,128)(2,1)}, u32[]{:S(2)}, u32[]{:S(2)}) %all-to-all-start) | async-done | bytes 3145760 | tf_op jit(solution)/shard_map/all_to_all | solution.py:409
  408.2 60.2 %all-gather.6.cloned.1.call-done = bf16[1536,2048]{1,0:T(8,128)(2,1)} async-done(((bf16[192,2048]{1,0:T(8,128)(2,1)}), bf16[1536,2048]{1,0:T(8,128)(2,1)}) %all-gather.6.cloned.1.call-update) | async-done | bytes 6291472 | tf_op jit(solution)/shard_map/all_gather | solution.py:414
  473.2 9.0 fusion.4
  482.2 11.4 fusion.158
  493.6 12.2 %fusion.156 = f32[1536,1408]{0,1:T(8,128)} fusion(bf16[1536,2048]{1,0:T(8,128)(2,1)S(1)} %bitcast.350, bf16[2048,1408]{1,0:T(8,128)(2,1)S(1)} %bitcast.401), kind=kOutput, calls=%fused_computation.353 | convolution fusion | flops 8858370048 | bytes 20709376 | tf_op jit(solution)/shard_map/dot_general | solution.py:25
  505.8 20.3 %multiply_convert_fusion.2 = (bf16[1536,1408]{0,1:T(8,128)(2,1)}, bf16[1536,1408]{0,1:T(8,128)(2,1)}, bf16[1536,1408]{0,1:T(8,128)(2,1)}) fusion(f32[1536,1408]{0,1:T(8,128)} %fusion.156, f32[1536,1408]{0,1:T(8,128)} %fusion.158, bf16[1536,2048]{1,0:T(8,128)(2,1)S(1)} %bitcast.350, bf16[2048,1408]{1,0:T(8,128)(2,1)} %get-tuple-element.38), kind=kOutput, calls=%fused_computation.43 | convolution fusion | flops 8892973056 | bytes 42336256 | tf_op jit(solution)/shard_map/dot_general | solution.py:25
  526.1 15.3 %convolution_convert_fusion.1 = bf16[1536,2048]{1,0:T(8,128)(2,1)} fusion(bf16[1536,1408]{0,1:T(8,128)(2,1)} %get-tuple-element.219, bf16[1408,2048]{1,0:T(8,128)(2,1)} %get-tuple-element.39), kind=kOutput, calls=%fused_computation.46 | convolution fusion | flops 8861515776 | bytes 16384000 | tf_op jit(solution)/shard_map/dot_general | solution.py:25
  541.5 9.2 fusion.160
  557.4 11.2 multiply_convert_fusion.6
  568.6 13.4 %fusion.7 = (f32[1536]{0:T(1024)S(1)}, f32[1536]{0:T(1024)S(1)}, bf16[1536,2048]{1,0:T(8,128)(2,1)}) fusion(bf16[8,8,24,2048]{3,2,1,0:T(8,128)(2,1)S(1)} %bitcast.345, bf16[1536,2048]{1,0:T(8,128)(2,1)} %convolution_convert_fusion.1, f32[1536]{0:T(1024)S(1)} %divide_reduce_fusion, f32[1536]{0:T(1024)S(1)} %divide_select_fusion, ...), kind=kOutput, calls=%fused_computation.29 | convolution fusion | flops 4460639232 | bytes 23945216 | tf_op jit(solution)/shard_map/dot_general | solution.py:25
  583.5 16.7 %fusion.159 = f32[1536,2048]{1,0:T(8,128)} fusion(bf16[1536,1408]{0,1:T(8,128)(2,1)} %get-tuple-element.220, bf16[2048,1408]{1,0:T(8,128)(2,1)} %get-tuple-element.37), kind=kOutput, calls=%fused_computation.356 | convolution fusion | flops 8858370048 | bytes 22675456 | tf_op jit(solution)/shard_map/dot_general | solution.py:33
  600.2 8.3 fusion.161
  608.4 17.1 %add_convert_fusion.1 = bf16[1536,2048]{1,0:T(8,128)(2,1)} fusion(f32[1536,2048]{1,0:T(8,128)} %fusion.159, bf16[1536,1408]{0,1:T(8,128)(2,1)} %get-tuple-element.221, bf16[2048,1408]{1,0:T(8,128)(2,1)} %get-tuple-element.38), kind=kOutput, calls=%fused_computation.31 | convolution fusion | flops 8864661504 | bytes 28966912 | tf_op jit(solution)/shard_map/dot_general | solution.py:33
  625.5 11.3 add_convert_fusion
  636.8 11.7 concatenate.90
  661.8 59.2 %reduce-scatter.7.cloned.1.call-done = bf16[192,2176]{1,0:T(8,128)(2,1)} async-done(((bf16[1536,2176]{1,0:T(8,128)(2,1)}), bf16[192,2176]{1,0:T(8,128)(2,1)}) %reduce-scatter.7.cloned.1.call-update) | async-done | bytes 835600 | tf_op jit(solution)/shard_map/reduce_scatter | solution.py:445
  756.8 26.9 %all-gather.8.cloned.1.call-done = bf16[2,384,2048]{2,1,0:T(8,128)(2,1)} async-done(((bf16[2,96,2048]{2,1,0:T(8,128)(2,1)}), bf16[2,384,2048]{2,1,0:T(8,128)(2,1)}) %all-gather.8.cloned.1.call-update) | async-done | bytes 3145744 | tf_op jit(solution)/shard_map/all_gather | solution.py:505
  794.0 9.7 fusion.86
  803.7 9.5 fusion.83
  830.7 8.0 convolution_convert_fusion.5
  898.3 17.1 %convolution_convert_fusion.2 = bf16[512,4224]{1,0:T(8,128)(2,1)} fusion(bf16[1536,2048]{1,0:T(8,128)(2,1)} %all-gather.6.cloned.1.call-done, bf16[1536,704]{0,1:T(8,128)(2,1)} %get-tuple-element.232, bf16[1536,704]{0,1:T(8,128)(2,1)S(1)} %copy-done.75, bf16[1536,1408]{0,1:T(8,128)(2,1)} %get-tuple-element.221, bf16[1536,1408]{0,1:T(8,128)(2,1)} %get-tuple-element.220), kind=kOutput, calls=%fused_computation.47 | convolution fusion | flops 6697844736 | bytes 18874368 | tf_op jit(solution)/shard_map/dot_general | solution.py:29
  916.9 17.3 %convolution_convert_fusion.3 = bf16[512,4224]{1,0:T(8,128)(2,1)} fusion(bf16[1536,2048]{1,0:T(8,128)(2,1)} %all-gather.6.cloned.1.call-done, bf16[1536,704]{0,1:T(8,128)(2,1)} %get-tuple-element.232, bf16[1536,704]{0,1:T(8,128)(2,1)S(1)} %copy-done.75, bf16[1536,1408]{0,1:T(8,128)(2,1)} %get-tuple-element.221, bf16[1536,1408]{0,1:T(8,128)(2,1)} %get-tuple-element.220), kind=kOutput, calls=%fused_computation.48 | convolution fusion | flops 6697844736 | bytes 18874368 | tf_op jit(solution)/shard_map/dot_general | solution.py:29
  942.1 23.3 %fusion.22 = f32[1024,4224]{1,0:T(8,128)} fusion(bf16[1536,2048]{1,0:T(8,128)(2,1)} %all-gather.6.cloned.1.call-done, bf16[1536,704]{0,1:T(8,128)(2,1)} %get-tuple-element.232, bf16[1536,704]{0,1:T(8,128)(2,1)S(1)} %copy-done.75, bf16[1536,1408]{0,1:T(8,128)(2,1)} %get-tuple-element.221, bf16[1536,1408]{0,1:T(8,128)(2,1)} %get-tuple-element.220), kind=kOutput, calls=%fused_computation.84 | convolution fusion | flops 13339459584 | bytes 33423360 | tf_op jit(solution)/shard_map/dot_general | solution.py:29
  965.4 56.6 %collective-permute-done.2 = bf16[512,4224]{1,0:T(8,128)(2,1)} collective-permute-done((bf16[512,4224]{1,0:T(8,128)(2,1)}, bf16[512,4224]{1,0:T(8,128)(2,1)}, u32[]{:S(2)}, u32[]{:S(2)}) %collective-permute-start.2) | collective-permute-done | bytes 4325408 | tf_op jit(solution)/shard_map/ppermute | solution.py:58
  1031.6 7.6 fusion.20
  1045.7 29.9 %collective-permute-done.3 = bf16[256,4224]{1,0:T(8,128)(2,1)S(1)} collective-permute-done((bf16[256,4224]{1,0:T(8,128)(2,1)S(1)}, bf16[256,4224]{1,0:T(8,128)(2,1)S(1)}, u32[]{:S(2)}, u32[]{:S(2)}) %collective-permute-start.3) | collective-permute-done | bytes 2162720 | tf_op jit(solution)/shard_map/ppermute | solution.py:58
  1088.7 9.0 collective-permute-done.7
  1104.6 23.6 %collective-permute-done.1 = bf16[256,4224]{1,0:T(8,128)(2,1)} collective-permute-done((bf16[256,4224]{1,0:T(8,128)(2,1)}, bf16[256,4224]{1,0:T(8,128)(2,1)}, u32[]{:S(2)}, u32[]{:S(2)}) %collective-permute-start.1) | collective-permute-done | bytes 2162720 | tf_op jit(solution)/shard_map/ppermute | solution.py:58
  1166.2 7.6 all-to-all-done.3
  (528 shorter events, 320.9 us)
Async XLA Ops:
  7.2 267.2 %copy-start = (s32[2,8,4]{1,2,0:T(4,128)S(1)}, s32[2,8,4]{1,2,0:T(4,128)}, u32[]{:S(2)}) copy-start(s32[2,8,4]{1,2,0:T(4,128)} %param.28) | copy-start | bytes 772
  7.2 311.4 %all-gather.4.cloned.1.call-start = ((), (), s32[]{:S(2)}) async-start(), calls=%async_computation.8 | async-start | bytes 3932160 | tf_op jit(solution)/shard_map/all_gather | solution.py:394
  271.0 85.6 %copy-start.41 = (f32[32,64]{1,0:T(8,128)}, f32[32,64]{1,0:T(8,128)S(1)}, u32[]{:S(2)}) copy-start(f32[32,64]{1,0:T(8,128)S(1)} %get-tuple-element.260) | copy-start | bytes 24580
  272.7 123.0 %copy-start.2 = (f32[8,24,2048]{2,0,1:T(8,128)}, f32[8,24,2048]{2,0,1:T(8,128)S(1)}, u32[]{:S(2)}) copy-start(f32[8,24,2048]{2,0,1:T(8,128)S(1)} %copy.683) | copy-start | bytes 4718596
  277.0 61.3 %copy-start.19 = (f32[2,384,128]{2,1,0:T(8,128)}, f32[2,384,128]{2,1,0:T(8,128)S(1)}, u32[]{:S(2)}) copy-start(f32[2,384,128]{2,1,0:T(8,128)S(1)} %get-tuple-element.255) | copy-start | bytes 1179652
  277.0 61.3 %copy-start.21 = (f32[2,384,128]{2,1,0:T(8,128)}, f32[2,384,128]{2,1,0:T(8,128)S(1)}, u32[]{:S(2)}) copy-start(f32[2,384,128]{2,1,0:T(8,128)S(1)} %get-tuple-element.256) | copy-start | bytes 1179652
  351.8 41.3 %all-to-all-start = ((bf16[2,4,96,2048]{3,2,0,1:T(8,128)(2,1)}), bf16[2,4,96,2048]{3,2,0,1:T(8,128)(2,1)}, u32[]{:S(2)}, u32[]{:S(2)}) async-start(bf16[2,4,96,2048]{3,2,0,1:T(8,128)(2,1)} %copy.691), calls=%async_computation | async-start | bytes 6291456 | tf_op jit(solution)/shard_map/all_to_all | solution.py:409
  356.6 111.7 %all-gather.6.cloned.1.call-start = ((), (), s32[]{:S(2)}) async-start(), calls=%async_computation.9 | async-start | bytes 7077888 | tf_op jit(solution)/shard_map/all_gather | solution.py:414
  403.4 317.6 %reduce-scatter.7.cloned.1.call-start = ((), (), s32[]{:S(2)}) async-start(), calls=%async_computation.11 | async-start | bytes 7520256 | tf_op jit(solution)/shard_map/reduce_scatter | solution.py:445
  406.0 67.0 %copy-start.13 = (f32[128,12,4]{1,2,0:T(4,128)}, f32[128,12,4]{1,2,0:T(4,128)S(1)}, u32[]{:S(2)}) copy-start(f32[128,12,4]{1,2,0:T(4,128)S(1)} %gather_fusion.3) | copy-start | bytes 73732
  648.6 135.1 %all-gather.8.cloned.1.call-start = ((), (), s32[]{:S(2)}) async-start(), calls=%async_computation.12 | async-start | bytes 3932160 | tf_op jit(solution)/shard_map/all_gather | solution.py:505
  653.6 73.1 %copy-start.54 = (s32[1024]{0:T(1024)}, s32[1024]{0:T(1024)S(1)}, u32[]{:S(2)}) copy-start(s32[1024]{0:T(1024)S(1)} %pad_clamp_fusion.2) | copy-start | bytes 12292
  741.2 118.7 %reduce-scatter.5.cloned.1.call-start = ((), (), s32[]{:S(2)}) async-start(), calls=%async_computation.10 | async-start | bytes 7077888 | tf_op jit(solution)/shard_map/reduce_scatter | solution.py:433
  840.7 42.3 %all-to-all-start.1 = ((bf16[2,4,96,2048]{3,2,0,1:T(8,128)(2,1)}), bf16[2,4,96,2048]{3,2,0,1:T(8,128)(2,1)}, u32[]{:S(2)}, u32[]{:S(2)}) async-start(bf16[2,4,96,2048]{3,2,0,1:T(8,128)(2,1)} %copy.739), calls=%async_computation.3 | async-start | bytes 6291456 | tf_op jit(solution)/shard_map/all_to_all | solution.py:521
  845.5 299.3 %all-reduce.4.cloned.1.call-start = ((), (), s32[]{:S(2)}) async-start(), calls=%async_computation.15 | async-start | bytes 229376
  848.4 190.8 %collective-permute-start.4 = (bf16[2112,512]{1,0:T(8,128)(2,1)}, bf16[2112,512]{1,0:T(8,128)(2,1)}, u32[]{:S(2)}, u32[]{:S(2)}) collective-permute-start(bf16[2112,512]{1,0:T(8,128)(2,1)} %pad_maximum_fusion.2), channel_id=1, source_target_pairs={{0,8},{8,0},{16,24},{24,16},{1,9},{9,1},{17,25},{25,17},{2,10},{10... | collective-permute-start | bytes 6488072 | tf_op jit(solution)/shard_map/ppermute | solution.py:58
  858.5 180.7 %collective-permute-start.6 = (bf16[2112,512]{1,0:T(8,128)(2,1)}, bf16[2112,512]{1,0:T(8,128)(2,1)}, u32[]{:S(2)}, u32[]{:S(2)}) collective-permute-start(bf16[2112,512]{1,0:T(8,128)(2,1)} %pad_maximum_fusion.3), channel_id=1, source_target_pairs={{0,16},{8,24},{16,0},{24,8},{1,17},{9,25},{17,1},{25,9},{2,18},{10... | collective-permute-start | bytes 6488072 | tf_op jit(solution)/shard_map/ppermute | solution.py:58
  892.4 256.7 %reduce-scatter.11.cloned.1.call-start = ((), (), s32[]{:S(2)}) async-start(), calls=%async_computation.14 | async-start | bytes 2359296 | tf_op jit(solution)/shard_map/reduce_scatter | solution.py:534
  897.9 261.9 %reduce-scatter.9.cloned.1.call-start = ((), (), s32[]{:S(2)}) async-start(), calls=%async_computation.13 | async-start | bytes 7077888 | tf_op jit(solution)/shard_map/reduce_scatter | solution.py:531
  915.5 106.5 %collective-permute-start.2 = (bf16[512,4224]{1,0:T(8,128)(2,1)}, bf16[512,4224]{1,0:T(8,128)(2,1)}, u32[]{:S(2)}, u32[]{:S(2)}) collective-permute-start(bf16[512,4224]{1,0:T(8,128)(2,1)} %convolution_convert_fusion.2), channel_id=1, source_target_pairs={{0,16},{8,24},{16,0},{24,8},{1,17},{9,25},{17,1},{25,9},{2,18},{10... | collective-permute-start | bytes 12976136 | tf_op jit(solution)/shard_map/ppermute | solution.py:58
  934.3 111.4 %collective-permute-start = (bf16[512,4224]{1,0:T(8,128)(2,1)}, bf16[512,4224]{1,0:T(8,128)(2,1)}, u32[]{:S(2)}, u32[]{:S(2)}) collective-permute-start(bf16[512,4224]{1,0:T(8,128)(2,1)} %convolution_convert_fusion.3), channel_id=1, source_target_pairs={{0,8},{8,0},{16,24},{24,16},{1,9},{9,1},{17,25},{25,17},{2,10},{10... | collective-permute-start | bytes 12976136 | tf_op jit(solution)/shard_map/ppermute | solution.py:58
  965.4 61.8 %copy-start.73 = (bf16[1536,704]{0,1:T(8,128)(2,1)S(1)}, bf16[1536,704]{0,1:T(8,128)(2,1)}, u32[]{:S(2)}) copy-start(bf16[1536,704]{0,1:T(8,128)(2,1)} %get-tuple-element.230) | copy-start | bytes 6488068
  1025.5 50.0 %collective-permute-start.3 = (bf16[256,4224]{1,0:T(8,128)(2,1)S(1)}, bf16[256,4224]{1,0:T(8,128)(2,1)S(1)}, u32[]{:S(2)}, u32[]{:S(2)}) collective-permute-start(bf16[256,4224]{1,0:T(8,128)(2,1)S(1)} %fusion.9), channel_id=1, source_target_pairs={{0,8},{8,0},{16,24},{24,16},{1,9},{9,1},{17,25},{25,17},{2,10},{10... | collective-permute-start | bytes 6488072 | tf_op jit(solution)/shard_map/ppermute | solution.py:58
  1031.5 44.1 %slice-start.2 = ((s8[17301504]{0:T(1024)(128)(4,1)}), s8[4194304]{0:T(1024)(128)(4,1)S(1)}, s32[]{:S(2)}) async-start(s8[17301504]{0:T(1024)(128)(4,1)} %bitcast.336), calls=%async_computation.18 | async-start | bytes 8388608
  1031.5 44.1 %slice-start.3 = ((s8[17301504]{0:T(1024)(128)(4,1)}), s8[4194304]{0:T(1024)(128)(4,1)S(1)}, s32[]{:S(2)}) async-start(s8[17301504]{0:T(1024)(128)(4,1)} %bitcast.336), calls=%async_computation.19 | async-start | bytes 8388608
  1031.5 44.1 %slice-start.4 = ((s8[17301504]{0:T(1024)(128)(4,1)}), s8[4194304]{0:T(1024)(128)(4,1)S(1)}, s32[]{:S(2)}) async-start(s8[17301504]{0:T(1024)(128)(4,1)} %bitcast.336), calls=%async_computation.20 | async-start | bytes 8388608
  1031.5 44.0 %slice-start.5 = ((s8[17301504]{0:T(1024)(128)(4,1)}), s8[4194304]{0:T(1024)(128)(4,1)S(1)}, s32[]{:S(2)}) async-start(s8[17301504]{0:T(1024)(128)(4,1)} %bitcast.336), calls=%async_computation.21 | async-start | bytes 8388608
  1044.6 53.1 %collective-permute-start.7 = (bf16[2112,256]{1,0:T(8,128)(2,1)}, bf16[2112,256]{1,0:T(8,128)(2,1)S(1)}, u32[]{:S(2)}, u32[]{:S(2)}) collective-permute-start(bf16[2112,256]{1,0:T(8,128)(2,1)} %get-tuple-element.226), channel_id=1, source_target_pairs={{0,8},{8,0},{16,24},{24,16},{1,9},{9,1},{17,25},{25,17},{2,10},{10... | collective-permute-start | bytes 3244040 | tf_op jit(solution)/shard_map/ppermute | solution.py:58
  1045.4 52.3 %collective-permute-start.5 = (bf16[2112,256]{1,0:T(8,128)(2,1)}, bf16[2112,256]{1,0:T(8,128)(2,1)}, u32[]{:S(2)}, u32[]{:S(2)}) collective-permute-start(bf16[2112,256]{1,0:T(8,128)(2,1)} %get-tuple-element.227), channel_id=1, source_target_pairs={{0,16},{8,24},{16,0},{24,8},{1,17},{9,25},{17,1},{25,9},{2,18},{10... | collective-permute-start | bytes 3244040 | tf_op jit(solution)/shard_map/ppermute | solution.py:58
  1080.7 47.4 %collective-permute-start.1 = (bf16[256,4224]{1,0:T(8,128)(2,1)}, bf16[256,4224]{1,0:T(8,128)(2,1)}, u32[]{:S(2)}, u32[]{:S(2)}) collective-permute-start(bf16[256,4224]{1,0:T(8,128)(2,1)} %get-tuple-element.218), channel_id=1, source_target_pairs={{0,16},{8,24},{16,0},{24,8},{1,17},{9,25},{17,1},{25,9},{2,18},{10... | collective-permute-start | bytes 6488072 | tf_op jit(solution)/shard_map/ppermute | solution.py:58
  1084.1 66.7 %all-to-all-start.2 = ((bf16[2,12,8,4096]{3,0,1,2:T(2,128)(2,1)}), bf16[2,12,8,4096]{3,0,1,2:T(2,128)(2,1)S(1)}, u32[]{:S(2)}, u32[]{:S(2)}) async-start(bf16[2,12,8,4096]{3,0,1,2:T(2,128)(2,1)} %copy.742), calls=%async_computation.4 | async-start | bytes 3145728 | tf_op jit(solution)/shard_map/all_to_all | solution.py:527
  1159.8 14.1 %all-to-all-start.3 = ((bf16[4,64,1536]{2,1,0:T(8,128)(2,1)}), bf16[4,64,1536]{2,1,0:T(8,128)(2,1)S(1)}, u32[]{:S(2)}, u32[]{:S(2)}) async-start(bf16[4,64,1536]{2,1,0:T(8,128)(2,1)} %reduce-scatter.9.cloned.1.call-done), calls=%async_computation.6 | async-start | bytes 1572864 | tf_op jit(solution)/shard_map/all_to_all | solution.py:532
  (87 other events, 753.9 us)
Sparse Core Ops, SparseCore 0:
  274.4 44.0 all-gather.3
  403.5 64.7 all-gather.5
  648.7 72.1 reduce-scatter.6
  741.3 42.3 all-gather.7
  786.0 69.8 reduce-scatter.4
  892.5 121.2 all-reduce.3
  1016.2 36.2 reduce-scatter.10
  1054.9 93.4 reduce-scatter.8

commit v3 on v2

--- a/solution.py
+++ b/solution.py
@@ -148,65 +148,86 @@
 
             self.side(origin, self.core).start()
 
-    def finish(self):
+    def arrive(self):
+        for origin in range(self.n):
+            self.side(origin, 1 - self.core).wait_recv()
+
+    def drain(self):
         for step in range(self.n - 1):
             self.send(step, lambda copy: copy.wait_send())
         for origin in range(self.n):
             self.side(origin, self.core).wait_send()
-            self.side(origin, 1 - self.core).wait_recv()
 
 
 PLACE = {key: i for i, key in enumerate(ORDER)}
 
 
-def prologue_kernel(
-    S, N, shapes, tok, cot, wq, wo, small, *rest,
-):
-    shards_in, rest = rest[:6], rest[6:]
-    d_tok, g_all, w_in, w_back, small_all, *rest = rest
-    fulls, rest = rest[:6], rest[6:]
-    bounce, rest = rest[:11], rest[11:]
-    local_sem, deal_send, deal_recv, seq_send, seq_recv, small_send, small_recv, half_send, half_recv, *line_sems = rest
+def gather_vector(small, row, length, own, N):
+    per = 128 // own
+    for block in range(length // 128):
+        total = None
+        for i in range(block * per, (block + 1) * per):
+            part = small[i % N, i // N, row : row + 1, :]
+            total = part if total is None else total + part
+        yield block, total
+
+
+def forward_kernel(S, N, sizes, *refs):
+    MB, piece, D, own, heads = sizes
+    tok, cot, wq, wo, small, *refs = refs
+    shards_in, refs = refs[:6], refs[6:]
+    cos, sin, first, place, place_row, *refs = refs
+    x_rows, g_all, w_in, w_back, small_all, normed_out, qkv_out, ctx_out, hid_out, x_all, *refs = refs
+    fulls, refs = refs[:6], refs[6:]
+    cot_by, shard_by, refs = refs[0], refs[1:7], refs[7:]
+    small_v, tok_v, w_v, wb_v, x_v, gain_v, bias_v, na_v, qkv_v, ctx_v, part_send, part_recv, hid_v, n2_v, xo_v, *refs = refs
+    (local_sem, deal_send, deal_recv, seq_send, seq_recv, small_send, small_recv, half_send, half_recv, part_sems,
+     part_semr, norm_sems, norm_semr, out_sem, *line_sems) = refs
     s, f = lax.axis_index("seq"), lax.axis_index("fsdp")
     px, py, pd = partners(s)
-    eighth = shapes[0]
-
-    def spot(full, i, place):
-        cut = pl.ds(place * eighth, eighth)
+    eighth = D // 8
+    pr = MB * piece
+    L = pr * N
+    R = S * L
+    width = heads * HD
+
+    def spot(full, i, where):
+        cut = pl.ds(where * eighth, eighth)
         return full.at[cut] if i < 4 else full.at[:, cut]
 
     def own_half(shard, i, half):
         cut = pl.ds(half * eighth, eighth)
         return shard.at[cut] if i < 4 else shard.at[:, cut]
 
-    places = [small_all.at[f, s], w_in.at[s, f], w_back.at[f], d_tok.at[f], g_all.at[f, f]]
+    def remote(src, dst, send, recv, device):
+        return pltpu.make_async_remote_copy(src, dst, send, recv, device_id=device, device_id_type=MESH)
+
+    pairs = [
+        (small, small_v.at[f, s]), (wq.at[s], w_v.at[s, f]), (wo, wb_v.at[f]), (tok.at[f], tok_v.at[f]), (cot.at[f], cot_by),
+    ] + list(zip(shards_in, shard_by))
+    take = [pltpu.make_async_copy(a, b, local_sem.at[i]) for i, (a, b) in enumerate(pairs)]
+    put = [pltpu.make_async_copy(cot_by, g_all.at[f, f], local_sem.at[4])]
     for i in range(6):
         cut = pl.ds(0, 2 * eighth)
-        places.append(fulls[i].at[cut] if i < 4 else fulls[i].at[:, cut])
-    sources = [small, wq.at[s], wo, tok.at[f], cot.at[f], *shards_in]
-    take = [pltpu.make_async_copy(src, by, local_sem.at[i]) for i, (src, by) in enumerate(zip(sources, bounce))]
-    put = [pltpu.make_async_copy(by, dst, local_sem.at[i]) for i, (by, dst) in enumerate(zip(bounce, places))]
+        target = fulls[i].at[cut] if i < 4 else fulls[i].at[:, cut]
+        put.append(pltpu.make_async_copy(shard_by[i], target, local_sem.at[5 + i]))
     for copy in take:
         copy.start()
     greet(s, f, S, N)
 
-    def remote(src, dst, send, recv, device):
-        return pltpu.make_async_remote_copy(src, dst, send, recv, device_id=device, device_id_type=MESH)
-
     over_seq = []
     for k, other in enumerate((px, py, pd)):
-        over_seq.append(remote(small, small_all.at[f, s], seq_send.at[0, k], seq_recv.at[0, k], (other, f)))
-        over_seq.append(remote(wq.at[other], w_in.at[s, f], seq_send.at[1, k], seq_recv.at[1, k], (other, f)))
+        over_seq.append(remote(small, small_v.at[f, s], seq_send.at[0, k], seq_recv.at[0, k], (other, f)))
+        over_seq.append(remote(wq.at[other], w_v.at[s, f], seq_send.at[1, k], seq_recv.at[1, k], (other, f)))
     for copy in over_seq:
         copy.start()
-    dealt = []
+    deal_tok, deal_cot, to_all = [], [], []
     for k in range(1, N):
         to = lax.rem(f + k, N)
-        dealt.append(remote(tok.at[to], d_tok.at[f], deal_send.at[0, k - 1], deal_recv.at[0, k - 1], (s, to)))
-    for k in range(1, N):
-        to = lax.rem(f + k, N)
-        dealt.append(remote(cot.at[to], g_all.at[to, f], deal_send.at[1, k - 1], deal_recv.at[1, k - 1], (s, to)))
-    for copy in dealt:
+        deal_tok.append(remote(tok.at[to], tok_v.at[f], deal_send.at[0, k - 1], deal_recv.at[0, k - 1], (s, to)))
+        deal_cot.append(remote(cot.at[to], g_all.at[to, f], deal_send.at[1, k - 1], deal_recv.at[1, k - 1], (s, to)))
+        to_all.append(remote(small_v.at[f], small_v.at[f], small_send.at[k - 1], small_recv.at[k - 1], (s, to)))
+    for copy in deal_tok:
         copy.start()
 
     def half_copy(i, k):
@@ -216,97 +237,218 @@
             (where, f),
         )
 
-    def pass_on(i, k):
+    def pass_copy(i, k):
         where, rel, half = ((py, 1, 0), (px, 2, 1))[k]
         return remote(
             spot(fulls[i], i, PLACE[rel, half]), spot(fulls[i], i, PLACE[3, half]), half_send.at[i, 4 + k],
             half_recv.at[i, 4 + k], (where, f),
         )
 
-    for i in range(6):
+    def give(i):
         for k in range(4):
             half_copy(i, k).start()
 
-    for copy, after in zip(take, put):
+    def pass_on(i):
+        for k in range(2):
+            half_copy(i, k).wait_recv()
+            pass_copy(i, k).start()
+
+    give(0)
+    for copy in take:
         copy.wait()
-        after.start()
+    for copy in put:
+        copy.start()
+    for copy in over_seq:
+        copy.wait_recv()
+    for copy in to_all:
+        copy.start()
+    w_line = Line(s, f, N, lambda j: w_v.at[:, j], *line_sems[0:4])
+    b_line = Line(s, f, N, lambda j: wb_v.at[j], *line_sems[4:8])
+    g_line = Line(s, f, N, lambda j: g_all.at[j], *line_sems[8:12])
+    x_line = Line(s, f, N, lambda j: x_all.at[j], *line_sems[12:16])
+    w_line.begin()
+    b_line.begin()
+
+    for copy in deal_tok + to_all:
+        copy.wait_recv()
+    for row in range(2):
+        for block, part in gather_vector(small_v, row, D, own, N):
+            gain_v[row : row + 1, block * 128 : (block + 1) * 128] = part
+    nb = 3 * own
+    for line in range(3 * D // 128):
+        total = None
+        for i in range(S * N):
+            for half in range(2):
+                if (i * nb) // 128 + half == line and (half == 0 or (i * nb) % 128 + nb > 128):
+                    part = small_v[i % N, i // N, 2 + half : 3 + half, :]
+                    total = part if total is None else total + part
+        bias_v[line : line + 1, :] = total
+    for j in range(N):
+        x_v[j * pr : (j + 1) * pr, :] = tok_v[j].astype(F32)
+    x = x_v[...]
+    inverse = lax.rsqrt(jnp.mean(x * x, axis=-1, keepdims=True) + EPS)
+    na_v[s] = (x * inverse * gain_v[0:1, :]).astype(BF16)
+    spread = [
+        remote(na_v.at[s], na_v.at[s], norm_sems.at[k], norm_semr.at[k], (other, f)) for k, other in enumerate((px, py, pd))
+    ]
+    for copy in spread:
+        copy.start()
+    for copy in deal_cot:
+        copy.start()
+    give(1)
+    chips = N // 2
+    for step in range(chips - 1):
+        w_line.step(step)
+        b_line.step(step)
+        if step == 0:
+            give(4)
+        if step == 1:
+            pass_on(0)
+    pass_on(1)
+    give(2)
+    for copy in deal_cot:
+        copy.wait_recv()
     for copy in put:
         copy.wait()
-    for copy in over_seq:
+    g_line.begin()
+    w_line.arrive()
+    b_line.arrive()
+    for copy in spread:
         copy.wait_recv()
-    to_all = []
-    for k in range(1, N):
-        to = lax.rem(f + k, N)
-        to_all.append(remote(small_all.at[f], small_all.at[f], small_send.at[k - 1], small_recv.at[k - 1], (s, to)))
-    for copy in to_all:
+
+    for t in range(3):
+
+        def project(pair, carry, t=t):
+            column = pl.multiple_of(t * width + pair * 2 * HD, 2 * HD)
+            w = w_v[:, :, :, pl.ds(column, 2 * HD)].reshape(D, 2 * HD)
+            out = dot(na_v[...].reshape(R, D), w)
+            for k in range(2):
+                u = out[:, k * HD : (k + 1) * HD]
+                u = u + bias_v[pl.ds(t * (D // 128) + s * heads + 2 * pair + k, 1), :]
+                if t < 2:
+                    u = u * cos[...] + pltpu.roll(u, HD // 2, 1) * sin[...]
+                qkv_v[t * heads + 2 * pair + k] = u.astype(BF16)
+            return carry
+
+        lax.fori_loop(0, heads // 2, project, 0)
+    g_line.step(0)
+
+    def attend(h, carry):
+        rows = R // 4
+        for block in range(4):
+            cut = pl.ds(block * rows, rows)
+            raw = dot_nt(qkv_v[h, cut, :], qkv_v[heads + h])
+            ok = (first[cut, :] <= place_row[...]) & (place_row[...] <= place[cut, :])
+            scores = jnp.where(ok, raw * HD**-0.5, MASKED)
+            weights = jnp.exp(scores - jnp.max(scores, axis=-1, keepdims=True))
+            chance = (weights / jnp.sum(weights, axis=-1, keepdims=True)).astype(BF16)
+            ctx_v[cut, pl.ds(pl.multiple_of(h * HD, HD), HD)] = dot(chance, qkv_v[2 * heads + h]).astype(BF16)
+        return carry
+
+    lax.fori_loop(0, heads, attend, 0)
+    for step in range(1, chips - 1):
+        g_line.step(step)
+        if step == 1:
+            give(3)
+            give(5)
+
+    wb = wb_v[...].reshape(width, D)
+    exchange = []
+    for k, other in enumerate((px, py, pd)):
+        rows = pl.ds(pl.multiple_of(other * L, L), L)
+        part_send[k] = dot(ctx_v[rows, :], wb).astype(BF16)
+        exchange.append(remote(part_send.at[k], part_recv.at[k], part_sems.at[k], part_semr.at[k], (other, f)))
+        exchange[-1].start()
+    pass_on(4)
+    hid_v[...] = x_v[...] + dot(ctx_v[pl.ds(pl.multiple_of(s * L, L), L), :], wb)
+    outs = [
+        (tok_v, x_rows), (w_v, w_in), (wb_v, w_back), (small_v, small_all), (na_v, normed_out), (qkv_v, qkv_out),
+        (ctx_v, ctx_out), (hid_v, hid_out), (xo_v, x_all.at[f]),
+    ]
+    outs = [pltpu.make_async_copy(a, b, out_sem.at[i]) for i, (a, b) in enumerate(outs)]
+    for k in range(3):
+        exchange[k].wait_recv()
+        hid_v[...] += part_recv[k].astype(F32)
+    hidden = hid_v[...]
+    inverse = lax.rsqrt(jnp.mean(hidden * hidden, axis=-1, keepdims=True) + EPS)
+    n2_v[...] = (hidden * inverse * gain_v[1:2, :]).astype(BF16)
+    owners = (s, px, py, pd)
+    for i, (rel, half) in enumerate(ORDER):
+        column = pl.multiple_of((owners[rel] * 2 + half) * eighth, eighth)
+        xo_v[:, i * eighth : (i + 1) * eighth] = n2_v[:, pl.ds(column, eighth)]
+    outs[8].start()
+    outs[8].wait()
+    x_line.begin()
+    pass_on(2)
+    for step in range(chips - 1):
+        x_line.step(step)
+    pass_on(3)
+    pass_on(5)
+    for line in (w_line, b_line):
+        line.drain()
+    for copy in over_seq + to_all + spread:
+        copy.wait_send()
+    for copy in outs[:8]:
         copy.start()
-    lines = [
-        Line(s, f, N, lambda j: w_in.at[:, j], *line_sems[0:4]),
-        Line(s, f, N, lambda j: w_back.at[j], *line_sems[4:8]),
-        Line(s, f, N, lambda j: g_all.at[j], *line_sems[8:12]),
-    ]
-    lines[0].begin()
-    lines[1].begin()
-    for copy in dealt:
-        copy.wait_recv()
-    for step in range(N // 2 - 1):
-        lines[0].step(step)
-        lines[1].step(step)
-    lines[2].begin()
-    for step in range(N // 2 - 1):
-        lines[2].step(step)
-    for i in range(6):
-        for k in range(2):
-            half_copy(i, k).wait_recv()
-            pass_on(i, k).start()
     for i in range(6):
         for k in range(2, 4):
             half_copy(i, k).wait_recv()
         for k in range(2):
-            pass_on(i, k).wait_recv()
+            pass_copy(i, k).wait_recv()
     for i in range(6):
         for k in range(4):
             half_copy(i, k).wait_send()
         for k in range(2):
-            pass_on(i, k).wait_send()
-    for line in lines:
-        line.finish()
-    for copy in over_seq + dealt:
+            pass_copy(i, k).wait_send()
+    for line in (g_line, x_line):
+        line.arrive()
+        line.drain()
+    for copy in deal_tok + deal_cot + exchange:
         copy.wait_send()
-    for copy in to_all:
+    for copy in outs[:8]:
         copy.wait()
 
 
-def prologue(S, N, tok, cot, wq, wo, small, shards_in):
-    D = wo.shape[1]
-    own = wo.shape[0]
+def forward(S, N, MB, tok, cot, wq, wo, small, shards_in, tables):
+    own, D = wo.shape
+    pr = tok.shape[1]
+    L = pr * N
+    R = S * L
+    heads = H // S
+    width = heads * HD
     chips = N // 2
     dma = pltpu.SemaphoreType.DMA
     line = [dma((2, chips - 1)), dma((2, chips - 1)), dma((chips,)), dma((chips,))]
+    shape = jax.ShapeDtypeStruct
+    w_shape, wb_shape, small_shape = (S, N) + wq.shape[1:], (N,) + wo.shape, (N, S) + small.shape
     out = [
-        jax.ShapeDtypeStruct(tok.shape, BF16),
-        jax.ShapeDtypeStruct((N,) + cot.shape, BF16),
-        jax.ShapeDtypeStruct((S, N) + wq.shape[1:], BF16),
-        jax.ShapeDtypeStruct((N,) + wo.shape, BF16),
-        jax.ShapeDtypeStruct((N, S) + small.shape, F32),
+        shape(tok.shape, BF16), shape((N,) + cot.shape, BF16), shape(w_shape, BF16), shape(wb_shape, BF16),
+        shape(small_shape, F32), shape((S, L, D), BF16), shape((3 * heads, R, HD), BF16), shape((R, width), BF16),
+        shape((L, D), F32), shape((N, L, D), BF16),
     ]
     for i, shard in enumerate(shards_in):
         rows, columns = shard.shape
-        out.append(jax.ShapeDtypeStruct((4 * rows, columns) if i < 4 else (rows, 4 * columns), BF16))
+        out.append(shape((4 * rows, columns) if i < 4 else (rows, 4 * columns), BF16))
     anywhere = pl.BlockSpec(memory_space=pl.ANY)
+    in_vmem = pl.BlockSpec(memory_space=pltpu.VMEM)
+    vmem = pltpu.VMEM
     return pl.pallas_call(
-        functools.partial(prologue_kernel, S, N, (D // 8,)),
+        functools.partial(forward_kernel, S, N, (MB, pr // MB, D, own, heads)),
         out_shape=out,
-        in_specs=[anywhere] * 11,
-        out_specs=[anywhere] * 11,
-        scratch_shapes=[pltpu.VMEM(u.shape, u.dtype) for u in (small, wq[0], wo, tok[0], cot[0], *shards_in)]
+        in_specs=[anywhere] * 11 + [in_vmem] * 5,
+        out_specs=[anywhere] * 16,
+        scratch_shapes=[vmem(u.shape, u.dtype) for u in (cot[0], *shards_in)]
         + [
+            vmem(small_shape, F32), vmem(tok.shape, BF16), vmem(w_shape, BF16), vmem(wb_shape, BF16), vmem((L, D), F32),
+            vmem((8, D), F32), vmem((3 * D // 128, 128), F32), vmem((S, L, D), BF16), vmem((3 * heads, R, HD), BF16),
+            vmem((R, width), BF16), vmem((3, L, D), BF16), vmem((3, L, D), BF16), vmem((L, D), F32), vmem((L, D), BF16),
+            vmem((L, D), BF16),
             dma((11,)), dma((2, N - 1)), dma((2, N - 1)), dma((2, 3)), dma((2, 3)), dma((N - 1,)), dma((N - 1,)),
-            dma((6, 6)), dma((6, 6)),
-        ] + line * 3,
+            dma((6, 6)), dma((6, 6)), dma((3,)), dma((3,)), dma((3,)), dma((3,)), dma((9,)),
+        ] + line * 4,
         compiler_params=pltpu.CompilerParams(collective_id=0, has_side_effects=True, vmem_limit_bytes=VMEM_LIMIT),
-        name="prologue",
-    )(tok, cot, wq, wo, small, *shards_in)
+        name="forward",
+    )(tok, cot, wq, wo, small, *shards_in, *tables)
 
 
 def shards(
@@ -339,79 +481,65 @@
         u = jnp.stack([jnp.take(u[m], inverse_deal[m, f], axis=1) for m in range(MB)])
         return u.transpose(2, 0, 1, 3).reshape(N, MB * piece, D)
 
-    small = jnp.concatenate([gain_attn, gain_ffn, w_router.reshape(-1), w_shared_gate, b_qkv]).astype(F32)
-    small = jnp.concatenate([small, ids.reshape(-1).astype(F32)])
-    n_small = small.shape[0]
-    small = jnp.pad(small, (0, -n_small % 1024)).reshape(-1, 128)
+    index = s * N + f
+
+    def placed(u, length):
+        return lax.dynamic_update_slice(jnp.zeros((length,), F32), u.astype(F32), ((index * u.shape[0]) % 128,))
+
+    parts = [placed(gain_attn, 128), placed(gain_ffn, 128), placed(b_qkv, 256), placed(w_shared_gate, 128)]
+    for u in (w_router.reshape(-1), ids.reshape(-1)):
+        parts.append(jnp.pad(u.astype(F32), (0, -u.shape[0] % 128)))
+    r_line = 5
+    i_line = r_line + parts[4].shape[0] // 128
+    small = jnp.concatenate(parts)
+    small = jnp.pad(small, (0, -small.shape[0] % 1024)).reshape(-1, 128)
+
+    spots = ((jnp.arange(S)[:, None, None] * piece + jnp.arange(piece)[None, None, :]) * N + jnp.arange(N)[None, :, None])
+    spots = jnp.broadcast_to(spots[:, :, None, :], (S, N, MB, piece)).astype(jnp.int32)
+    micro = jnp.arange(MB, dtype=jnp.int32)[None, None, :, None]
+    my_lengths = lengths[:, f]
+    ends = jnp.cumsum(my_lengths, axis=1)
+    past = ends[None, None, :, None, :] <= spots[..., None]
+    start = jnp.sum(jnp.where(past, my_lengths[None, None, :, None, :], 0), axis=4)
+    frequency = THETA ** (-jnp.arange(0, HD, 2, dtype=F32) / HD)
+    angle = (spots - start).astype(F32).reshape(-1, 1) * frequency
+    cosine, sine = jnp.cos(angle), jnp.sin(angle)
+    cosine = jnp.concatenate([cosine, cosine], axis=1)
+    sine = jnp.concatenate([-sine, sine], axis=1)
+    place = (spots + pack * micro).reshape(-1)
+    first = (start + pack * micro).reshape(-1)
+    tables = (cosine, sine, first[:, None], place[:, None], place[None, :])
+
     wq = w_qkv.reshape(own, 3, S, width).transpose(2, 0, 1, 3).reshape(S, own, 3 * width)
-    d_tok, g_all, w_in, w_back, small, *fulls = prologue(
-        S, N, deal_out(tokens), deal_out(arrange(cotangent, order)), wq, w_out, small,
-        (e_gate[0], e_up[0], s_gate, s_up, e_down[0], s_down),
+    x_rows, g_all, w_in, w_back, small, normed_all, qkv, context, hidden, x_all, *fulls = forward(
+        S, N, MB, deal_out(tokens), deal_out(arrange(cotangent, order)), wq, w_out, small,
+        (e_gate[0], e_up[0], s_gate, s_up, e_down[0], s_down), tables,
     )
-    small = small.reshape(N, S, -1)[:, :, :n_small]
-    cuts = (own, 2 * own, 2 * own + own * E, 3 * own + own * E, 6 * own + own * E)
-    small, all_ids = small[:, :, : cuts[4]].swapaxes(0, 1).reshape(S * N, cuts[4]), small[:, :, cuts[4] :]
-    gain_1 = small[:, : cuts[0]].reshape(D)
-    gain_2 = small[:, cuts[0] : cuts[1]].reshape(D)
-    router_w = small[:, cuts[1] : cuts[2]].reshape(D, E).astype(BF16)
-    shared_w = small[:, cuts[2] : cuts[3]].reshape(D).astype(BF16)
-    bias = lax.dynamic_slice_in_dim(small[:, cuts[3] :].reshape(3, S, width), s, 1, 1).reshape(3 * width)
+    L, R = MB * T, MB * pack
+
+    def vector(row):
+        return small[:, :, row].swapaxes(0, 1).reshape(D // 128, 128 // own, 128).sum(1).reshape(D)
+
+    gain_1, gain_2, shared_w = vector(0), vector(1), vector(4).astype(BF16)
+    router_w = small[:, :, r_line:i_line].swapaxes(0, 1).reshape(S * N, -1)[:, : own * E].reshape(D, E).astype(BF16)
+    all_ids = small[:, :, i_line:].reshape(N, S, -1)[:, :, : MB * T * TOP]
     w_in, w_back = w_in.reshape(D, 3 * width), w_back.reshape(width, D)
     eg, eu, sg, su, ed, sd = fulls
-    x0 = d_tok.reshape(N, MB, piece, D).transpose(1, 2, 0, 3).reshape(MB, T, D).astype(F32)
-    d_cot = lax.dynamic_index_in_dim(g_all, f, 0, keepdims=False)
-    cot = arrange(d_cot.reshape(N, MB, piece, D).transpose(1, 2, 0, 3).reshape(MB, T, D), inverse_order)
+    x0 = x_rows.reshape(L, D).astype(F32)
+    cot = arrange(lax.dynamic_index_in_dim(g_all, f, 0, keepdims=False).reshape(L, D), inverse_order)
     g_rows = g_all.reshape(rows, D)
     all_ids = lax.dynamic_index_in_dim(all_ids, s, 1, keepdims=False).reshape(N, MB, piece, N, TOP)
     where = inverse_deal.transpose(2, 1, 0)
     chosen = jnp.take_along_axis(
         all_ids[None], where[:, :, :, None, None, None], axis=4
-    ).reshape(N, MB * T, TOP).astype(jnp.int32)
+    ).reshape(N, L, TOP).astype(jnp.int32)
     own_ids = lax.dynamic_index_in_dim(chosen, f, 0, keepdims=False)
-    own_ids = own_ids.reshape(N, MB, piece, TOP).transpose(1, 2, 0, 3).reshape(MB * T, TOP)
     chosen = chosen.reshape(rows, TOP)
-
-    def to_rows(u):
-        return u.reshape(MB, piece, N, -1).transpose(2, 0, 1, 3).reshape(MB * T, -1)
-
-    def to_pack(u):
-        return u.reshape(N, MB, piece, -1).transpose(1, 2, 0, 3).reshape(MB * T, -1)
-
-    ends = jnp.cumsum(lengths[:, f], axis=1)
-    spots = jnp.arange(pack, dtype=jnp.int32)
-    past = ends[:, None, :] <= spots[None, :, None]
-    segment = jnp.sum(past.astype(jnp.int32), axis=2)
-    start = jnp.sum(jnp.where(past, lengths[:, f][:, None, :], 0), axis=2)
-    frequency = THETA ** (-jnp.arange(0, HD, 2, dtype=F32) / HD)
-    angle = (spots[None] - start).astype(F32)[..., None] * frequency
-    angle = jnp.concatenate([angle, angle], axis=2)
-    cosine, sine = jnp.cos(angle)[:, None, None], jnp.sin(angle)[:, None, None]
-    allowed = (segment[:, :, None] == segment[:, None, :]) & (spots[None, None, :] <= spots[None, :, None])
-    allowed = allowed[:, None]
-
+    x = x_all.reshape(rows, D)
+    x_own = lax.dynamic_index_in_dim(x_all, f, 0, keepdims=False)
     unit_1, inverse_1 = rms_forward(x0)
-    normed = (unit_1 * gain_1).astype(BF16)
-    normed_all = lax.all_gather(normed, "seq", axis=1, tiled=True)
-    flat = normed_all.reshape(MB * pack, D)
-    qkv = (dot(flat, w_in) + bias).reshape(MB, pack, 3, heads, HD).transpose(0, 2, 3, 1, 4)
-    qk = qkv[:, :2]
-    qk = (qk * cosine + turn(qk) * sine).astype(BF16)
-    q, k, v = qk[:, 0], qk[:, 1], qkv[:, 2].astype(BF16)
-    scale = HD ** -0.5
-    raw = jnp.einsum("mhqd,mhkd->mhqk", q, k, preferred_element_type=F32)
-    scores = jnp.where(allowed, raw * scale, MASKED)
-    weights = jnp.exp(scores - jnp.max(scores, axis=-1, keepdims=True))
-    chance = weights / jnp.sum(weights, axis=-1, keepdims=True)
-    chance_low = chance.astype(BF16)
-    context = jnp.einsum("mhqk,mhkd->mqhd", chance_low, v, preferred_element_type=F32).astype(BF16)
-    context = context.reshape(MB * pack, width)
-    partial = dot(context, w_back).astype(BF16).reshape(MB, S, T, D)
-    partial = lax.all_to_all(partial, "seq", split_axis=1, concat_axis=1, tiled=True)
-    hidden = x0 + jnp.sum(partial.astype(F32), axis=1)
     unit_2, inverse_2 = rms_forward(hidden)
-    normed2 = (unit_2 * gain_2).astype(BF16)
-
-    x = lax.all_gather(to_rows(arrange(normed2, order)), "fsdp", axis=0, tiled=True)
+
     lead = jnp.concatenate([router_w, shared_w[:, None]], axis=1)
     lead_order = jnp.take(lead.reshape(8, D // 8, E + 1), order, axis=0).reshape(D, E + 1)
     logits = dot(x, lead_order)
@@ -480,15 +608,13 @@
     )
     g_eg, g_eu, g_sg, g_su = jnp.split(grad_a, (FE, 2 * FE, 2 * FE + FS), axis=1)
 
-    y = arrange(to_pack(y).astype(F32).reshape(MB, T, D), inverse_order)
-    dx = to_pack(dx)
-    mixed = (hidden + y).astype(BF16)
+    mixed = (hidden + arrange(y, inverse_order).astype(F32)).astype(BF16)
     base = D
     gg_own = sum(dx[:, base + i * N : base + (i + 1) * N] for i in range(3))
     gs_own = jnp.sum(dx[:, base + 3 * N : base + 6 * N], axis=1)
     grad_normed2 = arrange(dx[:, :D], inverse_order)
-    flat2 = normed2.reshape(MB * T, D)
-    logits = dot(flat2, lead)
+    flat2 = arrange(x_own, inverse_order)
+    logits = dot(x_own, lead_order)
     shifted = jnp.exp(logits[:, :E] - jnp.max(logits[:, :E], axis=-1, keepdims=True))
     router = shifted / jnp.sum(shifted, axis=-1, keepdims=True)
     sigma = jax.nn.sigmoid(logits[:, E])
@@ -499,33 +625,51 @@
     grad_normed2 = grad_normed2 + dot_nt(grad_logits, router_w) + grad_sigma[:, None] * shared_w.astype(F32)[None, :]
     g_router = dot_t(flat2, grad_logits)
     g_shared = jnp.sum(grad_sigma[:, None] * flat2.astype(F32), axis=0)
-    from_norm, g_gain_2 = rms_backward(grad_normed2.reshape(MB, T, D), unit_2, inverse_2, gain_2)
+    from_norm, g_gain_2 = rms_backward(grad_normed2, unit_2, inverse_2, gain_2)
     grad_hidden = cot.astype(F32) + from_norm
 
-    grad_attn = lax.all_gather(grad_hidden.astype(BF16), "seq", axis=1, tiled=True).reshape(MB * pack, D)
+    grad_attn = lax.all_gather(grad_hidden.astype(BF16), "seq", axis=0, tiled=True)
     g_out = dot_t(context, grad_attn)
-    gc = dot_nt(grad_attn, w_back).astype(BF16).reshape(MB, pack, heads, HD).transpose(0, 2, 1, 3)
+    gc = dot_nt(grad_attn, w_back).astype(BF16)
+
+    def by_micro(u):
+        u = u.reshape(u.shape[0], S * N, MB, piece, HD).transpose(2, 0, 1, 3, 4)
+        return u.reshape(MB, u.shape[1], pack, HD)
+
+    qkv = by_micro(qkv)
+    q, k, v = qkv[:, :heads], qkv[:, heads : 2 * heads], qkv[:, 2 * heads :]
+    gc = by_micro(gc.reshape(R, heads, HD).swapaxes(0, 1))
+    at = spots[:, :, 0].reshape(-1)
+    low = start.transpose(2, 0, 1, 3).reshape(MB, pack)
+    allowed = (low[:, :, None] <= at[None, None, :]) & (at[None, None, :] <= at[None, :, None])
+    scale = HD ** -0.5
+    raw = jnp.einsum("mhqd,mhkd->mhqk", q, k, preferred_element_type=F32)
+    scores = jnp.where(allowed[:, None], raw * scale, MASKED)
+    weights = jnp.exp(scores - jnp.max(scores, axis=-1, keepdims=True))
+    chance = weights / jnp.sum(weights, axis=-1, keepdims=True)
+    chance_low = chance.astype(BF16)
     grad_chance = jnp.einsum("mhqd,mhkd->mhqk", gc, v, preferred_element_type=F32)
     delta = jnp.sum(chance * grad_chance, axis=-1, keepdims=True)
     grad_raw = (chance * (grad_chance - delta) * scale).astype(BF16)
     gq = jnp.einsum("mhqk,mhkd->mhqd", grad_raw, k, preferred_element_type=F32)
     gk = jnp.einsum("mhqk,mhqd->mhkd", grad_raw, q, preferred_element_type=F32)
     gv = jnp.einsum("mhqk,mhqd->mhkd", chance_low, gc, preferred_element_type=F32)
-    gqk = jnp.stack([gq, gk], axis=1).astype(BF16).astype(F32)
-    gqk = (gqk * cosine + turn_back(gqk * sine)).astype(BF16)
-    grad_qkv = jnp.concatenate([gqk, gv.astype(BF16)[:, None]], axis=1).transpose(0, 3, 1, 2, 4)
-    grad_qkv = grad_qkv.reshape(MB * pack, 3 * width)
+    moved = jnp.stack([gq, gk, gv], axis=0).astype(BF16)
+    moved = moved.reshape(3, MB, heads, S * N, piece, HD).transpose(3, 1, 4, 0, 2, 5).reshape(R, 3, heads, HD)
+    gqk = moved[:, :2].astype(F32)
+    gqk = (gqk * cosine[:, None, None] + jnp.roll(gqk * sine[:, None, None], HD // 2, axis=-1)).astype(BF16)
+    grad_qkv = jnp.concatenate([gqk, moved[:, 2:]], axis=1).reshape(R, 3 * width)
     g_bias = jnp.sum(grad_qkv.astype(F32), axis=0)
-    g_in = dot_t(flat, grad_qkv)
-    partial = dot_nt(grad_qkv, w_in).astype(BF16).reshape(MB, S, T, D)
-    partial = lax.all_to_all(partial, "seq", split_axis=1, concat_axis=1, tiled=True)
-    grad_normed = jnp.sum(partial.astype(F32), axis=1)
+    g_in = dot_t(normed_all.reshape(R, D), grad_qkv)
+    partial = dot_nt(grad_qkv, w_in).astype(BF16).reshape(S, L, D)
+    partial = lax.all_to_all(partial, "seq", split_axis=0, concat_axis=0, tiled=True)
+    grad_normed = jnp.sum(partial.astype(F32), axis=0)
     from_first, g_gain_1 = rms_backward(grad_normed, unit_1, inverse_1, gain_1)
     grad_x = (grad_hidden + from_first).astype(BF16)
 
-    back = jnp.concatenate([mixed, grad_x], axis=2).reshape(MB, piece, N, 2 * D)
-    back = lax.all_to_all(back, "fsdp", split_axis=2, concat_axis=2, tiled=True)
-    back = jnp.stack([jnp.take(back[m], deal[m, f], axis=1) for m in range(MB)]).reshape(MB, T, 2 * D)
+    back = jnp.concatenate([mixed, grad_x], axis=1).reshape(N, MB * piece, 2 * D)
+    back = lax.all_to_all(back, "fsdp", split_axis=0, concat_axis=0, tiled=True).reshape(N, MB, piece, 2 * D)
+    back = jnp.stack([jnp.take(back[:, m], deal[m, f], axis=0).swapaxes(0, 1) for m in range(MB)]).reshape(MB, T, 2 * D)
     mixed, grad_tokens = back[..., :D], back[..., D:].astype(F32)
 
     g_in = lax.psum_scatter(g_in.astype(BF16).reshape(S, N * own, 3 * width), "fsdp", scatter_dimension=1, tiled=True)
@@ -542,6 +686,7 @@
         axis=1,
     )
     small = lax.psum_scatter(small, ("seq", "fsdp"), scatter_dimension=0, tiled=True)[0]
+    cuts = (own, 2 * own, 2 * own + own * E, 3 * own + own * E)
     return (
         mixed, grad_tokens, g_in, small[cuts[3] :], g_out, small[: cuts[0]], small[cuts[0] : cuts[1]],
         small[cuts[1] : cuts[2]].reshape(own, E), small[cuts[2] : cuts[3]],

time: 1200 us -> 1090 us (0.908)
  waiting for transfers between devices: 352 us -> 202 us
  Pallas kernels: 233 us -> 331 us
  local copies, waits for them, and re-layouts: 146 us -> 115 us
  matrix products: 318 us -> 306 us
    all_gather x3 -> x1, waiting for transfers between devices: 128 us -> 22.5 us  [shards(): lax.all_gather(grad_hidden.astype(BF16), 'seq', axis=0, tiled=True)]
    pallas_call x1, Pallas kernels: 233 us -> 331 us  [forward(): pl.pallas_call(functools.partial(forward_kernel, S, N, (MB, pr // MB, D,...]
    reduce_scatter x1, waiting for transfers between devices: 0.02 us -> 65.3 us  [shards(): lax.psum_scatter(g_in.astype(BF16).reshape(S, N * own, 3 * width), 'fsdp'...]
    ppermute x8, waiting for transfers between devices: 119 us -> 55.9 us  [across(): return lax.ppermute(a, 'seq', [(i, i ^ which) for i in range(4)])]
    reduce_scatter x1, waiting for transfers between devices: 59.2 us -> 26.5 us  [shards(): lax.psum_scatter(payload, 'fsdp', scatter_dimension=0, tiled=True)]
    reshape x13 -> x6, local copies, waits for them, and re-layouts: 26.8 us -> 8.98 us  [the longest x1 3.53 us: by_micro(): u = u.reshape(u.shape[0], S * N, MB, piece, HD).transpose(2, 0, 1, 3, 4)]
    all_to_all x3 -> x2, waiting for transfers between devices: 37.3 us -> 20.1 us  [the longest x1 20.1 us: shards(): lax.all_to_all(partial, 'seq', split_axis=0, concat_axis=0, tiled=True)]
    dot_general x10 -> x8, matrix products: 97.2 us -> 86.7 us  [dot(): return jnp.dot(a, b, preferred_element_type=F32)]
  transfers between devices with their start and end apart: 20 -> 17, of which waited for: 11 -> 9; matrix products, arithmetic and copies ran while one was open for 23% -> 32% of each run, Pallas kernels for 0% -> 0%
where the time goes in v3:
time: 1090 us; the launch traced here: 1080 us
  Pallas kernels  331 us (30%)
  matrix products  306 us (28%)
  waiting for transfers between devices  202 us (19%)
  local copies, waits for them, and re-layouts  115 us (11%)
  other arithmetic  85.6 us (8%)
  starting transfers between devices  25 us (2%)
  between operations  16.5 us (2%)
    pallas_call x1, Pallas kernels, forward(): pl.pallas_call(functools.partial(forward_kernel, S, N, (MB, pr // MB, D,...  331 us
    dot_general x12, matrix products, dot_t(): lax.dot_general(a, b, (((0,), (0,)), ((), ())), preferred_element_type=F32)  102 us
    dot_general x9, matrix products, dot_nt(): lax.dot_general(a, b, (((1,), (1,)), ((), ())), preferred_element_type=F32)  96.9 us
    dot_general x8, matrix products, dot(): return jnp.dot(a, b, preferred_element_type=F32)  86.7 us
    reduce_scatter x1, waiting for transfers between devices, shards(): lax.psum_scatter(g_in.astype(BF16).reshape(S, N * own, 3 * width), 'fsdp'...  65.3 us
    ppermute x8, waiting for transfers between devices, across(): return lax.ppermute(a, 'seq', [(i, i ^ which) for i in range(4)])  55.9 us
    reduce_scatter x1, waiting for transfers between devices, shards(): lax.psum_scatter(payload, 'fsdp', scatter_dimension=0, tiled=True)  26.5 us
    all_gather x1, waiting for transfers between devices, shards(): lax.all_gather(grad_hidden.astype(BF16), 'seq', axis=0, tiled=True)  22.5 us
  transfers between devices with their start and end apart: 17, of which 9 were waited for; matrix products, arithmetic and copies ran while one was open for 32% of the time, Pallas kernels for 0%

profile of v3, /device:TPU:0, one launch (start us, length us, event | category | flops | bytes accessed | tf_op | source)
XLA Modules:
  0.0 1081.6 jit_solution(528346621580036257)
XLA Ops:
  34.2 331.3 %forward.1 = (bf16[8,24,2048]{2,1,0:T(8,128)(2,1)}, bf16[8,8,24,2048]{3,2,1,0:T(8,128)(2,1)}, bf16[4,8,64,1536]{3,2,1,0:T(8,128)(2,1)}, bf16[8,64,2048]{2,1,0:T(...) custom-call(bf16[8,24,2048]{2,1,0:T(8,128)(2,1)} %copy.468.refs_0_, ...), custom_call_target="tpu_custom_call" | custom-call | tf_op jit(solution)/shard_map/forward/pallas_call | solution.py:435
  375.6 14.8 %fusion.138 = f32[1536,1408]{0,1:T(8,128)} fusion(bf16[1536,2048]{1,0:T(8,128)(2,1)S(1)} %bitcast.295, bf16[2048,1408]{1,0:T(8,128)(2,1)} %get-tuple-element.40), kind=kOutput, calls=%fused_computation.337 | convolution fusion | flops 8858370048 | bytes 20709376 | tf_op jit(solution)/shard_map/dot_general | solution.py:25
  393.4 7.7 fusion.4
  401.0 15.5 %fusion.140 = f32[1536,1408]{0,1:T(8,128)} fusion(bf16[1536,2048]{1,0:T(8,128)(2,1)S(1)} %get-tuple-element.211, bf16[1408,2048]{1,0:T(8,128)(2,1)} %get-tuple-element.42), kind=kOutput, calls=%fused_computation.339 | convolution fusion | flops 8858370048 | bytes 20709376 | tf_op jit(solution)/shard_map/dot_general | solution.py:33
  416.5 20.6 %multiply_convert_fusion.2 = (bf16[1536,1408]{0,1:T(8,128)(2,1)}, bf16[1536,1408]{0,1:T(8,128)(2,1)}, bf16[1536,1408]{0,1:T(8,128)(2,1)}) fusion(f32[1536,1408]{0,1:T(8,128)} %fusion.138, f32[1536,1408]{0,1:T(8,128)} %fusion.140, bf16[1536,2048]{1,0:T(8,128)(2,1)S(1)} %bitcast.298, bf16[2048,1408]{1,0:T(8,128)(2,1)} %get-tuple-element.41), kind=kOutput, calls=%fused_computation.43 | convolution fusion | flops 8892973056 | bytes 42336256 | tf_op jit(solution)/shard_map/dot_general | solution.py:25
  437.2 15.3 %convolution_convert_fusion.1 = bf16[1536,2048]{1,0:T(8,128)(2,1)} fusion(bf16[1536,1408]{0,1:T(8,128)(2,1)} %get-tuple-element.197, bf16[1408,2048]{1,0:T(8,128)(2,1)} %get-tuple-element.42), kind=kOutput, calls=%fused_computation.46 | convolution fusion | flops 8861515776 | bytes 16384000 | tf_op jit(solution)/shard_map/dot_general | solution.py:25
  452.5 6.6 fusion.139
  459.1 8.6 fusion.142
  467.6 11.2 %multiply_convert_fusion.6 = (bf16[1536,704]{0,1:T(8,128)(2,1)}, bf16[1536,704]{0,1:T(8,128)(2,1)}, bf16[1536,704]{0,1:T(8,128)(2,1)}) fusion(f32[1536,704]{0,1:T(8,128)} %fusion.139, f32[1536,704]{0,1:T(8,128)} %fusion.142, bf16[1536,2048]{1,0:T(8,128)(2,1)S(1)} %bitcast.300, bf16[2048,704]{1,0:T(8,128)(2,1)S(1)} %copy-done.56), kind=kOutput, calls=%fused_computation.68 | convolution fusion | flops 4446486528 | bytes 24313856 | tf_op jit(solution)/shard_map/dot_general | solution.py:25
  478.8 13.4 %fusion.7 = (f32[1536]{0:T(1024)S(1)}, f32[1536]{0:T(1024)S(1)}, bf16[1536,2048]{1,0:T(8,128)(2,1)}) fusion(bf16[8,8,24,2048]{3,2,1,0:T(8,128)(2,1)S(1)} %bitcast.302, bf16[1536,2048]{1,0:T(8,128)(2,1)} %convolution_convert_fusion.1, f32[1536]{0:T(1024)S(1)} %divide_reduce_fusion, f32[1536]{0:T(1024)S(1)} %divide_select_fusion, ...), kind=kOutput, calls=%fused_computation.29 | convolution fusion | flops 4460639232 | bytes 23945216 | tf_op jit(solution)/shard_map/dot_general | solution.py:25
  493.8 10.6 fusion.143
  504.3 16.3 %fusion.141 = f32[1536,2048]{1,0:T(8,128)} fusion(bf16[1536,1408]{0,1:T(8,128)(2,1)} %get-tuple-element.198, bf16[2048,1408]{1,0:T(8,128)(2,1)} %get-tuple-element.40), kind=kOutput, calls=%fused_computation.340 | convolution fusion | flops 8858370048 | bytes 22675456 | tf_op jit(solution)/shard_map/dot_general | solution.py:33
  520.6 15.3 %add_convert_fusion.1 = bf16[1536,2048]{1,0:T(8,128)(2,1)} fusion(f32[1536,2048]{1,0:T(8,128)} %fusion.141, bf16[1536,1408]{0,1:T(8,128)(2,1)} %get-tuple-element.199, bf16[2048,1408]{1,0:T(8,128)(2,1)S(1)} %bitcast.365), kind=kOutput, calls=%fused_computation.31 | convolution fusion | flops 8864661504 | bytes 28966912 | tf_op jit(solution)/shard_map/dot_general | solution.py:33
  535.9 14.6 %add_convert_fusion = bf16[1536,2048]{1,0:T(8,128)(2,1)} fusion(f32[1536,2048]{1,0:T(8,128)} %fusion.143, bf16[1536,2048]{1,0:T(8,128)(2,1)} %add_convert_fusion.1, bf16[1536,704]{0,1:T(8,128)(2,1)} %get-tuple-element.210, bf16[2048,704]{1,0:T(8,128)(2,1)} %get-tuple-element.44), kind=kOutput, calls=%fused_computation.30 | convolution fusion | flops 4441767936 | bytes 30212096 | tf_op jit(solution)/shard_map/dot_general | solution.py:33
  550.5 11.8 %concatenate.78 = bf16[1536,2176]{1,0:T(8,128)(2,1)} concatenate(bf16[1536,2048]{1,0:T(8,128)(2,1)} %add_convert_fusion, bf16[1536,8]{1,0:T(8,128)(2,1)S(1)} %copy.488, bf16[1536,8]{1,0:T(8,128)(2,1)S(1)} %copy.489, bf16[1536,8]{1,0:T(8,128)(2,1)S(1)} %copy.490, bf16[1536,8]{1,0:T(8,128)(2,1)S(1)} %copy.491, bf16[1536,8]{1,0:T(8,128)(2,1)S(1)} %copy.492, ...), dimensions={1} | concatenate | bytes 13369344 | tf_op jit(solution)/shard_map/concatenate | solution.py:572
  563.9 17.0 %convolution_convert_fusion.2 = bf16[512,4224]{1,0:T(8,128)(2,1)} fusion(bf16[1536,2048]{1,0:T(8,128)(2,1)} %bitcast.292, bf16[1536,704]{0,1:T(8,128)(2,1)} %get-tuple-element.210, bf16[1536,704]{0,1:T(8,128)(2,1)S(1)} %copy-done.65, bf16[1536,1408]{0,1:T(8,128)(2,1)} %get-tuple-element.199, bf16[1536,1408]{0,1:T(8,128)(2,1)} %get-tuple-element.198), kind=kOutput, calls=%fused_computation.47 | convolution fusion | flops 6697844736 | bytes 18874368 | tf_op jit(solution)/shard_map/dot_general | solution.py:29
  608.0 26.5 %reduce-scatter.7.cloned.1.call-done = bf16[192,2176]{1,0:T(8,128)(2,1)} async-done(((bf16[1536,2176]{1,0:T(8,128)(2,1)}), bf16[192,2176]{1,0:T(8,128)(2,1)}) %reduce-scatter.7.cloned.1.call-update) | async-done | bytes 835600 | tf_op jit(solution)/shard_map/reduce_scatter | solution.py:573
  649.5 17.0 %convolution_convert_fusion.3 = bf16[512,4224]{1,0:T(8,128)(2,1)} fusion(bf16[1536,2048]{1,0:T(8,128)(2,1)} %bitcast.293, bf16[1536,704]{0,1:T(8,128)(2,1)} %get-tuple-element.210, bf16[1536,704]{0,1:T(8,128)(2,1)} %get-tuple-element.209, bf16[1536,1408]{0,1:T(8,128)(2,1)} %get-tuple-element.199, bf16[1536,1408]{0,1:T(8,128)(2,1)} %get-tuple-element.198), kind=kOutput, calls=%fused_computation.48 | convolution fusion | flops 6697844736 | bytes 18874368 | tf_op jit(solution)/shard_map/dot_general | solution.py:29
  694.8 22.5 %all-gather.2.cloned.1.call-done = bf16[768,2048]{1,0:T(8,128)(2,1)} async-done(((bf16[192,2048]{1,0:T(8,128)(2,1)}), bf16[768,2048]{1,0:T(8,128)(2,1)}) %all-gather.2.cloned.1.call-update) | async-done | bytes 3145744 | tf_op jit(solution)/shard_map/all_gather | solution.py:631
  728.9 8.1 fusion.75
  737.0 8.4 fusion.72
  760.3 9.1 convolution_convert_fusion.4
  791.6 20.1 %all-to-all-done = bf16[4,192,2048]{2,1,0:T(8,128)(2,1)} async-done(((bf16[4,192,2048]{2,1,0:T(8,128)(2,1)}), bf16[4,192,2048]{2,1,0:T(8,128)(2,1)}, u32[]{:S(2)}, u32[]{:S(2)}) %all-to-all-start) | async-done | bytes 3145760 | tf_op jit(solution)/shard_map/all_to_all | solution.py:665
  821.2 22.4 %fusion.22 = f32[1024,4224]{1,0:T(8,128)} fusion(bf16[1536,2048]{1,0:T(8,128)(2,1)} %bitcast.294, bf16[1536,704]{0,1:T(8,128)(2,1)} %get-tuple-element.210, bf16[1536,704]{0,1:T(8,128)(2,1)} %get-tuple-element.209, bf16[1536,1408]{0,1:T(8,128)(2,1)} %get-tuple-element.199, bf16[1536,1408]{0,1:T(8,128)(2,1)} %get-tuple-element.198), kind=kOutput, calls=%fused_computation.80 | convolution fusion | flops 13339459584 | bytes 33423360 | tf_op jit(solution)/shard_map/dot_general | solution.py:29
  843.5 9.1 convolution_convert_fusion
  859.1 5.9 fusion.18
  865.1 7.8 fusion.20
  880.4 27.8 %collective-permute-done.3 = bf16[256,4224]{1,0:T(8,128)(2,1)} collective-permute-done((bf16[256,4224]{1,0:T(8,128)(2,1)}, bf16[256,4224]{1,0:T(8,128)(2,1)}, u32[]{:S(2)}, u32[]{:S(2)}) %collective-permute-start.3) | collective-permute-done | bytes 2162720 | tf_op jit(solution)/shard_map/ppermute | solution.py:58
  936.2 22.6 %collective-permute-done.1 = bf16[256,4224]{1,0:T(8,128)(2,1)} collective-permute-done((bf16[256,4224]{1,0:T(8,128)(2,1)}, bf16[256,4224]{1,0:T(8,128)(2,1)}, u32[]{:S(2)}, u32[]{:S(2)}) %collective-permute-start.1) | collective-permute-done | bytes 2162720 | tf_op jit(solution)/shard_map/ppermute | solution.py:58
  968.2 5.6 fusion.29
  989.7 65.3 %reduce-scatter.9.cloned.1.call-done = bf16[4,64,1536]{2,1,0:T(8,128)(2,1)} async-done(((bf16[4,512,1536]{2,1,0:T(8,128)(2,1)}), bf16[4,64,1536]{2,1,0:T(8,128)(2,1)}) %reduce-scatter.9.cloned.1.call-update) | async-done | bytes 786448 | tf_op jit(solution)/shard_map/reduce_scatter | solution.py:675
  1061.3 6.1 all-to-all-done.2
  (470 shorter events, 250.6 us)
Async XLA Ops:
  7.2 592.1 %reduce-scatter.5.cloned.1.call-start = ((), (), s32[]{:S(2)}) async-start(), calls=%async_computation.7 | async-start | bytes 7077888 | tf_op jit(solution)/shard_map/reduce_scatter | solution.py:561
  393.3 23.2 %slice-start.7 = ((s8[6291456]{0:T(1024)(128)(4,1)}), s8[4194304]{0:T(1024)(128)(4,1)S(1)}, s32[]{:S(2)}) async-start(s8[6291456]{0:T(1024)(128)(4,1)} %bitcast.296), calls=%async_computation.20 | async-start | bytes 8388608
  437.2 21.9 %slice-start.11 = ((s8[6291456]{0:T(1024)(128)(4,1)}), s8[4194304]{0:T(1024)(128)(4,1)S(1)}, s32[]{:S(2)}) async-start(s8[6291456]{0:T(1024)(128)(4,1)} %bitcast.311), calls=%async_computation.24 | async-start | bytes 8388608
  459.0 19.8 %slice-start.9 = ((s8[6291456]{0:T(1024)(128)(4,1)}), s8[4194304]{0:T(1024)(128)(4,1)S(1)}, s32[]{:S(2)}) async-start(s8[6291456]{0:T(1024)(128)(4,1)} %bitcast.301), calls=%async_computation.22 | async-start | bytes 8388608
  492.2 142.4 %reduce-scatter.7.cloned.1.call-start = ((), (), s32[]{:S(2)}) async-start(), calls=%async_computation.8 | async-start | bytes 7520256 | tf_op jit(solution)/shard_map/reduce_scatter | solution.py:573
  493.7 26.9 %slice-start.13 = ((s8[5767168]{0:T(1024)(128)(4,1)}), s8[4194304]{0:T(1024)(128)(4,1)S(1)}, s32[]{:S(2)}) async-start(s8[5767168]{0:T(1024)(128)(4,1)} %bitcast.364), calls=%async_computation.26 | async-start | bytes 8388608
  562.3 20.1 %copy-start.30 = (bf16[4,8,4,128]{3,2,1,0:T(4,128)(2,1)S(1)}, bf16[4,8,4,128]{3,2,1,0:T(4,128)(2,1)}, u32[]{:S(2)}) copy-start(bf16[4,8,4,128]{3,2,1,0:T(4,128)(2,1)} %copy-done.29) | copy-start | bytes 98308
  562.3 21.5 %copy-start.8 = (f32[128,12,4]{1,2,0:T(4,128)S(1)}, f32[128,12,4]{1,2,0:T(4,128)}, u32[]{:S(2)}) copy-start(f32[128,12,4]{1,2,0:T(4,128)} %copy-done.7) | copy-start | bytes 73732
  562.4 154.8 %all-gather.2.cloned.1.call-start = ((), (), s32[]{:S(2)}) async-start(), calls=%async_computation.9 | async-start | bytes 3932160 | tf_op jit(solution)/shard_map/all_gather | solution.py:631
  580.9 271.8 %collective-permute-start.2 = (bf16[512,4224]{1,0:T(8,128)(2,1)}, bf16[512,4224]{1,0:T(8,128)(2,1)}, u32[]{:S(2)}, u32[]{:S(2)}) collective-permute-start(bf16[512,4224]{1,0:T(8,128)(2,1)} %convolution_convert_fusion.2), channel_id=1, source_target_pairs={{0,16},{8,24},{16,0},{24,8},{1,17},{9,25},{17,1},{25,9},{2,18},{10... | collective-permute-start | bytes 12976136 | tf_op jit(solution)/shard_map/ppermute | solution.py:58
  666.5 213.8 %collective-permute-start = (bf16[512,4224]{1,0:T(8,128)(2,1)}, bf16[512,4224]{1,0:T(8,128)(2,1)}, u32[]{:S(2)}, u32[]{:S(2)}) collective-permute-start(bf16[512,4224]{1,0:T(8,128)(2,1)} %convolution_convert_fusion.3), channel_id=1, source_target_pairs={{0,8},{8,0},{16,24},{24,16},{1,9},{9,1},{17,25},{25,17},{2,10},{10... | collective-permute-start | bytes 12976136 | tf_op jit(solution)/shard_map/ppermute | solution.py:58
  677.4 195.5 %collective-permute-start.6 = (bf16[2112,512]{1,0:T(8,128)(2,1)}, bf16[2112,512]{1,0:T(8,128)(2,1)}, u32[]{:S(2)}, u32[]{:S(2)}) collective-permute-start(bf16[2112,512]{1,0:T(8,128)(2,1)} %pad_maximum_fusion.4), channel_id=1, source_target_pairs={{0,16},{8,24},{16,0},{24,8},{1,17},{9,25},{17,1},{25,9},{2,18},{10... | collective-permute-start | bytes 6488072 | tf_op jit(solution)/shard_map/ppermute | solution.py:58
  769.4 42.3 %all-to-all-start = ((bf16[4,192,2048]{2,1,0:T(8,128)(2,1)}), bf16[4,192,2048]{2,1,0:T(8,128)(2,1)}, u32[]{:S(2)}, u32[]{:S(2)}) async-start(bf16[4,192,2048]{2,1,0:T(8,128)(2,1)} %bitcast.76), calls=%async_computation.2 | async-start | bytes 6291456 | tf_op jit(solution)/shard_map/all_to_all | solution.py:665
  774.1 199.7 %all-reduce.4.cloned.1.call-start = ((), (), s32[]{:S(2)}) async-start(), calls=%async_computation.12 | async-start | bytes 229376
  783.7 89.2 %collective-permute-start.4 = (bf16[2112,512]{1,0:T(8,128)(2,1)}, bf16[2112,512]{1,0:T(8,128)(2,1)}, u32[]{:S(2)}, u32[]{:S(2)}) collective-permute-start(bf16[2112,512]{1,0:T(8,128)(2,1)} %pad_maximum_fusion.3), channel_id=1, source_target_pairs={{0,8},{8,0},{16,24},{24,16},{1,9},{9,1},{17,25},{25,17},{2,10},{10... | collective-permute-start | bytes 6488072 | tf_op jit(solution)/shard_map/ppermute | solution.py:58
  791.6 24.2 %copy-start.24 = (bf16[768,512]{1,0:T(8,128)(2,1)S(1)}, bf16[768,512]{1,0:T(8,128)(2,1)}, u32[]{:S(2)}) copy-start(bf16[768,512]{1,0:T(8,128)(2,1)} %get-tuple-element.53) | copy-start | bytes 2359300
  815.7 167.4 %reduce-scatter.11.cloned.1.call-start = ((), (), s32[]{:S(2)}) async-start(), calls=%async_computation.11 | async-start | bytes 2359296 | tf_op jit(solution)/shard_map/reduce_scatter | solution.py:678
  820.9 234.1 %reduce-scatter.9.cloned.1.call-start = ((), (), s32[]{:S(2)}) async-start(), calls=%async_computation.10 | async-start | bytes 7077888 | tf_op jit(solution)/shard_map/reduce_scatter | solution.py:675
  857.5 50.6 %collective-permute-start.3 = (bf16[256,4224]{1,0:T(8,128)(2,1)}, bf16[256,4224]{1,0:T(8,128)(2,1)}, u32[]{:S(2)}, u32[]{:S(2)}) collective-permute-start(bf16[256,4224]{1,0:T(8,128)(2,1)} %fusion.9), channel_id=1, source_target_pairs={{0,8},{8,0},{16,24},{24,16},{1,9},{9,1},{17,25},{25,17},{2,10},{10... | collective-permute-start | bytes 6488072 | tf_op jit(solution)/shard_map/ppermute | solution.py:58
  865.1 43.1 %slice-start.2 = ((s8[17301504]{0:T(1024)(128)(4,1)}), s8[4194304]{0:T(1024)(128)(4,1)S(1)}, s32[]{:S(2)}) async-start(s8[17301504]{0:T(1024)(128)(4,1)} %bitcast.281), calls=%async_computation.15 | async-start | bytes 8388608
  865.1 43.1 %slice-start.3 = ((s8[17301504]{0:T(1024)(128)(4,1)}), s8[4194304]{0:T(1024)(128)(4,1)S(1)}, s32[]{:S(2)}) async-start(s8[17301504]{0:T(1024)(128)(4,1)} %bitcast.281), calls=%async_computation.16 | async-start | bytes 8388608
  865.1 43.1 %slice-start.4 = ((s8[17301504]{0:T(1024)(128)(4,1)}), s8[4194304]{0:T(1024)(128)(4,1)S(1)}, s32[]{:S(2)}) async-start(s8[17301504]{0:T(1024)(128)(4,1)} %bitcast.281), calls=%async_computation.17 | async-start | bytes 8388608
  865.1 43.1 %slice-start.5 = ((s8[17301504]{0:T(1024)(128)(4,1)}), s8[4194304]{0:T(1024)(128)(4,1)S(1)}, s32[]{:S(2)}) async-start(s8[17301504]{0:T(1024)(128)(4,1)} %bitcast.281), calls=%async_computation.18 | async-start | bytes 8388608
  872.9 35.3 %slice-start.6 = ((s8[17301504]{0:T(1024)(128)(4,1)}), s8[524288]{0:T(1024)(128)(4,1)S(1)}, s32[]{:S(2)}) async-start(s8[17301504]{0:T(1024)(128)(4,1)} %bitcast.281), calls=%async_computation.19 | async-start | bytes 1048576
  878.3 51.1 %collective-permute-start.7 = (bf16[2112,256]{1,0:T(8,128)(2,1)}, bf16[2112,256]{1,0:T(8,128)(2,1)}, u32[]{:S(2)}, u32[]{:S(2)}) collective-permute-start(bf16[2112,256]{1,0:T(8,128)(2,1)} %get-tuple-element.204), channel_id=1, source_target_pairs={{0,8},{8,0},{16,24},{24,16},{1,9},{9,1},{17,25},{25,17},{2,10},{10... | collective-permute-start | bytes 3244040 | tf_op jit(solution)/shard_map/ppermute | solution.py:58
  878.8 50.7 %collective-permute-start.5 = (bf16[2112,256]{1,0:T(8,128)(2,1)}, bf16[2112,256]{1,0:T(8,128)(2,1)}, u32[]{:S(2)}, u32[]{:S(2)}) collective-permute-start(bf16[2112,256]{1,0:T(8,128)(2,1)} %get-tuple-element.205), channel_id=1, source_target_pairs={{0,16},{8,24},{16,0},{24,8},{1,17},{9,25},{17,1},{25,9},{2,18},{10... | collective-permute-start | bytes 3244040 | tf_op jit(solution)/shard_map/ppermute | solution.py:58
  913.4 45.4 %collective-permute-start.1 = (bf16[256,4224]{1,0:T(8,128)(2,1)}, bf16[256,4224]{1,0:T(8,128)(2,1)}, u32[]{:S(2)}, u32[]{:S(2)}) collective-permute-start(bf16[256,4224]{1,0:T(8,128)(2,1)} %get-tuple-element.196), channel_id=1, source_target_pairs={{0,16},{8,24},{16,0},{24,8},{1,17},{9,25},{17,1},{25,9},{2,18},{10... | collective-permute-start | bytes 6488072 | tf_op jit(solution)/shard_map/ppermute | solution.py:58
  919.4 65.5 %all-to-all-start.1 = ((bf16[8,24,4096]{2,1,0:T(8,128)(2,1)}), bf16[8,24,4096]{2,1,0:T(8,128)(2,1)}, u32[]{:S(2)}, u32[]{:S(2)}) async-start(bf16[8,24,4096]{2,1,0:T(8,128)(2,1)} %bitcast.305), calls=%async_computation.3 | async-start | bytes 3145728 | tf_op jit(solution)/shard_map/all_to_all | solution.py:671
  934.2 28.8 %slice-start = ((s8[4325376]{0:T(1024)(128)(4,1)}), s8[4194304]{0:T(1024)(128)(4,1)S(1)}, s32[]{:S(2)}) async-start(s8[4325376]{0:T(1024)(128)(4,1)} %bitcast.279), calls=%async_computation.13 | async-start | bytes 8388608
  936.2 26.8 %slice-start.1 = ((s8[4325376]{0:T(1024)(128)(4,1)}), s8[131072]{0:T(1024)(128)(4,1)S(1)}, s32[]{:S(2)}) async-start(s8[4325376]{0:T(1024)(128)(4,1)} %bitcast.279), calls=%async_computation.14 | async-start | bytes 262144
  988.9 69.7 %copy-start.47 = (pred[8]{0:T(512)(128)(4,1)S(1)}, pred[8]{0:T(512)(128)(4,1)}, u32[]{:S(2)}) copy-start(pred[8]{0:T(512)(128)(4,1)} %get-tuple-element.238) | copy-start | bytes 28
  1055.0 12.5 %all-to-all-start.2 = ((bf16[4,64,1536]{2,1,0:T(8,128)(2,1)}), bf16[4,64,1536]{2,1,0:T(8,128)(2,1)S(1)}, u32[]{:S(2)}, u32[]{:S(2)}) async-start(bf16[4,64,1536]{2,1,0:T(8,128)(2,1)} %reduce-scatter.9.cloned.1.call-done), calls=%async_computation.5 | async-start | bytes 1572864 | tf_op jit(solution)/shard_map/all_to_all | solution.py:676
  (66 other events, 391.9 us)
Sparse Core Ops, SparseCore 0:
  492.3 67.9 reduce-scatter.4
  562.7 71.8 reduce-scatter.6
  649.6 67.5 all-gather.1
  815.9 124.3 all-reduce.3
  942.6 40.5 reduce-scatter.10
  985.4 69.5 reduce-scatter.8

commit v4 on v3

--- a/solution.py
+++ b/solution.py
@@ -16,7 +16,7 @@
 F32 = jnp.float32
 BF16 = jnp.bfloat16
 MESH = pl.DeviceIdType.MESH
-VMEM_LIMIT = 56 * 2**20
+VMEM_LIMIT = 61 * 2**20
 
 ORDER = ((0, 0), (0, 1), (2, 0), (1, 1), (1, 0), (3, 0), (2, 1), (3, 1))
 
@@ -193,11 +193,11 @@
 
     def spot(full, i, where):
         cut = pl.ds(where * eighth, eighth)
-        return full.at[cut] if i < 4 else full.at[:, cut]
+        return full.at[cut] if i < 2 else full.at[:, cut]
 
     def own_half(shard, i, half):
         cut = pl.ds(half * eighth, eighth)
-        return shard.at[cut] if i < 4 else shard.at[:, cut]
+        return shard.at[cut] if i < 2 else shard.at[:, cut]
 
     def remote(src, dst, send, recv, device):
         return pltpu.make_async_remote_copy(src, dst, send, recv, device_id=device, device_id_type=MESH)
@@ -209,7 +209,7 @@
     put = [pltpu.make_async_copy(cot_by, g_all.at[f, f], local_sem.at[4])]
     for i in range(6):
         cut = pl.ds(0, 2 * eighth)
-        target = fulls[i].at[cut] if i < 4 else fulls[i].at[:, cut]
+        target = fulls[i].at[cut] if i < 2 else fulls[i].at[:, cut]
         put.append(pltpu.make_async_copy(shard_by[i], target, local_sem.at[5 + i]))
     for copy in take:
         copy.start()
@@ -428,7 +428,7 @@
     ]
     for i, shard in enumerate(shards_in):
         rows, columns = shard.shape
-        out.append(shape((4 * rows, columns) if i < 4 else (rows, 4 * columns), BF16))
+        out.append(shape((4 * rows, columns) if i < 2 else (rows, 4 * columns), BF16))
     anywhere = pl.BlockSpec(memory_space=pl.ANY)
     in_vmem = pl.BlockSpec(memory_space=pltpu.VMEM)
     vmem = pltpu.VMEM
@@ -451,6 +451,356 @@
     )(tok, cot, wq, wo, small, *shards_in, *tables)
 
 
+def backward_kernel(S, N, sizes, *refs):
+    D, own, heads = sizes
+    to_x, to_y, from_x, from_y, keep, refs = refs[:2], refs[2:4], refs[4:8], refs[8:12], refs[12:18], refs[18:]
+    w_in, w_back, normed_all, qkv, mixed, gh, unit, inverse, gain_row, ready, ctx, cos, sin, first, place, place_row, *refs = refs
+    grads, refs = refs[:6], refs[6:]
+    mixed_out, gx_out, gin_out, gout_out, small_out, bias_out, vec_far, gin_buf, gout_buf, gin_pair, gout_pair, *refs = refs
+    from_x, from_y, refs = (*refs[:2], *from_x), (*refs[2:4], *from_y), refs[4:]
+    then_y, then_x, pair_y, pair_x, refs = refs[:6], refs[6:12], refs[12:18], refs[18:24], refs[24:]
+    loads, sums, refs = refs[:3], refs[3:6], refs[6:]
+    w_v, wb_v, ga_v, na_v, qkv_v, gc_v, gk_v, gv_v, part_send, part_recv, gn_v, gi_v, go_v, *refs = refs
+    in_mine, in_pair, in_stage, in_far, out_mine, out_pair, out_stage, out_far, *refs = refs
+    vec_v, vec_tmp, vec_sum, vec_near, mixed_v, gx_v, *refs = refs
+    (step_send, step_recv, load_sem, ga_send, ga_recv, part_sems, part_semr, pair_send, pair_recv, far_send, far_recv,
+     last_send, last_recv, vec_sems, vec_semr, near_sems, near_semr, home_send, home_recv, local_sem) = refs
+    s, f = lax.axis_index("seq"), lax.axis_index("fsdp")
+    px, py, pd = partners(s)
+    chip, core, chips = f // 2, lax.rem(f, 2), N // 2
+    eighth = D // 8
+    L = gh.shape[0]
+    R = S * L
+    width = heads * HD
+    pr = L // N
+    kind = (0, 0, 1, 1, 2, 1)
+
+    def remote(src, dst, send, recv, device):
+        return pltpu.make_async_remote_copy(src, dst, send, recv, device_id=device, device_id_type=MESH)
+
+    def part(ref, i, k):
+        cut = pl.ds(k * eighth, eighth)
+        return ref.at[cut] if i < 2 else ref.at[:, cut]
+
+    def give_copy(i, way):
+        a, b, to = ((to_x, from_x, px), (to_y, from_y, py))[way]
+        return remote(a[i], b[i], step_send.at[i, way], step_recv.at[i, way], (to, f))
+
+    def then_copy(i, way):
+        a, b, to = ((pair_y, then_y, py), (pair_x, then_x, px))[way]
+        return remote(a[i], b[i], step_send.at[i, 2 + way], step_recv.at[i, 2 + way], (to, f))
+
+    def give(i):
+        for way in range(2):
+            give_copy(i, way).start()
+
+    def fetch(i, sources):
+        copies = [pltpu.make_async_copy(u, loads[kind[i]].at[k], load_sem.at[k]) for k, u in enumerate(sources)]
+        for copy in copies:
+            copy.start()
+        for copy in copies:
+            copy.wait()
+
+    def second(i):
+        buf = loads[kind[i]]
+        for way, (place_in_keep, arrived) in enumerate(((2, from_x[i]), (3, from_y[i]))):
+            if i < 2:
+                give_copy(i, way).wait_recv()
+            fetch(i, (part(keep[i], i, place_in_keep), part(arrived, i, 1)))
+            buf[0] = (buf[0].astype(F32) + buf[1].astype(F32)).astype(BF16)
+            copy = pltpu.make_async_copy(buf.at[0], (pair_y, pair_x)[way][i], load_sem.at[0])
+            copy.start()
+            copy.wait()
+            then_copy(i, way).start()
+
+    def third(i):
+        buf, total = loads[kind[i]], sums[kind[i]]
+        for way, (arrived, last) in enumerate(((from_x[i], then_y[i]), (from_y[i], then_x[i]))):
+            then_copy(i, way).wait_recv()
+            fetch(i, (part(keep[i], i, way), part(arrived, i, 0), last))
+            total[...] = buf[0].astype(F32) + buf[1].astype(F32) + buf[2].astype(F32)
+            copy = pltpu.make_async_copy(total, part(grads[i], i, way), load_sem.at[0])
+            copy.start()
+            copy.wait()
+
+    def reducer(block, pair, mine, other, stage, far, k):
+        def pair_copy(q):
+            return remote(block(2 * q + 1 - core), pair.at[q], pair_send.at[k, q], pair_recv.at[k, q], (s, 2 * chip + 1 - core))
+
+        def far_copy(d):
+            to = lax.rem(chip + d, chips)
+            return remote(stage.at[d], far.at[d - 1], far_send.at[k, d - 1], far_recv.at[k, d - 1], (s, 2 * to + core))
+
+        def begin():
+            for q in range(chips):
+                pair_copy(q).start()
+
+        def middle():
+            for q in range(chips):
+                pair_copy(q).wait_recv()
+            for d in range(1, chips + 1):
+                d = d % chips
+                q = lax.rem(chip + d, chips)
+                copies = (
+                    pltpu.make_async_copy(block(2 * q + core), mine, load_sem.at[0]),
+                    pltpu.make_async_copy(pair.at[q], other, load_sem.at[1]),
+                )
+                for copy in copies:
+                    copy.start()
+                for copy in copies:
+                    copy.wait()
+                stage[d] = (mine[...].astype(F32) + other[...].astype(F32)).astype(BF16)
+                if d:
+                    far_copy(d).start()
+
+        def end():
+            total = stage[0].astype(F32)
+            for d in range(1, chips):
+                far_copy(d).wait_recv()
+                total = total + far[d - 1].astype(F32)
+            return total
+
+        def drain():
+            for q in range(chips):
+                pair_copy(q).wait_send()
+            for d in range(1, chips):
+                far_copy(d).wait_send()
+
+        return begin, middle, end, drain
+
+    in_begin, in_middle, in_end, in_drain = reducer(
+        lambda j: gin_buf.at[:, j], gin_pair, in_mine, in_pair, in_stage, in_far, 0)
+    out_begin, out_middle, out_end, out_drain = reducer(
+        lambda j: gout_buf.at[j], gout_pair, out_mine, out_pair, out_stage, out_far, 1)
+
+    begin = [
+        pltpu.make_async_copy(w_back, wb_v, local_sem.at[0]), pltpu.make_async_copy(w_in, w_v, local_sem.at[1]),
+        pltpu.make_async_copy(qkv, qkv_v, local_sem.at[2]), pltpu.make_async_copy(normed_all, na_v, local_sem.at[3]),
+        pltpu.make_async_copy(mixed.at[f], mixed_v, local_sem.at[4]),
+    ]
+    for copy in begin:
+        copy.start()
+    ga_v[s] = gh[...].astype(BF16)
+    greet(s, f, S, N)
+    spread = [
+        remote(ga_v.at[s], ga_v.at[s], ga_send.at[k], ga_recv.at[k], (other, f)) for k, other in enumerate((px, py, pd))
+    ]
+    for copy in spread:
+        copy.start()
+    give(0)
+    homing = []
+    for k in range(1, N):
+        to = lax.rem(f + k, N)
+        homing.append(remote(mixed.at[to], mixed_out.at[f], home_send.at[0, k - 1], home_recv.at[0, k - 1], (s, to)))
+        homing[-1].start()
+    for copy in begin:
+        copy.wait()
+    done = [pltpu.make_async_copy(mixed_v, mixed_out.at[f], local_sem.at[4 + N])]
+    done[0].start()
+    for copy in spread:
+        copy.wait_recv()
+    give(1)
+
+    def project(pair, carry):
+        out = dot_nt(ga_v[...].reshape(R, D), wb_v.at[pl.ds(pair * (N * 2 // heads), N * 2 // heads)][...].reshape(2 * HD, D))
+        gc_v[2 * pair] = out[:, :HD].astype(BF16)
+        gc_v[2 * pair + 1] = out[:, HD:].astype(BF16)
+        return carry
+
+    lax.fori_loop(0, heads // 2, project, 0)
+
+    def out_grad(column, carry):
+        cut = pl.ds(pl.multiple_of(column * 2 * eighth, 2 * eighth), 2 * eighth)
+        go_v[:, cut] = dot_t(ctx[...], ga_v[:, :, cut].reshape(R, 2 * eighth)).astype(BF16)
+        return carry
+
+    lax.fori_loop(0, 4, out_grad, 0)
+    second(4)
+    for j in range(N):
+        pltpu.make_async_copy(go_v.at[pl.ds(j * own, own)], gout_buf.at[j], local_sem.at[4 + j]).start()
+    for j in range(N):
+        pltpu.make_async_copy(go_v.at[pl.ds(j * own, own)], gout_buf.at[j], local_sem.at[4 + j]).wait()
+    out_begin()
+
+    def attend(h, carry):
+        rows = R // 4
+        gk_v[...] = jnp.zeros_like(gk_v)
+        gv_v[...] = jnp.zeros_like(gv_v)
+        for block in range(4):
+            cut = pl.ds(block * rows, rows)
+            q, gc = qkv_v[h, cut, :], gc_v[h, cut, :]
+            raw = dot_nt(q, qkv_v[heads + h])
+            ok = (first[cut, :] <= place_row[...]) & (place_row[...] <= place[cut, :])
+            scores = jnp.where(ok, raw * HD**-0.5, MASKED)
+            weights = jnp.exp(scores - jnp.max(scores, axis=-1, keepdims=True))
+            chance = weights / jnp.sum(weights, axis=-1, keepdims=True)
+            grad_chance = dot_nt(gc, qkv_v[2 * heads + h])
+            delta = jnp.sum(chance * grad_chance, axis=-1, keepdims=True)
+            grad_raw = (chance * (grad_chance - delta) * HD**-0.5).astype(BF16)
+            gk_v[...] += dot_t(grad_raw, q)
+            gv_v[...] += dot_t(chance.astype(BF16), gc)
+            gq = dot(grad_raw, qkv_v[heads + h]).astype(BF16).astype(F32)
+            gq = gq * cos[cut, :] + pltpu.roll(gq * sin[cut, :], HD // 2, 1)
+            qkv_v[h, cut, :] = gq.astype(BF16)
+        gk = gk_v[...].astype(BF16).astype(F32)
+        gk = gk * cos[...] + pltpu.roll(gk * sin[...], HD // 2, 1)
+        qkv_v[heads + h] = gk.astype(BF16)
+        qkv_v[2 * heads + h] = gv_v[...].astype(BF16)
+        return carry
+
+    lax.fori_loop(0, heads, attend, 0)
+    for c in range(3 * heads):
+        vec_v[D // 128 + c : D // 128 + c + 1, :] = jnp.sum(qkv_v[c].astype(F32), axis=0, keepdims=True)
+
+    def partial(rows):
+        cut = pl.ds(pl.multiple_of(rows * L, L), L)
+        left = jnp.concatenate([qkv_v[c, cut, :] for c in range(3 * heads)], axis=1)
+        return dot_nt(left, w_v[...].reshape(D, 3 * width))
+
+    exchange = []
+    for k, other in enumerate((px, py, pd)):
+        part_send[k] = partial(other).astype(BF16)
+        exchange.append(remote(part_send.at[k], part_recv.at[k], part_sems.at[k], part_semr.at[k], (other, f)))
+        exchange[-1].start()
+    gn_v[...] = partial(s)
+    second(5)
+    second(2)
+
+    def in_grad(i, carry):
+        cut = pl.ds(pl.multiple_of(i * 2 * eighth, 2 * eighth), 2 * eighth)
+        left = na_v[:, :, cut].reshape(R, 2 * eighth)
+        for c in range(0, 3 * heads, 2):
+            right = jnp.concatenate([qkv_v[c], qkv_v[c + 1]], axis=1)
+            gi_v[:, :, c * HD : (c + 2) * HD] = dot_t(left, right).astype(BF16).reshape(N, own, 2 * HD)
+        copy = pltpu.make_async_copy(gi_v, gin_buf.at[i], local_sem.at[0])
+        copy.start()
+        copy.wait()
+        return carry
+
+    lax.fori_loop(0, S, in_grad, 0)
+    in_begin()
+    out_middle()
+    second(3)
+    in_middle()
+    for k in range(3):
+        exchange[k].wait_recv()
+        gn_v[...] += part_recv[k].astype(F32)
+    scaled = gn_v[...] * gain_row[...]
+    scaled = scaled - unit[...] * jnp.mean(scaled * unit[...], axis=-1, keepdims=True)
+    gx = (gh[...] + inverse[...] * scaled).astype(BF16)
+    for j in range(N):
+        gx_v[j] = gx[j * pr : (j + 1) * pr, :]
+    done.append(pltpu.make_async_copy(gx_v.at[f], gx_out.at[f], local_sem.at[5 + N]))
+    done[1].start()
+    for k in range(1, N):
+        to = lax.rem(f + k, N)
+        homing.append(remote(gx_v.at[to], gx_out.at[f], home_send.at[1, k - 1], home_recv.at[1, k - 1], (s, to)))
+        homing[-1].start()
+    gain = jnp.sum(gn_v[...] * unit[...], axis=0, keepdims=True)
+    for line in range(D // 128):
+        vec_v[line : line + 1, :] = gain[:, line * 128 : (line + 1) * 128]
+    vec_v[D // 128 + 16 :, :] = ready[...]
+    small = []
+    for k in range(1, N):
+        to = lax.rem(f + k, N)
+        small.append(remote(vec_v, vec_far.at[k - 1], vec_sems.at[k - 1], vec_semr.at[k - 1], (s, to)))
+        small[-1].start()
+    second(0)
+    second(1)
+    vec_sum[...] = vec_v[...]
+    for k in range(1, N):
+        small[k - 1].wait_recv()
+        copy = pltpu.make_async_copy(vec_far.at[k - 1], vec_tmp, local_sem.at[2])
+        copy.start()
+        copy.wait()
+        vec_sum[...] += vec_tmp[...]
+    for k, other in enumerate((px, py, pd)):
+        small.append(remote(vec_sum, vec_near.at[k], near_sems.at[k], near_semr.at[k], (other, f)))
+        small[-1].start()
+    gout_out[...] = out_end()
+    in_stage[0] = in_end().astype(BF16)
+    last = [
+        remote(in_stage.at[0, other], gin_out.at[s], last_send.at[k], last_recv.at[k], (other, f))
+        for k, other in enumerate((px, py, pd))
+    ]
+    for copy in last:
+        copy.start()
+    done.append(pltpu.make_async_copy(in_stage.at[0, s], gin_out.at[s], local_sem.at[1]))
+    done[2].start()
+    for i in (4, 5, 2, 3, 0, 1):
+        third(i)
+    for i in range(6):
+        for way in range(2):
+            if i < 2:
+                give_copy(i, way).wait_send()
+            then_copy(i, way).wait_send()
+    in_drain()
+    out_drain()
+    for copy in spread + exchange + small:
+        copy.wait_send()
+    for copy in last + homing:
+        copy.wait()
+    bias_out[s] = vec_sum[D // 128 : D // 128 + 16, :]
+    for k, other in enumerate((px, py, pd)):
+        small[N - 1 + k].wait_recv()
+        bias_out[other] = vec_near[k, D // 128 : D // 128 + 16, :]
+    small_out[...] = vec_sum[...] + vec_near[0] + vec_near[1] + vec_near[2]
+    for copy in done:
+        copy.wait()
+
+
+def backward(S, N, to_x, to_y, from_x, from_y, keep, w_in, w_back, normed_all, qkv, mixed, gh, unit, inverse, gain_row, ready, ctx, tables):
+    own, D = w_back.shape[1:]
+    L = gh.shape[0]
+    R = S * L
+    heads = H // S
+    width = heads * HD
+    chips = N // 2
+    dma = pltpu.SemaphoreType.DMA
+    shape = jax.ShapeDtypeStruct
+    vmem = pltpu.VMEM
+    eighth = D // 8
+    blocks = [(eighth, u.shape[1]) if i < 2 else (u.shape[0], eighth) for i, u in enumerate(keep)]
+    wholes = [(2 * eighth, u.shape[1]) if i < 2 else (u.shape[0], 2 * eighth) for i, u in enumerate(keep)]
+    kinds = [blocks[i] for i in (0, 2, 4)]
+    in_block, out_block = (S, own, 3 * width), (own, D)
+    vec = (D // 128 + 16 + ready.shape[0], 128)
+    out = [shape(w, F32) for w in wholes] + [
+        shape(mixed.shape, BF16), shape(mixed.shape, BF16), shape(in_block, BF16), shape(out_block, F32), shape(vec, F32),
+        shape((S, 16, 128), F32),
+        shape((N - 1,) + vec, F32),
+        shape((S, N) + in_block[1:], BF16), shape((N,) + out_block, BF16), shape((chips,) + in_block, BF16),
+        shape((chips,) + out_block, BF16),
+    ]
+    out += [shape(w, BF16) for w in wholes[:2] * 2] + [shape(b, BF16) for b in blocks * 4]
+    anywhere = pl.BlockSpec(memory_space=pl.ANY)
+    in_vmem = pl.BlockSpec(memory_space=vmem)
+    result = pl.pallas_call(
+        functools.partial(backward_kernel, S, N, (D, own, heads)),
+        out_shape=out,
+        in_specs=[anywhere] * 23 + [in_vmem] * 11,
+        out_specs=[anywhere] * 9 + [in_vmem] * 3 + [anywhere] * (len(out) - 12),
+        scratch_shapes=[vmem((3,) + k, BF16) for k in kinds] + [vmem(k, F32) for k in kinds]
+        + [
+            vmem(w_in.shape, BF16), vmem(w_back.shape, BF16), vmem((S, L, D), BF16), vmem((S, L, D), BF16),
+            vmem(qkv.shape, BF16), vmem((heads, R, HD), BF16), vmem((R, HD), F32), vmem((R, HD), F32),
+            vmem((3, L, D), BF16), vmem((3, L, D), BF16), vmem((L, D), F32), vmem((N, own, 3 * width), BF16),
+            vmem((width, D), BF16),
+            vmem(in_block, BF16), vmem(in_block, BF16), vmem((chips,) + in_block, BF16), vmem((chips - 1,) + in_block, BF16),
+            vmem(out_block, BF16), vmem(out_block, BF16), vmem((chips,) + out_block, BF16),
+            vmem((chips - 1,) + out_block, BF16),
+            vmem(vec, F32), vmem(vec, F32), vmem(vec, F32), vmem((3,) + vec, F32),
+            vmem(mixed.shape[1:], BF16), vmem(mixed.shape, BF16),
+            dma((6, 4)), dma((6, 4)), dma((3,)), dma((3,)), dma((3,)), dma((3,)), dma((3,)), dma((2, chips)),
+            dma((2, chips)), dma((2, chips - 1)), dma((2, chips - 1)), dma((3,)), dma((3,)), dma((N - 1,)), dma((N - 1,)),
+            dma((3,)), dma((3,)), dma((2, N - 1)), dma((2, N - 1)), dma((6 + N,)),
+        ],
+        compiler_params=pltpu.CompilerParams(collective_id=1, has_side_effects=True, vmem_limit_bytes=VMEM_LIMIT),
+        name="backward",
+    )(*to_x, *to_y, *from_x, *from_y, *keep, w_in, w_back, normed_all, qkv, mixed, gh, unit, inverse, gain_row, ready, ctx, *tables)
+    return result[:12]
+
+
 def shards(
     tokens, cotangent, ids, deal, lengths, w_qkv, b_qkv, w_out, gain_attn, gain_ffn, w_router,
     w_shared_gate, e_gate, e_up, e_down, s_gate, s_up, s_down,
@@ -513,7 +863,7 @@
     wq = w_qkv.reshape(own, 3, S, width).transpose(2, 0, 1, 3).reshape(S, own, 3 * width)
     x_rows, g_all, w_in, w_back, small, normed_all, qkv, context, hidden, x_all, *fulls = forward(
         S, N, MB, deal_out(tokens), deal_out(arrange(cotangent, order)), wq, w_out, small,
-        (e_gate[0], e_up[0], s_gate, s_up, e_down[0], s_down), tables,
+        (e_gate[0], e_up[0], s_gate.T, s_up.T, e_down[0], s_down), tables,
     )
     L, R = MB * T, MB * pack
 
@@ -523,7 +873,6 @@
     gain_1, gain_2, shared_w = vector(0), vector(1), vector(4).astype(BF16)
     router_w = small[:, :, r_line:i_line].swapaxes(0, 1).reshape(S * N, -1)[:, : own * E].reshape(D, E).astype(BF16)
     all_ids = small[:, :, i_line:].reshape(N, S, -1)[:, :, : MB * T * TOP]
-    w_in, w_back = w_in.reshape(D, 3 * width), w_back.reshape(width, D)
     eg, eu, sg, su, ed, sd = fulls
     x0 = x_rows.reshape(L, D).astype(F32)
     cot = arrange(lax.dynamic_index_in_dim(g_all, f, 0, keepdims=False).reshape(L, D), inverse_order)
@@ -554,7 +903,7 @@
     gate, up = dot(x, eg), dot(x, eu)
     act = (jax.nn.silu(gate) * up).astype(BF16)
     out_e = dot(act, ed).astype(BF16).astype(F32)
-    sgate, sup = dot(x, sg), dot(x, su)
+    sgate, sup = dot_nt(x, sg), dot_nt(x, su)
     sact = (jax.nn.silu(sgate) * sup).astype(BF16)
     out_s = dot(sact, sd)
     y = (gate_f * out_e + sigma_rows * out_s).astype(BF16)
@@ -565,48 +914,29 @@
     grad_gate, grad_up = swiglu_back(dot_nt(geo, ed), gate, up)
     grad_sgate, grad_sup = swiglu_back(dot_nt(gso, sd), sgate, sup)
     dx_e = (dot_nt(grad_gate, eg) + dot_nt(grad_up, eu)).astype(BF16).astype(F32)
-    dx = dx_e + dot_nt(grad_sgate, sg) + dot_nt(grad_sup, su)
+    dx = dx_e + dot(grad_sgate, sg) + dot(grad_sup, su)
     mine = (jnp.arange(N) == f).astype(F32)
     notes = [part[:, None] * mine for value in (gg, gs) for part in split3(value)]
     note_pad = -(6 * N) % 128
     payload = jnp.concatenate([dx] + notes + [jnp.zeros((rows, note_pad), F32)], axis=1).astype(BF16)
     dx = lax.psum_scatter(payload, "fsdp", scatter_dimension=0, tiled=True).astype(F32)
 
-    cat_grad = jnp.concatenate([grad_gate, grad_up, grad_sgate, grad_sup], axis=1)
     half = D // 8
-    send_x = dot_t(x[:, 4 * half : 6 * half], cat_grad).astype(BF16)
-    send_y = dot_t(x[:, 6 * half :], cat_grad).astype(BF16)
-    from_x, from_y = across(send_x, 1), across(send_y, 2)
-
-    def down_grad(lo, hi):
-        return jnp.concatenate([dot_t(act, geo[:, lo:hi]), dot_t(sact, gso[:, lo:hi])], axis=0)
-
-    bsend_x = down_grad(4 * half, 6 * half).astype(BF16)
-    bsend_y = down_grad(6 * half, 8 * half).astype(BF16)
-    bfrom_x, bfrom_y = across(bsend_x, 1), across(bsend_y, 2)
-    keep = dot_t(x[:, : 4 * half], cat_grad)
-    bkeep = down_grad(0, 4 * half)
-    to_y = (keep[2 * half : 3 * half] + from_x[half:].astype(F32)).astype(BF16)
-    to_x = (keep[3 * half :] + from_y[half:].astype(F32)).astype(BF16)
-    last_y, last_x = across(to_y, 2), across(to_x, 1)
-    bto_y = (bkeep[:, 2 * half : 3 * half] + bfrom_x[:, half:].astype(F32)).astype(BF16)
-    bto_x = (bkeep[:, 3 * half :] + bfrom_y[:, half:].astype(F32)).astype(BF16)
-    blast_y, blast_x = across(bto_y, 2), across(bto_x, 1)
-    grad_a = jnp.concatenate(
-        [
-            keep[:half] + from_x[:half].astype(F32) + last_y.astype(F32),
-            keep[half : 2 * half] + from_y[:half].astype(F32) + last_x.astype(F32),
-        ],
-        axis=0,
-    )
-    grad_b = jnp.concatenate(
-        [
-            bkeep[:, :half] + bfrom_x[:, :half].astype(F32) + blast_y.astype(F32),
-            bkeep[:, half : 2 * half] + bfrom_y[:, :half].astype(F32) + blast_x.astype(F32),
-        ],
-        axis=1,
-    )
-    g_eg, g_eu, g_sg, g_su = jnp.split(grad_a, (FE, 2 * FE, 2 * FE + FS), axis=1)
+    cuts = (slice(4 * half, 6 * half), slice(6 * half, 8 * half), slice(0, 4 * half))
+
+    def by_columns(cut):
+        return (
+            dot_t(grad_sgate, x[:, cut]).astype(BF16), dot_t(grad_sup, x[:, cut]).astype(BF16),
+            dot_t(act, geo[:, cut]).astype(BF16), dot_t(sact, gso[:, cut]).astype(BF16),
+        )
+
+    def by_rows(cut):
+        return dot_t(x[:, cut], grad_gate).astype(BF16), dot_t(x[:, cut], grad_up).astype(BF16)
+
+    from_x = [across(u, 1) for u in by_columns(cuts[0])]
+    from_y = [across(u, 2) for u in by_columns(cuts[1])]
+    to_x, to_y = by_rows(cuts[0]), by_rows(cuts[1])
+    keep = by_rows(cuts[2]) + by_columns(cuts[2])
 
     mixed = (hidden + arrange(y, inverse_order).astype(F32)).astype(BF16)
     base = D
@@ -628,69 +958,30 @@
     from_norm, g_gain_2 = rms_backward(grad_normed2, unit_2, inverse_2, gain_2)
     grad_hidden = cot.astype(F32) + from_norm
 
-    grad_attn = lax.all_gather(grad_hidden.astype(BF16), "seq", axis=0, tiled=True)
-    g_out = dot_t(context, grad_attn)
-    gc = dot_nt(grad_attn, w_back).astype(BF16)
-
-    def by_micro(u):
-        u = u.reshape(u.shape[0], S * N, MB, piece, HD).transpose(2, 0, 1, 3, 4)
-        return u.reshape(MB, u.shape[1], pack, HD)
-
-    qkv = by_micro(qkv)
-    q, k, v = qkv[:, :heads], qkv[:, heads : 2 * heads], qkv[:, 2 * heads :]
-    gc = by_micro(gc.reshape(R, heads, HD).swapaxes(0, 1))
-    at = spots[:, :, 0].reshape(-1)
-    low = start.transpose(2, 0, 1, 3).reshape(MB, pack)
-    allowed = (low[:, :, None] <= at[None, None, :]) & (at[None, None, :] <= at[None, :, None])
-    scale = HD ** -0.5
-    raw = jnp.einsum("mhqd,mhkd->mhqk", q, k, preferred_element_type=F32)
-    scores = jnp.where(allowed[:, None], raw * scale, MASKED)
-    weights = jnp.exp(scores - jnp.max(scores, axis=-1, keepdims=True))
-    chance = weights / jnp.sum(weights, axis=-1, keepdims=True)
-    chance_low = chance.astype(BF16)
-    grad_chance = jnp.einsum("mhqd,mhkd->mhqk", gc, v, preferred_element_type=F32)
-    delta = jnp.sum(chance * grad_chance, axis=-1, keepdims=True)
-    grad_raw = (chance * (grad_chance - delta) * scale).astype(BF16)
-    gq = jnp.einsum("mhqk,mhkd->mhqd", grad_raw, k, preferred_element_type=F32)
-    gk = jnp.einsum("mhqk,mhqd->mhkd", grad_raw, q, preferred_element_type=F32)
-    gv = jnp.einsum("mhqk,mhqd->mhkd", chance_low, gc, preferred_element_type=F32)
-    moved = jnp.stack([gq, gk, gv], axis=0).astype(BF16)
-    moved = moved.reshape(3, MB, heads, S * N, piece, HD).transpose(3, 1, 4, 0, 2, 5).reshape(R, 3, heads, HD)
-    gqk = moved[:, :2].astype(F32)
-    gqk = (gqk * cosine[:, None, None] + jnp.roll(gqk * sine[:, None, None], HD // 2, axis=-1)).astype(BF16)
-    grad_qkv = jnp.concatenate([gqk, moved[:, 2:]], axis=1).reshape(R, 3 * width)
-    g_bias = jnp.sum(grad_qkv.astype(F32), axis=0)
-    g_in = dot_t(normed_all.reshape(R, D), grad_qkv)
-    partial = dot_nt(grad_qkv, w_in).astype(BF16).reshape(S, L, D)
-    partial = lax.all_to_all(partial, "seq", split_axis=0, concat_axis=0, tiled=True)
-    grad_normed = jnp.sum(partial.astype(F32), axis=0)
-    from_first, g_gain_1 = rms_backward(grad_normed, unit_1, inverse_1, gain_1)
-    grad_x = (grad_hidden + from_first).astype(BF16)
-
-    back = jnp.concatenate([mixed, grad_x], axis=1).reshape(N, MB * piece, 2 * D)
-    back = lax.all_to_all(back, "fsdp", split_axis=0, concat_axis=0, tiled=True).reshape(N, MB, piece, 2 * D)
-    back = jnp.stack([jnp.take(back[:, m], deal[m, f], axis=0).swapaxes(0, 1) for m in range(MB)]).reshape(MB, T, 2 * D)
-    mixed, grad_tokens = back[..., :D], back[..., D:].astype(F32)
-
-    g_in = lax.psum_scatter(g_in.astype(BF16).reshape(S, N * own, 3 * width), "fsdp", scatter_dimension=1, tiled=True)
-    g_in = lax.all_to_all(g_in, "seq", split_axis=0, concat_axis=0, tiled=True)
+    ready = jnp.concatenate([g_gain_2, g_shared, g_router.reshape(-1)]).reshape(-1, 128)
+    *expert_grads, mixed, grad_x, g_in, g_out, small, g_bias = backward(
+        S, N, to_x, to_y, from_x, from_y, keep, w_in, w_back, normed_all, qkv, mixed.reshape(N, MB * piece, D), grad_hidden, unit_1,
+        inverse_1, gain_1[None], ready, context, tables,
+    )
+    def take_home(u):
+        u = u.reshape(N, MB, piece, D)
+        return jnp.stack([jnp.take(u[:, m], deal[m, f], axis=0).swapaxes(0, 1) for m in range(MB)]).reshape(MB, T, D)
+
+    mixed, grad_tokens = take_home(mixed), take_home(grad_x).astype(F32)
+
     g_in = g_in.reshape(S, own, 3, width).transpose(1, 2, 0, 3).reshape(own, 3 * D).astype(F32)
-    g_out = lax.psum_scatter(g_out.astype(BF16), "fsdp", scatter_dimension=0, tiled=True).astype(F32)
-    g_bias = jnp.where(jnp.arange(S)[None, :, None] == s, g_bias.reshape(3, 1, width), 0.0)
-    count = S * N
-    small = jnp.concatenate(
-        [
-            g_gain_1.reshape(count, own), g_gain_2.reshape(count, own), g_router.reshape(count, own * E),
-            g_shared.reshape(count, own), g_bias.reshape(count, 3 * own),
-        ],
-        axis=1,
-    )
-    small = lax.psum_scatter(small, ("seq", "fsdp"), scatter_dimension=0, tiled=True)[0]
-    cuts = (own, 2 * own, 2 * own + own * E, 3 * own + own * E)
+    g_bias = g_bias[:, : 3 * heads].reshape(S, 3, width).swapaxes(0, 1).reshape(-1)
+
+    def mine(u):
+        return lax.dynamic_slice_in_dim(u, index * (u.shape[0] // (S * N)), u.shape[0] // (S * N))
+
+    small = small.reshape(-1)
+    after = D + 16 * 128
+    g_gain_1, g_gain_2, g_shared = mine(small[:D]), mine(small[after : after + D]), mine(small[after + D : after + 2 * D])
+    g_router = mine(small[after + 2 * D :]).reshape(own, E)
     return (
-        mixed, grad_tokens, g_in, small[cuts[3] :], g_out, small[: cuts[0]], small[cuts[0] : cuts[1]],
-        small[cuts[1] : cuts[2]].reshape(own, E), small[cuts[2] : cuts[3]],
-        g_eg[None], g_eu[None], grad_b[:FE][None], g_sg, g_su, grad_b[FE:],
+        mixed, grad_tokens, g_in, mine(g_bias), g_out, g_gain_1, g_gain_2, g_router, g_shared,
+        expert_grads[0][None], expert_grads[1][None], expert_grads[4][None], expert_grads[2].T, expert_grads[3].T, expert_grads[5],
     )
 
 

time: 1090 us -> 1020 us (0.936)
  Pallas kernels: 331 us -> 581 us
  waiting for transfers between devices: 202 us -> 39.1 us
  matrix products: 306 us -> 243 us
  other arithmetic: 85.6 us -> 25.2 us
  local copies, waits for them, and re-layouts: 115 us -> 95.2 us
  starting transfers between devices: 25 us -> 8.8 us
    pallas_call x0 -> x1, Pallas kernels: none -> 254 us  [backward(): pl.pallas_call(functools.partial(backward_kernel, S, N, (D, own, heads)),...]
    reduce_scatter x2 -> x0, waiting for transfers between devices: 70.4 us -> none  [the longest x1 65.3 us: shards(): lax.psum_scatter(g_in.astype(BF16).reshape(S, N * own, 3 * width), 'fsdp'...]
    reduce_scatter x1, waiting for transfers between devices: 26.5 us -> 0.01 us  [shards(): lax.psum_scatter(payload, 'fsdp', scatter_dimension=0, tiled=True)]
    all_to_all x3 -> x0, waiting for transfers between devices: 26.2 us -> none  [the longest x1 20.1 us: shards(): lax.all_to_all(partial, 'seq', split_axis=0, concat_axis=0, tiled=True)]
    dot_general x9 -> x7, matrix products: 96.9 us -> 71.3 us  [dot_nt(): lax.dot_general(a, b, (((1,), (1,)), ((), ())), preferred_element_type=F32)]
    all_gather x1 -> x0, waiting for transfers between devices: 22.5 us -> none  [shards(): lax.all_gather(grad_hidden.astype(BF16), 'seq', axis=0, tiled=True)]
    dot_general x12 -> x19, matrix products: 102 us -> 79.4 us  [dot_t(): lax.dot_general(a, b, (((0,), (0,)), ((), ())), preferred_element_type=F32)]
    dot_general x5 -> x0, matrix products: 21.1 us -> none  [the longest x1 8.36 us: shards(): gq = jnp.einsum('mhqk,mhkd->mhqd', grad_raw, k, preferred_element_type=F32)]
  transfers between devices with their start and end apart: 17 -> 10, of which waited for: 9 -> 3; matrix products, arithmetic and copies ran while one was open for 32% -> 18% of each run, Pallas kernels for 0% -> 0%
where the time goes in v4:
time: 1020 us; the launch traced here: 1010 us
  Pallas kernels  581 us (57%)
  matrix products  243 us (24%)
  local copies, waits for them, and re-layouts  95.2 us (9%)
  waiting for transfers between devices  39.1 us (4%)
  other arithmetic  25.2 us (2%)
  between operations  16.2 us (2%)
    pallas_call x1, Pallas kernels, forward(): pl.pallas_call(functools.partial(forward_kernel, S, N, (MB, pr // MB, D,...  328 us
    pallas_call x1, Pallas kernels, backward(): pl.pallas_call(functools.partial(backward_kernel, S, N, (D, own, heads)),...  254 us
    dot_general x8, matrix products, dot(): return jnp.dot(a, b, preferred_element_type=F32)  92.8 us
    dot_general x19, matrix products, dot_t(): lax.dot_general(a, b, (((0,), (0,)), ((), ())), preferred_element_type=F32)  79.4 us
    dot_general x7, matrix products, dot_nt(): lax.dot_general(a, b, (((1,), (1,)), ((), ())), preferred_element_type=F32)  71.3 us
    ppermute x8, waiting for transfers between devices, across(): return lax.ppermute(a, 'seq', [(i, i ^ which) for i in range(4)])  39.1 us
  transfers between devices with their start and end apart: 10, of which 3 were waited for; matrix products, arithmetic and copies ran while one was open for 18% of the time, Pallas kernels for 0%

profile of v4, /device:TPU:0, one launch (start us, length us, event | category | flops | bytes accessed | tf_op | source)
XLA Modules:
  0.0 1009.4 jit_solution(17761126145088317478)
XLA Ops:
  31.3 327.8 %forward.1 = (bf16[8,24,2048]{2,1,0:T(8,128)(2,1)}, bf16[8,8,24,2048]{3,2,1,0:T(8,128)(2,1)}, bf16[4,8,64,1536]{3,2,1,0:T(8,128)(2,1)}, bf16[8,64,2048]{2,1,0:T(...) custom-call(bf16[8,24,2048]{2,1,0:T(8,128)(2,1)} %copy.506.refs_0_, ...), custom_call_target="tpu_custom_call" | custom-call | tf_op jit(solution)/shard_map/forward/pallas_call | solution.py:435
  364.5 4.5 fusion.78
  372.0 15.8 %fusion.80 = f32[1536,1408]{1,0:T(8,128)} fusion(bf16[1536,2048]{1,0:T(8,128)(2,1)} %bitcast.277, bf16[2048,1408]{1,0:T(8,128)(2,1)} %get-tuple-element.54), kind=kOutput, calls=%fused_computation.254 | convolution fusion | flops 8858370048 | bytes 20709376 | tf_op jit(solution)/shard_map/dot_general | solution.py:25
  387.9 4.2 fusion.3
  392.1 15.8 %fusion.79 = f32[1536,1408]{1,0:T(8,128)} fusion(bf16[1536,2048]{1,0:T(8,128)(2,1)S(1)} %get-tuple-element.235, bf16[1408,2048]{1,0:T(8,128)(2,1)} %get-tuple-element.52), kind=kOutput, calls=%fused_computation.253 | convolution fusion | flops 8858370048 | bytes 20709376 | tf_op jit(solution)/shard_map/dot_general | solution.py:33
  407.9 19.4 %multiply_convert_fusion = (bf16[1536,1408]{1,0:T(8,128)(2,1)}, bf16[1536,1408]{1,0:T(8,128)(2,1)}, bf16[1536,1408]{1,0:T(8,128)(2,1)}) fusion(f32[1536,1408]{1,0:T(8,128)} %fusion.80, f32[1536,1408]{1,0:T(8,128)} %fusion.79, bf16[1536,2048]{1,0:T(8,128)(2,1)S(1)} %bitcast.281, bf16[2048,1408]{1,0:T(8,128)(2,1)} %get-tuple-element.53), kind=kOutput, calls=%fused_computation.28 | convolution fusion | flops 8892973056 | bytes 42336256 | tf_op jit(solution)/shard_map/dot_general | solution.py:25
  427.3 15.4 %convolution_convert_fusion = bf16[1536,2048]{1,0:T(8,128)(2,1)} fusion(bf16[1536,1408]{1,0:T(8,128)(2,1)} %get-tuple-element.228, bf16[1408,2048]{1,0:T(8,128)(2,1)} %get-tuple-element.52), kind=kOutput, calls=%fused_computation.32 | convolution fusion | flops 8861515776 | bytes 16384000 | tf_op jit(solution)/shard_map/dot_general | solution.py:25
  442.7 6.5 fusion.82
  449.2 6.5 fusion.81
  455.7 10.2 %multiply_convert_fusion.3 = (bf16[1536,704]{0,1:T(8,128)(2,1)S(1)}, bf16[1536,704]{0,1:T(8,128)(2,1)}, bf16[1536,704]{0,1:T(8,128)(2,1)}) fusion(f32[1536,704]{0,1:T(8,128)} %fusion.82, f32[1536,704]{0,1:T(8,128)} %fusion.81, bf16[1536,2048]{1,0:T(8,128)(2,1)S(1)} %bitcast.283, bf16[704,2048]{1,0:T(8,128)(2,1)S(1)} %copy-done.41), kind=kOutput, calls=%fused_computation.33 | convolution fusion | flops 4446486528 | bytes 24313856 | tf_op jit(solution)/shard_map/dot_general | solution.py:33
  466.0 12.7 %fusion.5 = (f32[1536]{0:T(1024)S(1)}, f32[1536]{0:T(1024)S(1)}, bf16[1536,2048]{1,0:T(8,128)(2,1)}) fusion(bf16[8,8,24,2048]{3,2,1,0:T(8,128)(2,1)S(1)} %bitcast.302, bf16[1536,2048]{1,0:T(8,128)(2,1)} %convolution_convert_fusion, f32[1536]{0:T(1024)S(1)} %divide_reduce_fusion, f32[1536]{0:T(1024)S(1)} %divide_select_fusion, ...), kind=kOutput, calls=%fused_computation.25 | convolution fusion | flops 4460639232 | bytes 23945216 | tf_op jit(solution)/shard_map/dot_general | solution.py:25
  478.8 4.3 fusion.34
  484.6 6.3 convolution_convert_fusion.4
  499.7 10.7 %fusion.84 = f32[1536,2048]{1,0:T(8,128)} fusion(bf16[1536,704]{0,1:T(8,128)(2,1)} %get-tuple-element.232, bf16[704,2048]{1,0:T(8,128)(2,1)} %get-tuple-element.57), kind=kOutput, calls=%fused_computation.258 | convolution fusion | flops 4429185024 | bytes 17629184 | tf_op jit(solution)/shard_map/dot_general | solution.py:25
  510.5 16.1 %fusion.83 = f32[1536,2048]{1,0:T(8,128)} fusion(bf16[1536,1408]{1,0:T(8,128)(2,1)} %get-tuple-element.229, bf16[2048,1408]{1,0:T(8,128)(2,1)} %get-tuple-element.54), kind=kOutput, calls=%fused_computation.257 | convolution fusion | flops 8858370048 | bytes 22675456 | tf_op jit(solution)/shard_map/dot_general | solution.py:33
  526.6 15.2 %add_convert_fusion.1 = bf16[1536,2048]{1,0:T(8,128)(2,1)} fusion(f32[1536,2048]{1,0:T(8,128)} %fusion.83, bf16[1536,1408]{1,0:T(8,128)(2,1)} %get-tuple-element.230, bf16[2048,1408]{1,0:T(8,128)(2,1)S(1)} %bitcast.371), kind=kOutput, calls=%fused_computation.27 | convolution fusion | flops 8864661504 | bytes 28966912 | tf_op jit(solution)/shard_map/dot_general | solution.py:33
  541.8 14.0 %add_convert_fusion = bf16[1536,2048]{1,0:T(8,128)(2,1)} fusion(f32[1536,2048]{1,0:T(8,128)} %fusion.84, bf16[1536,2048]{1,0:T(8,128)(2,1)} %add_convert_fusion.1, bf16[1536,704]{0,1:T(8,128)(2,1)} %get-tuple-element.233, bf16[704,2048]{1,0:T(8,128)(2,1)} %get-tuple-element.56), kind=kOutput, calls=%fused_computation.26 | convolution fusion | flops 4441767936 | bytes 30212096 | tf_op jit(solution)/shard_map/dot_general | solution.py:25
  555.9 11.8 %concatenate.47 = bf16[1536,2176]{1,0:T(8,128)(2,1)} concatenate(bf16[1536,2048]{1,0:T(8,128)(2,1)} %add_convert_fusion, bf16[1536,8]{1,0:T(8,128)(2,1)S(1)} %copy.524, bf16[1536,8]{1,0:T(8,128)(2,1)S(1)} %copy.525, bf16[1536,8]{1,0:T(8,128)(2,1)S(1)} %copy.526, bf16[1536,8]{1,0:T(8,128)(2,1)S(1)} %copy.527, bf16[1536,8]{1,0:T(8,128)(2,1)S(1)} %copy.528, ...), dimensions={1} | concatenate | bytes 13369344 | tf_op jit(solution)/shard_map/concatenate | solution.py:921
  567.8 6.4 convolution_convert_fusion.5
  588.5 4.3 fusion.31
  592.9 3.7 convolution_convert_fusion.12
  610.8 4.2 convolution_convert_fusion.6.refs_3_
  615.0 3.8 convolution_convert_fusion.7.refs_2_
  618.8 3.7 convolution_convert_fusion.8.refs_1_
  622.5 3.7 convolution_convert_fusion.9.refs_0_
  626.3 6.0 convolution_convert_fusion.1.refs_16_
  632.3 6.5 convolution_convert_fusion.2.refs_13_
  638.8 6.6 convolution_convert_fusion.3.refs_12_
  672.0 13.8 %collective-permute-done.3.refs_7_ = bf16[704,512]{1,0:T(8,128)(2,1)S(1)} collective-permute-done((bf16[704,512]{1,0:T(8,128)(2,1)S(1)}, bf16[704,512]{1,0:T(8,128)(2,1)S(1)}, u32[]{:S(2)}, u32[]{:S(2)}) %collective-permute-start.3) | collective-permute-done | bytes 720928 | tf_op jit(solution)/shard_map/ppermute | solution.py:58
  685.8 15.4 %collective-permute-done.1.refs_5_ = bf16[704,512]{1,0:T(8,128)(2,1)S(1)} collective-permute-done((bf16[704,512]{1,0:T(8,128)(2,1)S(1)}, bf16[704,512]{1,0:T(8,128)(2,1)S(1)}, u32[]{:S(2)}, u32[]{:S(2)}) %collective-permute-start.1) | collective-permute-done | bytes 720928 | tf_op jit(solution)/shard_map/ppermute | solution.py:58
  701.2 9.9 collective-permute-done.refs_4_
  711.1 253.6 %backward.1 = (f32[512,1408]{1,0:T(8,128)}, f32[512,1408]{1,0:T(8,128)}, f32[704,512]{1,0:T(8,128)}, f32[704,512]{1,0:T(8,128)}, f32[1408,512]{1,0:T(8,128)}, /*...) custom-call(bf16[512,1408]{1,0:T(8,128)(2,1)} %convolution_convert_f, ...), custom_call_target="tpu_custom_call" | custom-call | tf_op jit(solution)/shard_map/backward/pallas_call | solution.py:778
  (428 shorter events, 134.2 us)
Async XLA Ops:
  7.2 638.2 %reduce-scatter.3.cloned.1.call-start = ((), (), s32[]{:S(2)}) async-start(), calls=%async_computation.2 | async-start | bytes 7077888 | tf_op jit(solution)/shard_map/reduce_scatter | solution.py:910
  370.3 17.4 %copy-start.29 = (pred[8,8,2]{2,1,0:T(8,128)(4,1)}, pred[8,8,2]{2,1,0:T(8,128)(4,1)S(1)}, u32[]{:S(2)}) copy-start(pred[8,8,2]{2,1,0:T(8,128)(4,1)S(1)} %copy.510) | copy-start | bytes 388
  371.4 16.3 %copy-start.3 = (f32[128,12,4]{1,2,0:T(4,128)}, f32[128,12,4]{1,2,0:T(4,128)S(1)}, u32[]{:S(2)}) copy-start(f32[128,12,4]{1,2,0:T(4,128)S(1)} %gather_fusion.3) | copy-start | bytes 73732
  371.9 15.9 %slice-start.6 = ((s8[6291456]{0:T(1024)(128)(4,1)}), s8[4194304]{0:T(1024)(128)(4,1)S(1)}, s32[]{:S(2)}) async-start(s8[6291456]{0:T(1024)(128)(4,1)} %bitcast.299), calls=%async_computation.10 | async-start | bytes 8388608
  371.9 15.9 %slice-start.7 = ((s8[6291456]{0:T(1024)(128)(4,1)}), s8[2097152]{0:T(1024)(128)(4,1)S(1)}, s32[]{:S(2)}) async-start(s8[6291456]{0:T(1024)(128)(4,1)} %bitcast.299), calls=%async_computation.11 | async-start | bytes 4194304
  387.9 20.0 %slice-start = ((s8[6291456]{0:T(1024)(128)(4,1)}), s8[4194304]{0:T(1024)(128)(4,1)S(1)}, s32[]{:S(2)}) async-start(s8[6291456]{0:T(1024)(128)(4,1)} %bitcast.279), calls=%async_computation.4 | async-start | bytes 8388608
  392.1 15.8 %copy-start.6 = (bf16[1536,2048]{1,0:T(8,128)(2,1)}, bf16[1536,2048]{1,0:T(8,128)(2,1)S(1)}, u32[]{:S(2)}) copy-start(bf16[1536,2048]{1,0:T(8,128)(2,1)S(1)} %get-tuple-element.235) | copy-start | bytes 18874372
  392.1 15.8 %slice-start.1 = ((s8[6291456]{0:T(1024)(128)(4,1)}), s8[2097152]{0:T(1024)(128)(4,1)S(1)}, s32[]{:S(2)}) async-start(s8[6291456]{0:T(1024)(128)(4,1)} %bitcast.279), calls=%async_computation.5 | async-start | bytes 4194304
  427.3 15.4 %copy-start.42 = (bf16[704,2048]{1,0:T(8,128)(2,1)S(1)}, bf16[704,2048]{1,0:T(8,128)(2,1)}, u32[]{:S(2)}) copy-start(bf16[704,2048]{1,0:T(8,128)(2,1)} %get-tuple-element.57) | copy-start | bytes 8650756
  449.2 16.8 %slice-start.8 = ((s8[6291456]{0:T(1024)(128)(4,1)}), s8[4194304]{0:T(1024)(128)(4,1)S(1)}, s32[]{:S(2)}) async-start(s8[6291456]{0:T(1024)(128)(4,1)} %bitcast.301), calls=%async_computation.12 | async-start | bytes 8388608
  455.7 10.3 %slice-start.9 = ((s8[6291456]{0:T(1024)(128)(4,1)}), s8[2097152]{0:T(1024)(128)(4,1)S(1)}, s32[]{:S(2)}) async-start(s8[6291456]{0:T(1024)(128)(4,1)} %bitcast.301), calls=%async_computation.13 | async-start | bytes 4194304
  455.7 10.3 %copy-start.44 = (bf16[704,2048]{1,0:T(8,128)(2,1)S(1)}, bf16[704,2048]{1,0:T(8,128)(2,1)}, u32[]{:S(2)}) copy-start(bf16[704,2048]{1,0:T(8,128)(2,1)} %get-tuple-element.55) | copy-start | bytes 8650756
  465.9 12.8 %copy-start.55 = (bf16[1536,704]{0,1:T(8,128)(2,1)}, bf16[1536,704]{0,1:T(8,128)(2,1)S(1)}, u32[]{:S(2)}) copy-start(bf16[1536,704]{0,1:T(8,128)(2,1)S(1)} %get-tuple-element.231) | copy-start | bytes 6488068
  478.7 176.6 %reduce-scatter.5.cloned.1.call-start = ((), (), s32[]{:S(2)}) async-start(), calls=%async_computation.3 | async-start | bytes 7520256 | tf_op jit(solution)/shard_map/reduce_scatter | solution.py:922
  478.8 13.1 %slice-start.2 = ((s8[6291456]{0:T(1024)(128)(4,1)}), s8[4194304]{0:T(1024)(128)(4,1)S(1)}, s32[]{:S(2)}) async-start(s8[6291456]{0:T(1024)(128)(4,1)} %bitcast.284), calls=%async_computation.6 | async-start | bytes 8388608
  483.1 8.8 slice-start.3
  483.1 8.8 copy-start.53
  483.1 183.4 %collective-permute-start.7 = (bf16[704,512]{1,0:T(8,128)(2,1)}, bf16[704,512]{1,0:T(8,128)(2,1)}, u32[]{:S(2)}, u32[]{:S(2)}) collective-permute-start(bf16[704,512]{1,0:T(8,128)(2,1)} %fusion.34), channel_id=1, source_target_pairs={{0,16},{8,24},{16,0},{24,8},{1,17},{9,25},{17,1},{25,9},{2,18},{10... | collective-permute-start | bytes 2162696 | tf_op jit(solution)/shard_map/ppermute | solution.py:58
  490.9 220.2 %collective-permute-start.6 = (bf16[1408,512]{1,0:T(8,128)(2,1)}, bf16[1408,512]{1,0:T(8,128)(2,1)}, u32[]{:S(2)}, u32[]{:S(2)}) collective-permute-start(bf16[1408,512]{1,0:T(8,128)(2,1)} %convolution_convert_fusion.4), channel_id=1, source_target_pairs={{0,16},{8,24},{16,0},{24,8},{1,17},{9,25},{17,1},{25,9},{2,18},{10... | collective-permute-start | bytes 4325384 | tf_op jit(solution)/shard_map/ppermute | solution.py:58
  494.1 173.4 %collective-permute-start.5 = (bf16[704,512]{1,0:T(8,128)(2,1)}, bf16[704,512]{1,0:T(8,128)(2,1)}, u32[]{:S(2)}, u32[]{:S(2)}) collective-permute-start(bf16[704,512]{1,0:T(8,128)(2,1)} %convolution_convert_fusion.10), channel_id=1, source_target_pairs={{0,16},{8,24},{16,0},{24,8},{1,17},{9,25},{17,1},{25,9},{2,18},{10... | collective-permute-start | bytes 2162696 | tf_op jit(solution)/shard_map/ppermute | solution.py:58
  497.2 171.5 %collective-permute-start.4 = (bf16[704,512]{1,0:T(8,128)(2,1)}, bf16[704,512]{1,0:T(8,128)(2,1)}, u32[]{:S(2)}, u32[]{:S(2)}) collective-permute-start(bf16[704,512]{1,0:T(8,128)(2,1)} %convolution_convert_fusion.11), channel_id=1, source_target_pairs={{0,16},{8,24},{16,0},{24,8},{1,17},{9,25},{17,1},{25,9},{2,18},{10... | collective-permute-start | bytes 2162696 | tf_op jit(solution)/shard_map/ppermute | solution.py:58
  499.7 26.9 %slice-start.14 = ((s8[5767168]{0:T(1024)(128)(4,1)}), s8[4194304]{0:T(1024)(128)(4,1)S(1)}, s32[]{:S(2)}) async-start(s8[5767168]{0:T(1024)(128)(4,1)} %bitcast.370), calls=%async_computation.18 | async-start | bytes 8388608
  510.5 16.1 %slice-start.15 = ((s8[5767168]{0:T(1024)(128)(4,1)}), s8[1572864]{0:T(1024)(128)(4,1)S(1)}, s32[]{:S(2)}) async-start(s8[5767168]{0:T(1024)(128)(4,1)} %bitcast.370), calls=%async_computation.19 | async-start | bytes 3145728
  567.8 9.3 copy-start.10
  574.2 136.9 %collective-permute-start.2 = (bf16[1408,512]{1,0:T(8,128)(2,1)}, bf16[1408,512]{1,0:T(8,128)(2,1)}, u32[]{:S(2)}, u32[]{:S(2)}) collective-permute-start(bf16[1408,512]{1,0:T(8,128)(2,1)} %convolution_convert_fusion.5), channel_id=1, source_target_pairs={{0,8},{8,0},{16,24},{24,16},{1,9},{9,1},{17,25},{25,17},{2,10},{10... | collective-permute-start | bytes 4325384 | tf_op jit(solution)/shard_map/ppermute | solution.py:58
  603.6 11.4 %slice-start.16 = ((s8[4325376]{0:T(1024)(128)(4,1)}), s8[4194304]{0:T(1024)(128)(4,1)S(1)}, s32[]{:S(2)}) async-start(s8[4325376]{0:T(1024)(128)(4,1)} %bitcast.372), calls=%async_computation.20 | async-start | bytes 8388608
  666.7 19.1 %collective-permute-start.3 = (bf16[704,512]{1,0:T(8,128)(2,1)S(1)}, bf16[704,512]{1,0:T(8,128)(2,1)S(1)}, u32[]{:S(2)}, u32[]{:S(2)}) collective-permute-start(bf16[704,512]{1,0:T(8,128)(2,1)S(1)} %copy-done.47), channel_id=1, source_target_pairs={{0,8},{8,0},{16,24},{24,16},{1,9},{9,1},{17,25},{25,17},{2,10},{10... | collective-permute-start | bytes 2162696 | tf_op jit(solution)/shard_map/ppermute | solution.py:58
  667.5 33.7 %collective-permute-start.1 = (bf16[704,512]{1,0:T(8,128)(2,1)S(1)}, bf16[704,512]{1,0:T(8,128)(2,1)S(1)}, u32[]{:S(2)}, u32[]{:S(2)}) collective-permute-start(bf16[704,512]{1,0:T(8,128)(2,1)S(1)} %copy-done.46), channel_id=1, source_target_pairs={{0,8},{8,0},{16,24},{24,16},{1,9},{9,1},{17,25},{25,17},{2,10},{10... | collective-permute-start | bytes 2162696 | tf_op jit(solution)/shard_map/ppermute | solution.py:58
  668.7 42.3 %collective-permute-start = (bf16[704,512]{1,0:T(8,128)(2,1)S(1)}, bf16[704,512]{1,0:T(8,128)(2,1)}, u32[]{:S(2)}, u32[]{:S(2)}) collective-permute-start(bf16[704,512]{1,0:T(8,128)(2,1)S(1)} %copy-done.45), channel_id=1, source_target_pairs={{0,8},{8,0},{16,24},{24,16},{1,9},{9,1},{17,25},{25,17},{2,10},{10... | collective-permute-start | bytes 2162696 | tf_op jit(solution)/shard_map/ppermute | solution.py:58
  685.8 25.3 %copy-start.22 = (bf16[704,512]{1,0:T(8,128)(2,1)}, bf16[704,512]{1,0:T(8,128)(2,1)S(1)}, u32[]{:S(2)}) copy-start(bf16[704,512]{1,0:T(8,128)(2,1)S(1)} %collective-permute-done.3.refs_7_) | copy-start | bytes 2162692
  701.2 9.9 copy-start.23
  982.3 8.4 copy-start.14
  (57 other events, 242.8 us)
Sparse Core Ops, SparseCore 0:
  478.9 68.0 reduce-scatter.2
  567.9 72.0 reduce-scatter.4

commit v5 on v4

--- a/solution.py
+++ b/solution.py
@@ -451,15 +451,119 @@
     )(tok, cot, wq, wo, small, *shards_in, *tables)
 
 
+def experts_kernel(N, E, *refs):
+    x, g, picked, lead, *refs = refs
+    weights, refs = refs[:6], refs[6:]
+    y, dx, geo, gso, grad_gate, grad_up, grad_sgate, grad_sup, act, sact, *refs = refs
+    held, sems = refs[:6], refs[6]
+    eg, eu, sg, su, ed, sd = held
+    f = lax.axis_index("fsdp")
+    D = x.shape[1]
+    copies = [pltpu.make_async_copy(a, b, sems.at[i]) for i, (a, b) in enumerate(zip(weights, held))]
+    opening = pl.program_id(0) == 0
+
+    @pl.when(opening)
+    def _():
+        for i in (0, 1, 4, 2, 3, 5):
+            copies[i].start()
+
+    def need(i):
+        @pl.when(opening)
+        def _():
+            copies[i].wait()
+
+    rows = x[...]
+    logits = dot(rows, lead[...])
+    lane = lax.broadcasted_iota(jnp.int32, logits.shape, 1)
+    scores = jnp.where(lane < E, logits, MASKED)
+    shifted = jnp.exp(scores - jnp.max(scores, axis=-1, keepdims=True))
+    share = jnp.sum(jnp.where(lane == f, shifted, 0.0), axis=-1, keepdims=True)
+    share = share / jnp.sum(jnp.where(lane < E, shifted, 0.0), axis=-1, keepdims=True)
+    gate_f = jnp.where(picked[...] > 0.5, share, 0.0)
+    sigma = jax.nn.sigmoid(jnp.sum(jnp.where(lane == E, logits, 0.0), axis=-1, keepdims=True))
+    geo[...] = (gate_f * g[...].astype(F32)).astype(BF16)
+    gso[...] = (sigma * g[...].astype(F32)).astype(BF16)
+
+    need(0)
+    gate = dot(rows, eg[...])
+    need(1)
+    up = dot(rows, eu[...])
+    sig = jax.nn.sigmoid(gate)
+    act[...] = (gate * sig * up).astype(BF16)
+    need(4)
+    grad_act = dot_nt(geo[...], ed[...])
+    grad_gate[...] = (grad_act * up * sig * (1.0 + gate * (1.0 - sig))).astype(BF16)
+    grad_up[...] = (grad_act * gate * sig).astype(BF16)
+    out = dot(act[...], ed[...]).astype(BF16).astype(F32)
+    note_e = jnp.sum(out * g[...].astype(F32), axis=-1, keepdims=True)
+    out = gate_f * out
+    back = (dot_nt(grad_gate[...], eg[...]) + dot_nt(grad_up[...], eu[...])).astype(BF16)
+
+    need(2)
+    gate = dot_nt(rows, sg[...])
+    need(3)
+    up = dot_nt(rows, su[...])
+    sig = jax.nn.sigmoid(gate)
+    sact[...] = (gate * sig * up).astype(BF16)
+    need(5)
+    grad_act = dot_nt(gso[...], sd[...])
+    grad_sgate[...] = (grad_act * up * sig * (1.0 + gate * (1.0 - sig))).astype(BF16)
+    grad_sup[...] = (grad_act * gate * sig).astype(BF16)
+    out_s = dot(sact[...], sd[...])
+    note_s = jnp.sum(out_s * g[...].astype(F32), axis=-1, keepdims=True)
+    y[...] = (out + sigma * out_s).astype(BF16)
+    back = back.astype(F32) + dot(grad_sgate[...], sg[...]) + dot(grad_sup[...], su[...])
+    dx[:, :D] = back.astype(BF16)
+    lane = lax.broadcasted_iota(jnp.int32, (rows.shape[0], dx.shape[1] - D), 1)
+    notes = jnp.zeros(lane.shape, F32)
+    i = 0
+    for value in (note_e, note_s):
+        for _ in range(3):
+            part = value.astype(BF16).astype(F32)
+            notes = jnp.where(lane == i * N + f, part, notes)
+            value = value - part
+            i += 1
+    dx[:, D:] = notes.astype(BF16)
+
+
+def experts(N, E, x, g, picked, lead, weights):
+    rows, D = x.shape
+    tile = 256
+    FE, FS = weights[0].shape[1], weights[2].shape[0]
+    wide = D + 6 * N + -(6 * N) % 128
+    columns = (D, wide, D, D, FE, FE, FS, FS, FE, FS)
+    once = dict(pipeline_mode=pl.Buffered(1))
+    return pl.pallas_call(
+        functools.partial(experts_kernel, N, E),
+        grid=(rows // tile,),
+        out_shape=[jax.ShapeDtypeStruct((rows, c), BF16) for c in columns],
+        in_specs=[pl.BlockSpec((tile, c), lambda i: (i, 0)) for c in (D, D, 1)]
+        + [pl.BlockSpec(lead.shape, lambda i: (0, 0), **once)] + [pl.BlockSpec(memory_space=pl.ANY)] * 6,
+        out_specs=[pl.BlockSpec((tile, c), lambda i: (i, 0)) for c in columns],
+        scratch_shapes=[pltpu.VMEM(w.shape, BF16) for w in weights] + [pltpu.SemaphoreType.DMA((6,))],
+        compiler_params=pltpu.CompilerParams(
+            dimension_semantics=("arbitrary",), vmem_limit_bytes=VMEM_LIMIT
+        ),
+        cost_estimate=pl.CostEstimate(
+            flops=12 * rows * D * (FE + FS), bytes_accessed=40 * rows * D, transcendentals=rows * (FE + FS)
+        ),
+        name="experts",
+    )(x, g, picked, lead, *weights)
+
+
 def backward_kernel(S, N, sizes, *refs):
     D, own, heads = sizes
-    to_x, to_y, from_x, from_y, keep, refs = refs[:2], refs[2:4], refs[4:8], refs[8:12], refs[12:18], refs[18:]
+    to_x, to_y, stacked_x, stacked_y, keep, refs = refs[:2], refs[2:4], refs[4], refs[5], refs[6:12], refs[12:]
+    from_x, from_y, line = [], [], 0
+    for ref in keep[2:]:
+        from_x.append(stacked_x.at[pl.ds(line, ref.shape[0])])
+        from_y.append(stacked_y.at[pl.ds(line, ref.shape[0])])
+        line += ref.shape[0]
     w_in, w_back, normed_all, qkv, mixed, gh, unit, inverse, gain_row, ready, ctx, cos, sin, first, place, place_row, *refs = refs
-    grads, refs = refs[:6], refs[6:]
     mixed_out, gx_out, gin_out, gout_out, small_out, bias_out, vec_far, gin_buf, gout_buf, gin_pair, gout_pair, *refs = refs
     from_x, from_y, refs = (*refs[:2], *from_x), (*refs[2:4], *from_y), refs[4:]
     then_y, then_x, pair_y, pair_x, refs = refs[:6], refs[6:12], refs[12:18], refs[18:24], refs[24:]
-    loads, sums, refs = refs[:3], refs[3:6], refs[6:]
+    loads, refs = refs[:3], refs[3:]
     w_v, wb_v, ga_v, na_v, qkv_v, gc_v, gk_v, gv_v, part_send, part_recv, gn_v, gi_v, go_v, *refs = refs
     in_mine, in_pair, in_stage, in_far, out_mine, out_pair, out_stage, out_far, *refs = refs
     vec_v, vec_tmp, vec_sum, vec_near, mixed_v, gx_v, *refs = refs
@@ -512,16 +616,6 @@
             copy.start()
             copy.wait()
             then_copy(i, way).start()
-
-    def third(i):
-        buf, total = loads[kind[i]], sums[kind[i]]
-        for way, (arrived, last) in enumerate(((from_x[i], then_y[i]), (from_y[i], then_x[i]))):
-            then_copy(i, way).wait_recv()
-            fetch(i, (part(keep[i], i, way), part(arrived, i, 0), last))
-            total[...] = buf[0].astype(F32) + buf[1].astype(F32) + buf[2].astype(F32)
-            copy = pltpu.make_async_copy(total, part(grads[i], i, way), load_sem.at[0])
-            copy.start()
-            copy.wait()
 
     def reducer(block, pair, mine, other, stage, far, k):
         def pair_copy(q):
@@ -727,10 +821,9 @@
         copy.start()
     done.append(pltpu.make_async_copy(in_stage.at[0, s], gin_out.at[s], local_sem.at[1]))
     done[2].start()
-    for i in (4, 5, 2, 3, 0, 1):
-        third(i)
     for i in range(6):
         for way in range(2):
+            then_copy(i, way).wait_recv()
             if i < 2:
                 give_copy(i, way).wait_send()
             then_copy(i, way).wait_send()
@@ -765,7 +858,7 @@
     kinds = [blocks[i] for i in (0, 2, 4)]
     in_block, out_block = (S, own, 3 * width), (own, D)
     vec = (D // 128 + 16 + ready.shape[0], 128)
-    out = [shape(w, F32) for w in wholes] + [
+    out = [
         shape(mixed.shape, BF16), shape(mixed.shape, BF16), shape(in_block, BF16), shape(out_block, F32), shape(vec, F32),
         shape((S, 16, 128), F32),
         shape((N - 1,) + vec, F32),
@@ -778,9 +871,9 @@
     result = pl.pallas_call(
         functools.partial(backward_kernel, S, N, (D, own, heads)),
         out_shape=out,
-        in_specs=[anywhere] * 23 + [in_vmem] * 11,
-        out_specs=[anywhere] * 9 + [in_vmem] * 3 + [anywhere] * (len(out) - 12),
-        scratch_shapes=[vmem((3,) + k, BF16) for k in kinds] + [vmem(k, F32) for k in kinds]
+        in_specs=[anywhere] * 17 + [in_vmem] * 11,
+        out_specs=[anywhere] * 3 + [in_vmem] * 3 + [anywhere] * (len(out) - 6),
+        scratch_shapes=[vmem((2,) + k, BF16) for k in kinds]
         + [
             vmem(w_in.shape, BF16), vmem(w_back.shape, BF16), vmem((S, L, D), BF16), vmem((S, L, D), BF16),
             vmem(qkv.shape, BF16), vmem((heads, R, HD), BF16), vmem((R, HD), F32), vmem((R, HD), F32),
@@ -797,8 +890,24 @@
         ],
         compiler_params=pltpu.CompilerParams(collective_id=1, has_side_effects=True, vmem_limit_bytes=VMEM_LIMIT),
         name="backward",
-    )(*to_x, *to_y, *from_x, *from_y, *keep, w_in, w_back, normed_all, qkv, mixed, gh, unit, inverse, gain_row, ready, ctx, *tables)
-    return result[:12]
+    )(*to_x, *to_y, from_x, from_y, *keep, w_in, w_back, normed_all, qkv, mixed, gh, unit, inverse, gain_row, ready, ctx, *tables)
+    first_x, first_y, then_y, then_x = result[11:13], result[13:15], result[15:21], result[21:27]
+    grads, line = [], 0
+    for i, block in enumerate(keep):
+        if i < 2:
+            sources = (first_x[i][:eighth], first_y[i][:eighth])
+            halves = (block[:eighth], block[eighth : 2 * eighth])
+        else:
+            lines = slice(line, line + block.shape[0])
+            sources = (from_x[lines, :eighth], from_y[lines, :eighth])
+            halves = (block[:, :eighth], block[:, eighth : 2 * eighth])
+            line += block.shape[0]
+        sums = [
+            a.astype(F32) + b.astype(F32) + c.astype(F32)
+            for a, b, c in zip(halves, sources, (then_y[i], then_x[i]))
+        ]
+        grads.append(jnp.concatenate(sums, axis=min(i // 2, 1)))
+    return grads, result[:6]
 
 
 def shards(
@@ -873,7 +982,6 @@
     gain_1, gain_2, shared_w = vector(0), vector(1), vector(4).astype(BF16)
     router_w = small[:, :, r_line:i_line].swapaxes(0, 1).reshape(S * N, -1)[:, : own * E].reshape(D, E).astype(BF16)
     all_ids = small[:, :, i_line:].reshape(N, S, -1)[:, :, : MB * T * TOP]
-    eg, eu, sg, su, ed, sd = fulls
     x0 = x_rows.reshape(L, D).astype(F32)
     cot = arrange(lax.dynamic_index_in_dim(g_all, f, 0, keepdims=False).reshape(L, D), inverse_order)
     g_rows = g_all.reshape(rows, D)
@@ -891,35 +999,11 @@
 
     lead = jnp.concatenate([router_w, shared_w[:, None]], axis=1)
     lead_order = jnp.take(lead.reshape(8, D // 8, E + 1), order, axis=0).reshape(D, E + 1)
-    logits = dot(x, lead_order)
-    shifted = jnp.exp(logits[:, :E] - jnp.max(logits[:, :E], axis=-1, keepdims=True))
-    router_f = jnp.sum(jnp.where(jnp.arange(E) == f, shifted, 0.0), axis=1) / jnp.sum(shifted, axis=1)
-    gate_f = jnp.where(jnp.any(chosen == f, axis=1), router_f, 0.0)[:, None]
-    sigma_rows = jax.nn.sigmoid(logits[:, E])[:, None]
-    g32 = g_rows.astype(F32)
-    geo = (gate_f * g32).astype(BF16)
-    gso = (sigma_rows * g32).astype(BF16)
-
-    gate, up = dot(x, eg), dot(x, eu)
-    act = (jax.nn.silu(gate) * up).astype(BF16)
-    out_e = dot(act, ed).astype(BF16).astype(F32)
-    sgate, sup = dot_nt(x, sg), dot_nt(x, su)
-    sact = (jax.nn.silu(sgate) * sup).astype(BF16)
-    out_s = dot(sact, sd)
-    y = (gate_f * out_e + sigma_rows * out_s).astype(BF16)
-    y = lax.psum_scatter(y, "fsdp", scatter_dimension=0, tiled=True)
-    gg = jnp.sum(g32 * out_e, axis=1)
-    gs = jnp.sum(g32 * out_s, axis=1)
-
-    grad_gate, grad_up = swiglu_back(dot_nt(geo, ed), gate, up)
-    grad_sgate, grad_sup = swiglu_back(dot_nt(gso, sd), sgate, sup)
-    dx_e = (dot_nt(grad_gate, eg) + dot_nt(grad_up, eu)).astype(BF16).astype(F32)
-    dx = dx_e + dot(grad_sgate, sg) + dot(grad_sup, su)
-    mine = (jnp.arange(N) == f).astype(F32)
-    notes = [part[:, None] * mine for value in (gg, gs) for part in split3(value)]
-    note_pad = -(6 * N) % 128
-    payload = jnp.concatenate([dx] + notes + [jnp.zeros((rows, note_pad), F32)], axis=1).astype(BF16)
-    dx = lax.psum_scatter(payload, "fsdp", scatter_dimension=0, tiled=True).astype(F32)
+    picked_rows = jnp.any(chosen == f, axis=1, keepdims=True).astype(F32)
+    y, dx, geo, gso, grad_gate, grad_up, grad_sgate, grad_sup, act, sact = experts(
+        N, E, x, g_rows, picked_rows, jnp.pad(lead_order, ((0, 0), (0, 127 - E))), fulls
+    )
+    dx = lax.psum_scatter(dx, "fsdp", scatter_dimension=0, tiled=True)
 
     half = D // 8
     cuts = (slice(4 * half, 6 * half), slice(6 * half, 8 * half), slice(0, 4 * half))
@@ -933,10 +1017,14 @@
     def by_rows(cut):
         return dot_t(x[:, cut], grad_gate).astype(BF16), dot_t(x[:, cut], grad_up).astype(BF16)
 
-    from_x = [across(u, 1) for u in by_columns(cuts[0])]
-    from_y = [across(u, 2) for u in by_columns(cuts[1])]
+    by_x, by_y = jnp.concatenate(by_columns(cuts[0])), jnp.concatenate(by_columns(cuts[1]))
+    x, y, by_x, by_y = lax.optimization_barrier((x, y, by_x, by_y))
+    y = lax.psum_scatter(y, "fsdp", scatter_dimension=0, tiled=True)
+    from_x, from_y = across(by_x, 1), across(by_y, 2)
     to_x, to_y = by_rows(cuts[0]), by_rows(cuts[1])
     keep = by_rows(cuts[2]) + by_columns(cuts[2])
+    dx, from_x, from_y, to_x, to_y, keep = lax.optimization_barrier((dx, from_x, from_y, to_x, to_y, keep))
+    dx = dx.astype(F32)
 
     mixed = (hidden + arrange(y, inverse_order).astype(F32)).astype(BF16)
     base = D
@@ -959,7 +1047,7 @@
     grad_hidden = cot.astype(F32) + from_norm
 
     ready = jnp.concatenate([g_gain_2, g_shared, g_router.reshape(-1)]).reshape(-1, 128)
-    *expert_grads, mixed, grad_x, g_in, g_out, small, g_bias = backward(
+    expert_grads, (mixed, grad_x, g_in, g_out, small, g_bias) = backward(
         S, N, to_x, to_y, from_x, from_y, keep, w_in, w_back, normed_all, qkv, mixed.reshape(N, MB * piece, D), grad_hidden, unit_1,
         inverse_1, gain_1[None], ready, context, tables,
     )

time: 1020 us -> 967 us (0.948)
  matrix products: 243 us -> 77 us
  Pallas kernels: 581 us -> 689 us
  other arithmetic: 25.2 us -> 42.2 us
  waiting for transfers between devices: 39.1 us -> 50.6 us
  local copies, waits for them, and re-layouts: 95.2 us -> 84.3 us
    pallas_call x0 -> x1, Pallas kernels: none -> 125 us  [experts(): pl.pallas_call(functools.partial(experts_kernel, N, E), grid=(rows // til...]
    dot_general x8 -> x1, matrix products: 92.8 us -> 1.15 us  [dot(): return jnp.dot(a, b, preferred_element_type=F32)]
    dot_general x7 -> x1, matrix products: 71.3 us -> 0.9 us  [dot_nt(): lax.dot_general(a, b, (((1,), (1,)), ((), ())), preferred_element_type=F32)]
    reduce_scatter x1, waiting for transfers between devices: 0.01 us -> 50.3 us  [shards(): dx = lax.psum_scatter(dx, 'fsdp', scatter_dimension=0, tiled=True)]
    ppermute x8 -> x2, waiting for transfers between devices: 39.1 us -> 0.01 us  [across(): return lax.ppermute(a, 'seq', [(i, i ^ which) for i in range(4)])]
    pallas_call x1, Pallas kernels: 254 us -> 237 us  [backward(): pl.pallas_call(functools.partial(backward_kernel, S, N, (D, own, heads)),...]
    concatenate x1 -> x0, local copies, waits for them, and re-layouts: 11.8 us -> none  [shards(): jnp.concatenate([dx] + notes + [jnp.zeros((rows, note_pad), F32)], axis=1)]
  transfers between devices with their start and end apart: 10 -> 4, of which waited for: 3 -> 1; matrix products, arithmetic and copies ran while one was open for 18% -> 9% of each run, Pallas kernels for 0% -> 0%
where the time goes in v5:
time: 967 us; the launch traced here: 962 us
  Pallas kernels  689 us (71%)
  local copies, waits for them, and re-layouts  84.3 us (9%)
  matrix products  77 us (8%)
  waiting for transfers between devices  50.6 us (5%)
  other arithmetic  42.2 us (4%)
  between operations  15.8 us (2%)
    pallas_call x1, Pallas kernels, forward(): pl.pallas_call(functools.partial(forward_kernel, S, N, (MB, pr // MB, D,...  328 us
    pallas_call x1, Pallas kernels, backward(): pl.pallas_call(functools.partial(backward_kernel, S, N, (D, own, heads)),...  237 us
    pallas_call x1, Pallas kernels, experts(): pl.pallas_call(functools.partial(experts_kernel, N, E), grid=(rows // til...  125 us
    dot_general x19, matrix products, dot_t(): lax.dot_general(a, b, (((0,), (0,)), ((), ())), preferred_element_type=F32)  74.9 us
    reduce_scatter x1, waiting for transfers between devices, shards(): dx = lax.psum_scatter(dx, 'fsdp', scatter_dimension=0, tiled=True)  50.3 us
  transfers between devices with their start and end apart: 4, of which 1 were waited for; matrix products, arithmetic and copies ran while one was open for 9% of the time, Pallas kernels for 0%

profile of v5, /device:TPU:0, one launch (start us, length us, event | category | flops | bytes accessed | tf_op | source)
XLA Modules:
  0.0 962.0 jit_solution(11581877157660360597)
XLA Ops:
  26.8 1.8 reshape.836.refs_2_
  31.3 327.9 %forward.1 = (bf16[8,24,2048]{2,1,0:T(8,128)(2,1)}, bf16[8,8,24,2048]{3,2,1,0:T(8,128)(2,1)}, bf16[4,8,64,1536]{3,2,1,0:T(8,128)(2,1)}, bf16[8,64,2048]{2,1,0:T(...) custom-call(bf16[8,24,2048]{2,1,0:T(8,128)(2,1)} %copy.454.refs_0_, ...), custom_call_target="tpu_custom_call" | custom-call | tf_op jit(solution)/shard_map/forward/pallas_call | solution.py:435
  369.9 124.7 %experts.1 = (bf16[1536,2048]{1,0:T(8,128)(2,1)}, bf16[1536,2176]{1,0:T(8,128)(2,1)}, bf16[1536,2048]{1,0:T(8,128)(2,1)}, bf16[1536,2048]{1,0:T(8,128)(2,1)}, bf...) custom-call(bf16[1536,2048]{1,0:T(8,128)(2,1)} %bitcast.291, ...), custom_call_target="tpu_custom_call" | custom-call | flops 79725330432 | bytes 125829120 | tf_op jit(solution)/shard_map/experts/pallas_call | solution.py:536
  494.6 3.6 fusion.43
  498.3 2.9 fusion.37
  504.4 2.5 convolution_convert_fusion.7
  506.9 2.5 convolution_convert_fusion.8
  512.0 2.0 pad_maximum_fusion.1
  514.0 1.9 pad_maximum_fusion
  532.4 5.7 fusion.16.refs_11_
  538.2 3.7 fusion.13.refs_9_
  541.8 3.6 fusion.10.refs_8_
  545.4 4.0 convolution_convert_fusion.3.refs_3_
  549.4 3.8 convolution_convert_fusion.5.refs_1_
  553.2 3.8 convolution_convert_fusion.4.refs_2_
  557.0 3.8 convolution_convert_fusion.6.refs_0_
  569.8 9.6 convolution_convert_fusion.refs_10_
  579.3 9.3 convolution_convert_fusion.1.refs_7_
  588.7 9.6 convolution_convert_fusion.2.refs_6_
  598.3 2.1 copy.543
  600.3 2.6 gather_fusion.8
  608.2 50.3 %reduce-scatter.3.cloned.1.call-done = bf16[192,2176]{1,0:T(8,128)(2,1)} async-done(((bf16[1536,2176]{1,0:T(8,128)(2,1)}), bf16[192,2176]{1,0:T(8,128)(2,1)}) %reduce-scatter.3.cloned.1.call-update) | async-done | bytes 835600 | tf_op jit(solution)/shard_map/reduce_scatter | solution.py:1006
  667.2 2.1 gather_fusion.2
  672.2 1.9 multiply_add_fusion
  674.1 236.9 %backward.1 = (bf16[8,24,2048]{2,1,0:T(8,128)(2,1)}, bf16[8,24,2048]{2,1,0:T(8,128)(2,1)}, bf16[4,64,1536]{2,1,0:T(8,128)(2,1)}, f32[64,2048]{1,0:T(8,128)}, f32...) custom-call(bf16[512,1408]{1,0:T(8,128)(2,1)} %convolution_convert_f, ...), custom_call_target="tpu_custom_call" | custom-call | tf_op jit(solution)/shard_map/backward/pallas_call | solution.py:871
  922.9 2.2 copy.499
  925.1 3.6 reshape.863
  931.3 3.1 convert_add_fusion.6
  939.0 2.0 convert_add_fusion.1
  941.0 1.9 maximum_bitcast_fusion.2
  945.1 1.8 maximum_bitcast_fusion.1
  949.4 1.8 maximum_bitcast_fusion
  (365 shorter events, 107.7 us)
Async XLA Ops:
  7.2 591.1 %reduce-scatter.5.cloned.1.call-start = ((), (), s32[]{:S(2)}) async-start(), calls=%async_computation.3 | async-start | bytes 7077888 | tf_op jit(solution)/shard_map/reduce_scatter | solution.py:1022
  21.4 4.4 copy-start.19
  494.6 3.6 copy-start.44
  494.6 6.5 slice-start
  498.2 5.6 slice-start.12
  504.4 5.0 slice-start.4
  515.9 142.6 %reduce-scatter.3.cloned.1.call-start = ((), (), s32[]{:S(2)}) async-start(), calls=%async_computation.2 | async-start | bytes 7520256 | tf_op jit(solution)/shard_map/reduce_scatter | solution.py:1006
  516.7 10.1 %copy-start.13 = (bf16[8,24,2048]{2,1,0:T(8,128)(2,1)S(1)}, bf16[8,24,2048]{2,1,0:T(8,128)(2,1)}, u32[]{:S(2)}) copy-start(bf16[8,24,2048]{2,1,0:T(8,128)(2,1)} %get-tuple-element.128) | copy-start | bytes 2359300
  516.7 12.8 %copy-start.2 = (f32[192,2048]{1,0:T(8,128)S(1)}, f32[192,2048]{1,0:T(8,128)}, u32[]{:S(2)}) copy-start(f32[192,2048]{1,0:T(8,128)} %get-tuple-element.124) | copy-start | bytes 4718596
  516.7 91.5 %collective-permute-start = (bf16[3520,512]{1,0:T(8,128)(2,1)}, bf16[3520,512]{1,0:T(8,128)(2,1)}, u32[]{:S(2)}, u32[]{:S(2)}) collective-permute-start(bf16[3520,512]{1,0:T(8,128)(2,1)} %pad_maximum_fusion), channel_id=1, source_target_pairs={{0,8},{8,0},{16,24},{24,16},{1,9},{9,1},{17,25},{25,17},{2,10},{10... | collective-permute-start | bytes 10813448 | tf_op jit(solution)/shard_map/ppermute | solution.py:58
  518.2 90.0 %collective-permute-start.1 = (bf16[3520,512]{1,0:T(8,128)(2,1)}, bf16[3520,512]{1,0:T(8,128)(2,1)}, u32[]{:S(2)}, u32[]{:S(2)}) collective-permute-start(bf16[3520,512]{1,0:T(8,128)(2,1)} %pad_maximum_fusion.1), channel_id=1, source_target_pairs={{0,16},{8,24},{16,0},{24,8},{1,17},{9,25},{17,1},{25,9},{2,18},{10... | collective-permute-start | bytes 10813448 | tf_op jit(solution)/shard_map/ppermute | solution.py:58
  527.1 4.0 copy-start.14
  529.5 8.7 slice-start.2
  532.4 5.7 slice-start.3
  532.4 5.7 copy-start.47
  538.1 3.7 copy-start.45
  538.2 7.3 slice-start.10
  541.8 3.6 slice-start.11
  545.4 7.7 slice-start.8
  549.4 3.8 slice-start.9
  564.4 4.6 copy-start.34
  564.4 4.7 copy-start.33
  662.4 3.5 copy-start.7
  911.0 3.5 copy-start.20
  925.1 4.4 copy-start.36
  925.1 6.2 copy-start.10
  925.1 6.2 copy-start.11
  939.0 3.9 copy-start.32
  941.0 3.7 copy-start.31
  945.1 3.3 copy-start.23
  945.1 3.8 copy-start.29
  951.2 3.7 copy-start.1
  (36 other events, 85.8 us)
Sparse Core Ops, SparseCore 0:
  516.0 68.1 reduce-scatter.4
  586.6 71.8 reduce-scatter.2

commit v6 on v5

--- a/solution.py
+++ b/solution.py
@@ -451,20 +451,13 @@
     )(tok, cot, wq, wo, small, *shards_in, *tables)
 
 
-def experts_kernel(N, E, *refs):
-    x, g, picked, lead, *refs = refs
-    weights, refs = refs[:6], refs[6:]
-    y, dx, geo, gso, grad_gate, grad_up, grad_sgate, grad_sup, act, sact, *refs = refs
-    held, sems = refs[:6], refs[6]
-    eg, eu, sg, su, ed, sd = held
-    f = lax.axis_index("fsdp")
-    D = x.shape[1]
+def hold(weights, held, sems, order):
     copies = [pltpu.make_async_copy(a, b, sems.at[i]) for i, (a, b) in enumerate(zip(weights, held))]
     opening = pl.program_id(0) == 0
 
     @pl.when(opening)
     def _():
-        for i in (0, 1, 4, 2, 3, 5):
+        for i in order:
             copies[i].start()
 
     def need(i):
@@ -472,6 +465,16 @@
         def _():
             copies[i].wait()
 
+    return need
+
+
+def experts_forward_kernel(N, E, *refs):
+    x, g, picked, lead, *refs = refs
+    weights, refs = refs[:6], refs[6:]
+    y, notes, geo, gso, gate_o, up_o, sgate_o, sup_o, act, sact, *refs = refs
+    eg, eu, sg, su, ed, sd = refs[:6]
+    need = hold(weights, refs[:6], refs[6], (0, 1, 4, 2, 3, 5))
+    f = lax.axis_index("fsdp")
     rows = x[...]
     logits = dot(rows, lead[...])
     lane = lax.broadcasted_iota(jnp.int32, logits.shape, 1)
@@ -483,72 +486,101 @@
     sigma = jax.nn.sigmoid(jnp.sum(jnp.where(lane == E, logits, 0.0), axis=-1, keepdims=True))
     geo[...] = (gate_f * g[...].astype(F32)).astype(BF16)
     gso[...] = (sigma * g[...].astype(F32)).astype(BF16)
-
     need(0)
     gate = dot(rows, eg[...])
+    gate_o[...] = gate
     need(1)
     up = dot(rows, eu[...])
-    sig = jax.nn.sigmoid(gate)
-    act[...] = (gate * sig * up).astype(BF16)
+    up_o[...] = up
+    act[...] = (gate * jax.nn.sigmoid(gate) * up).astype(BF16)
     need(4)
-    grad_act = dot_nt(geo[...], ed[...])
-    grad_gate[...] = (grad_act * up * sig * (1.0 + gate * (1.0 - sig))).astype(BF16)
-    grad_up[...] = (grad_act * gate * sig).astype(BF16)
     out = dot(act[...], ed[...]).astype(BF16).astype(F32)
     note_e = jnp.sum(out * g[...].astype(F32), axis=-1, keepdims=True)
     out = gate_f * out
-    back = (dot_nt(grad_gate[...], eg[...]) + dot_nt(grad_up[...], eu[...])).astype(BF16)
-
     need(2)
     gate = dot_nt(rows, sg[...])
+    sgate_o[...] = gate
     need(3)
     up = dot_nt(rows, su[...])
-    sig = jax.nn.sigmoid(gate)
-    sact[...] = (gate * sig * up).astype(BF16)
+    sup_o[...] = up
+    sact[...] = (gate * jax.nn.sigmoid(gate) * up).astype(BF16)
     need(5)
-    grad_act = dot_nt(gso[...], sd[...])
-    grad_sgate[...] = (grad_act * up * sig * (1.0 + gate * (1.0 - sig))).astype(BF16)
-    grad_sup[...] = (grad_act * gate * sig).astype(BF16)
     out_s = dot(sact[...], sd[...])
     note_s = jnp.sum(out_s * g[...].astype(F32), axis=-1, keepdims=True)
     y[...] = (out + sigma * out_s).astype(BF16)
-    back = back.astype(F32) + dot(grad_sgate[...], sg[...]) + dot(grad_sup[...], su[...])
-    dx[:, :D] = back.astype(BF16)
-    lane = lax.broadcasted_iota(jnp.int32, (rows.shape[0], dx.shape[1] - D), 1)
-    notes = jnp.zeros(lane.shape, F32)
+    lane = lax.broadcasted_iota(jnp.int32, notes.shape, 1)
+    total = jnp.zeros(notes.shape, F32)
     i = 0
     for value in (note_e, note_s):
         for _ in range(3):
             part = value.astype(BF16).astype(F32)
-            notes = jnp.where(lane == i * N + f, part, notes)
+            total = jnp.where(lane == i * N + f, part, total)
             value = value - part
             i += 1
-    dx[:, D:] = notes.astype(BF16)
-
-
-def experts(N, E, x, g, picked, lead, weights):
-    rows, D = x.shape
+    notes[...] = total.astype(BF16)
+
+
+def experts_backward_kernel(*refs):
+    notes, geo, gso, gate_i, up_i, sgate_i, sup_i, *refs = refs
+    weights, refs = refs[:6], refs[6:]
+    dx, grad_gate, grad_up, grad_sgate, grad_sup, *refs = refs
+    eg, eu, sg, su, ed, sd = refs[:6]
+    need = hold(weights, refs[:6], refs[6], (4, 0, 1, 5, 2, 3))
+    D = geo.shape[1]
+
+    def local(grad_act, gate, up, gate_grad, up_grad):
+        sig = jax.nn.sigmoid(gate[...])
+        gate_grad[...] = (grad_act * up[...] * sig * (1.0 + gate[...] * (1.0 - sig))).astype(BF16)
+        up_grad[...] = (grad_act * gate[...] * sig).astype(BF16)
+
+    need(4)
+    local(dot_nt(geo[...], ed[...]), gate_i, up_i, grad_gate, grad_up)
+    need(0)
+    need(1)
+    back = (dot_nt(grad_gate[...], eg[...]) + dot_nt(grad_up[...], eu[...])).astype(BF16)
+    need(5)
+    local(dot_nt(gso[...], sd[...]), sgate_i, sup_i, grad_sgate, grad_sup)
+    need(2)
+    need(3)
+    back = back.astype(F32) + dot(grad_sgate[...], sg[...]) + dot(grad_sup[...], su[...])
+    dx[:, :D] = back.astype(BF16)
+    dx[:, D:] = notes[...]
+
+
+def experts_call(kernel, name, arrays, whole, weights, outs, products):
+    rows = arrays[0].shape[0]
     tile = 256
-    FE, FS = weights[0].shape[1], weights[2].shape[0]
-    wide = D + 6 * N + -(6 * N) % 128
-    columns = (D, wide, D, D, FE, FE, FS, FS, FE, FS)
-    once = dict(pipeline_mode=pl.Buffered(1))
+    units = weights[0].shape[1] + weights[2].shape[0]
     return pl.pallas_call(
-        functools.partial(experts_kernel, N, E),
+        kernel,
         grid=(rows // tile,),
-        out_shape=[jax.ShapeDtypeStruct((rows, c), BF16) for c in columns],
-        in_specs=[pl.BlockSpec((tile, c), lambda i: (i, 0)) for c in (D, D, 1)]
-        + [pl.BlockSpec(lead.shape, lambda i: (0, 0), **once)] + [pl.BlockSpec(memory_space=pl.ANY)] * 6,
-        out_specs=[pl.BlockSpec((tile, c), lambda i: (i, 0)) for c in columns],
+        out_shape=[jax.ShapeDtypeStruct((rows, c), t) for c, t in outs],
+        in_specs=[pl.BlockSpec((tile, u.shape[1]), lambda i: (i, 0)) for u in arrays]
+        + [pl.BlockSpec(u.shape, lambda i: (0, 0), pipeline_mode=pl.Buffered(1)) for u in whole]
+        + [pl.BlockSpec(memory_space=pl.ANY)] * 6,
+        out_specs=[pl.BlockSpec((tile, c), lambda i: (i, 0)) for c, _ in outs],
         scratch_shapes=[pltpu.VMEM(w.shape, BF16) for w in weights] + [pltpu.SemaphoreType.DMA((6,))],
-        compiler_params=pltpu.CompilerParams(
-            dimension_semantics=("arbitrary",), vmem_limit_bytes=VMEM_LIMIT
+        compiler_params=pltpu.CompilerParams(dimension_semantics=("arbitrary",), vmem_limit_bytes=VMEM_LIMIT),
+        cost_estimate=pl.CostEstimate(
+            flops=2 * products * rows * arrays[1].shape[1] * units, bytes_accessed=16 * rows * (units + 2048),
+            transcendentals=rows * units,
         ),
-        cost_estimate=pl.CostEstimate(
-            flops=12 * rows * D * (FE + FS), bytes_accessed=40 * rows * D, transcendentals=rows * (FE + FS)
-        ),
-        name="experts",
-    )(x, g, picked, lead, *weights)
+        name=name,
+    )(*arrays, *whole, *weights)
+
+
+def experts_forward(N, E, x, g, picked, lead, weights):
+    D, FE, FS = x.shape[1], weights[0].shape[1], weights[2].shape[0]
+    outs = [(D, BF16), (6 * N + -(6 * N) % 128, BF16), (D, BF16), (D, BF16)]
+    outs += [(c, F32) for c in (FE, FE, FS, FS)] + [(FE, BF16), (FS, BF16)]
+    kernel = functools.partial(experts_forward_kernel, N, E)
+    return experts_call(kernel, "experts_forward", (x, g, picked), (lead,), weights, outs, 3)
+
+
+def experts_backward(arrays, weights):
+    D, FE, FS = arrays[1].shape[1], weights[0].shape[1], weights[2].shape[0]
+    outs = [(c, BF16) for c in (D + arrays[0].shape[1], FE, FE, FS, FS)]
+    return experts_call(experts_backward_kernel, "experts_backward", arrays, (), weights, outs, 3)
 
 
 def backward_kernel(S, N, sizes, *refs):
@@ -1000,9 +1032,12 @@
     lead = jnp.concatenate([router_w, shared_w[:, None]], axis=1)
     lead_order = jnp.take(lead.reshape(8, D // 8, E + 1), order, axis=0).reshape(D, E + 1)
     picked_rows = jnp.any(chosen == f, axis=1, keepdims=True).astype(F32)
-    y, dx, geo, gso, grad_gate, grad_up, grad_sgate, grad_sup, act, sact = experts(
+    y, *saved, act, sact = experts_forward(
         N, E, x, g_rows, picked_rows, jnp.pad(lead_order, ((0, 0), (0, 127 - E))), fulls
     )
+    y = lax.psum_scatter(y, "fsdp", scatter_dimension=0, tiled=True)
+    geo, gso = saved[1:3]
+    dx, grad_gate, grad_up, grad_sgate, grad_sup = experts_backward(saved, fulls)
     dx = lax.psum_scatter(dx, "fsdp", scatter_dimension=0, tiled=True)
 
     half = D // 8
@@ -1018,8 +1053,7 @@
         return dot_t(x[:, cut], grad_gate).astype(BF16), dot_t(x[:, cut], grad_up).astype(BF16)
 
     by_x, by_y = jnp.concatenate(by_columns(cuts[0])), jnp.concatenate(by_columns(cuts[1]))
-    x, y, by_x, by_y = lax.optimization_barrier((x, y, by_x, by_y))
-    y = lax.psum_scatter(y, "fsdp", scatter_dimension=0, tiled=True)
+    x, by_x, by_y = lax.optimization_barrier((x, by_x, by_y))
     from_x, from_y = across(by_x, 1), across(by_y, 2)
     to_x, to_y = by_rows(cuts[0]), by_rows(cuts[1])
     keep = by_rows(cuts[2]) + by_columns(cuts[2])

time: 967 us -> 940 us (0.972)
  waiting for transfers between devices: 50.6 us -> 0.06 us
  Pallas kernels: 689 us -> 699 us
    reduce_scatter x1, waiting for transfers between devices: 50.3 us -> 0.01 us  [shards(): dx = lax.psum_scatter(dx, 'fsdp', scatter_dimension=0, tiled=True)]
    pallas_call x1 -> x2, Pallas kernels: 125 us -> 135 us  [experts_call(): pl.pallas_call(kernel, grid=(rows // tile,), out_shape=[jax.ShapeDtypeStr...]
  transfers between devices with their start and end apart: 4 -> 4, of which waited for: 1 -> 0; matrix products, arithmetic and copies ran while one was open for 9% -> 11% of each run, Pallas kernels for 0% -> 7%
where the time goes in v6:
time: 940 us; the launch traced here: 929 us
  Pallas kernels  699 us (74%)
  local copies, waits for them, and re-layouts  88.2 us (9%)
  matrix products  76.9 us (8%)
  other arithmetic  47.1 us (5%)
  between operations  15.8 us (2%)
    pallas_call x1, Pallas kernels, forward(): pl.pallas_call(functools.partial(forward_kernel, S, N, (MB, pr // MB, D,...  328 us
    pallas_call x1, Pallas kernels, backward(): pl.pallas_call(functools.partial(backward_kernel, S, N, (D, own, heads)),...  237 us
    pallas_call x2, Pallas kernels, experts_call(): pl.pallas_call(kernel, grid=(rows // tile,), out_shape=[jax.ShapeDtypeStr...  135 us
    dot_general x19, matrix products, dot_t(): lax.dot_general(a, b, (((0,), (0,)), ((), ())), preferred_element_type=F32)  74.7 us
  transfers between devices with their start and end apart: 4, of which 0 were waited for; matrix products, arithmetic and copies ran while one was open for 11% of the time, Pallas kernels for 7%

profile of v6, /device:TPU:0, one launch (start us, length us, event | category | flops | bytes accessed | tf_op | source)
XLA Modules:
  0.0 929.1 jit_solution(17771808339610927164)
XLA Ops:
  20.5 2.3 reshape.835
  35.8 327.9 %forward.1 = (bf16[8,24,2048]{2,1,0:T(8,128)(2,1)}, bf16[8,8,24,2048]{3,2,1,0:T(8,128)(2,1)}, bf16[4,8,64,1536]{3,2,1,0:T(8,128)(2,1)}, bf16[8,64,2048]{2,1,0:T(...) custom-call(bf16[8,24,2048]{2,1,0:T(8,128)(2,1)} %copy.454.refs_0_, ...), custom_call_target="tpu_custom_call" | custom-call | tf_op jit(solution)/shard_map/forward/pallas_call | solution.py:435
  373.8 69.7 %experts_forward.1 = (bf16[1536,2048]{1,0:T(8,128)(2,1)}, bf16[1536,128]{1,0:T(8,128)(2,1)}, bf16[1536,2048]{1,0:T(8,128)(2,1)}, bf16[1536,2048]{1,0:T(8,128)(2,...) custom-call(bf16[1536,2048]{1,0:T(8,128)(2,1)} %bitcast.291, ...), custom_call_target="tpu_custom_call" | custom-call | flops 39862665216 | bytes 102236160 | tf_op jit(solution)/shard_map/experts_forward/pallas_call | solution.py:554
  443.6 64.9 %experts_backward.1 = (bf16[1536,2176]{1,0:T(8,128)(2,1)}, bf16[1536,1408]{1,0:T(8,128)(2,1)}, bf16[1536,1408]{1,0:T(8,128)(2,1)}, bf16[1536,704]{1,0:T(8,128)(2,1)}, bf16[1536,704]{1,0:T(8,128)(2,1)}) custom-call(bf16[1536,128]{1,0:T(8,128)(2,1)} %get-tuple-element.99.refs_0_, bf16[1536,2048]{1,0:T(8,128)(2,1)} %get-tuple-element.100.refs_1_, ...), custom_call_target="tpu_custom_call" | custom-call | flops 39862665216 | bytes 102236160 | tf_op jit(solution)/shard_map/experts_backward/pallas_call | solution.py:554
  508.6 3.7 fusion.43
  512.3 2.9 fusion.37
  517.9 2.9 slice-done.5
  523.1 2.5 convolution_convert_fusion.7
  528.9 2.5 convolution_convert_fusion.8
  531.4 2.4 pad_maximum_fusion
  541.6 3.1 bitcast_multiply_fusion.refs_18_
  544.7 5.7 fusion.16.refs_11_
  550.4 3.6 fusion.10.refs_8_
  554.0 3.6 fusion.13.refs_9_
  557.6 3.8 convolution_convert_fusion.5.refs_1_
  561.4 3.8 convolution_convert_fusion.3.refs_3_
  565.2 3.8 convolution_convert_fusion.4.refs_2_
  569.0 3.9 convolution_convert_fusion.6.refs_0_
  581.9 9.6 %convolution_convert_fusion.refs_10_ = bf16[1408,1024]{1,0:T(8,128)(2,1)} fusion(bf16[1536,1408]{1,0:T(8,128)(2,1)} %get-tuple-element.109, bf16[1536,2048]{1,0:T(8,128)(2,1)} %get-tuple-element.100.refs_1_), kind=kOutput, calls=%fused_computation.15 | convolution fusion | flops 4430626816 | bytes 10354688 | tf_op jit(solution)/shard_map/dot_general | solution.py:29
  591.5 9.1 convolution_convert_fusion.1.refs_7_
  600.6 9.5 %convolution_convert_fusion.2.refs_6_ = bf16[1024,1408]{1,0:T(8,128)(2,1)} fusion(bf16[1536,1408]{1,0:T(8,128)(2,1)} %get-tuple-element.114, bf16[1536,2048]{1,0:T(8,128)(2,1)} %bitcast.295), kind=kOutput, calls=%fused_computation.17 | convolution fusion | flops 4430626816 | bytes 10354688 | tf_op jit(solution)/shard_map/dot_general | solution.py:29
  610.1 2.1 copy.543
  612.2 2.6 gather_fusion.8
  624.0 3.2 gather_fusion.2
  631.6 1.9 multiply_reduce_fusion.1
  637.5 3.9 multiply_add_fusion
  641.3 236.8 %backward.1 = (bf16[8,24,2048]{2,1,0:T(8,128)(2,1)}, bf16[8,24,2048]{2,1,0:T(8,128)(2,1)}, bf16[4,64,1536]{2,1,0:T(8,128)(2,1)}, f32[64,2048]{1,0:T(8,128)}, f32...) custom-call(bf16[512,1408]{1,0:T(8,128)(2,1)} %convolution_convert_f, ...), custom_call_target="tpu_custom_call" | custom-call | tf_op jit(solution)/shard_map/backward/pallas_call | solution.py:903
  892.7 2.2 copy.499
  894.9 3.6 reshape.863
  898.5 2.3 convert_add_fusion.1
  900.9 1.9 maximum_bitcast_fusion.2
  904.5 2.4 convert_add_fusion.6
  (350 shorter events, 109.5 us)
Async XLA Ops:
  7.2 11.1 %copy-start.17 = (bf16[2,96,2048]{2,1,0:T(8,128)(2,1)S(1)}, bf16[2,96,2048]{2,1,0:T(8,128)(2,1)}, u32[]{:S(2)}) copy-start(bf16[2,96,2048]{2,1,0:T(8,128)(2,1)} %param.25) | copy-start | bytes 2359300
  7.2 602.9 %reduce-scatter.5.cloned.1.call-start = ((), (), s32[]{:S(2)}) async-start(), calls=%async_computation.3 | async-start | bytes 7077888 | tf_op jit(solution)/shard_map/reduce_scatter | solution.py:1038
  443.6 176.5 %reduce-scatter.3.cloned.1.call-start = ((), (), s32[]{:S(2)}) async-start(), calls=%async_computation.2 | async-start | bytes 7520256 | tf_op jit(solution)/shard_map/reduce_scatter | solution.py:1041
  508.5 13.6 %slice-start.12 = ((s8[4325376]{0:T(1024)(128)(4,1)}), s8[131072]{0:T(1024)(128)(4,1)S(1)}, s32[]{:S(2)}) async-start(s8[4325376]{0:T(1024)(128)(4,1)} %bitcast.335), calls=%async_computation.16 | async-start | bytes 262144
  508.6 3.7 copy-start.40
  508.6 6.6 slice-start
  515.2 6.9 slice-start.13
  516.6 4.3 slice-start.5
  516.6 4.2 copy-start.36
  516.6 5.6 slice-start.6
  531.4 5.3 copy-start.12
  533.8 6.2 copy-start.2
  533.8 86.2 %collective-permute-start = (bf16[3520,512]{1,0:T(8,128)(2,1)}, bf16[3520,512]{1,0:T(8,128)(2,1)}, u32[]{:S(2)}, u32[]{:S(2)}) collective-permute-start(bf16[3520,512]{1,0:T(8,128)(2,1)} %pad_maximum_fusion), channel_id=1, source_target_pairs={{0,8},{8,0},{16,24},{24,16},{1,9},{9,1},{17,25},{25,17},{2,10},{10... | collective-permute-start | bytes 10813448 | tf_op jit(solution)/shard_map/ppermute | solution.py:58
  535.4 84.6 %collective-permute-start.1 = (bf16[3520,512]{1,0:T(8,128)(2,1)}, bf16[3520,512]{1,0:T(8,128)(2,1)}, u32[]{:S(2)}, u32[]{:S(2)}) collective-permute-start(bf16[3520,512]{1,0:T(8,128)(2,1)} %pad_maximum_fusion.1), channel_id=1, source_target_pairs={{0,16},{8,24},{16,0},{24,8},{1,17},{9,25},{17,1},{25,9},{2,18},{10... | collective-permute-start | bytes 10813448 | tf_op jit(solution)/shard_map/ppermute | solution.py:58
  540.0 4.7 copy-start.37
  540.0 10.4 %slice-start.2 = ((s8[6291456]{0:T(1024)(128)(4,1)}), s8[4194304]{0:T(1024)(128)(4,1)S(1)}, s32[]{:S(2)}) async-start(s8[6291456]{0:T(1024)(128)(4,1)} %bitcast.300), calls=%async_computation.6 | async-start | bytes 8388608
  544.7 5.7 slice-start.3
  544.7 5.7 copy-start.41
  550.4 7.2 slice-start.10
  557.6 7.6 slice-start.8
  561.4 3.8 slice-start.9
  627.3 4.4 copy-start.13
  633.6 3.9 copy-start.7
  878.1 5.9 copy-start.35
  879.7 4.8 copy-start.18
  898.5 4.3 copy-start.33
  898.5 4.3 copy-start.34
  904.4 3.7 copy-start.22
  904.4 3.7 copy-start.23
  904.5 3.7 copy-start.27
  904.5 3.7 copy-start.28
  909.8 3.8 copy-start.25
  (28 other events, 79.9 us)
Sparse Core Ops, SparseCore 0:
  443.7 68.1 reduce-scatter.4
  514.2 71.8 reduce-scatter.2

commit v7 on v6

--- a/solution.py
+++ b/solution.py
@@ -348,9 +348,6 @@
     lax.fori_loop(0, heads, attend, 0)
     for step in range(1, chips - 1):
         g_line.step(step)
-        if step == 1:
-            give(3)
-            give(5)
 
     wb = wb_v[...].reshape(width, D)
     exchange = []
@@ -359,7 +356,6 @@
         part_send[k] = dot(ctx_v[rows, :], wb).astype(BF16)
         exchange.append(remote(part_send.at[k], part_recv.at[k], part_sems.at[k], part_semr.at[k], (other, f)))
         exchange[-1].start()
-    pass_on(4)
     hid_v[...] = x_v[...] + dot(ctx_v[pl.ds(pl.multiple_of(s * L, L), L), :], wb)
     outs = [
         (tok_v, x_rows), (w_v, w_in), (wb_v, w_back), (small_v, small_all), (na_v, normed_out), (qkv_v, qkv_out),
@@ -369,6 +365,8 @@
     for k in range(3):
         exchange[k].wait_recv()
         hid_v[...] += part_recv[k].astype(F32)
+    give(3)
+    give(5)
     hidden = hid_v[...]
     inverse = lax.rsqrt(jnp.mean(hidden * hidden, axis=-1, keepdims=True) + EPS)
     n2_v[...] = (hidden * inverse * gain_v[1:2, :]).astype(BF16)
@@ -379,6 +377,7 @@
     outs[8].start()
     outs[8].wait()
     x_line.begin()
+    pass_on(4)
     pass_on(2)
     for step in range(chips - 1):
         x_line.step(step)

time: 940 us -> 910 us (0.968)
  Pallas kernels: 699 us -> 670 us
    pallas_call x1, Pallas kernels: 328 us -> 299 us  [forward(): pl.pallas_call(functools.partial(forward_kernel, S, N, (MB, pr // MB, D,...]
  transfers between devices with their start and end apart: 4 -> 4, of which waited for: 0 -> 0; matrix products, arithmetic and copies ran while one was open for 11% -> 12% of each run, Pallas kernels for 7% -> 7%
where the time goes in v7:
time: 910 us; the launch traced here: 900 us
  Pallas kernels  670 us (74%)
  local copies, waits for them, and re-layouts  88.2 us (10%)
  matrix products  76.9 us (8%)
  other arithmetic  47.1 us (5%)
  between operations  15.8 us (2%)
    pallas_call x1, Pallas kernels, forward(): pl.pallas_call(functools.partial(forward_kernel, S, N, (MB, pr // MB, D,...  299 us
    pallas_call x1, Pallas kernels, backward(): pl.pallas_call(functools.partial(backward_kernel, S, N, (D, own, heads)),...  237 us
    pallas_call x2, Pallas kernels, experts_call(): pl.pallas_call(kernel, grid=(rows // tile,), out_shape=[jax.ShapeDtypeStr...  135 us
    dot_general x19, matrix products, dot_t(): lax.dot_general(a, b, (((0,), (0,)), ((), ())), preferred_element_type=F32)  74.7 us
  transfers between devices with their start and end apart: 4, of which 0 were waited for; matrix products, arithmetic and copies ran while one was open for 12% of the time, Pallas kernels for 7%

profile of v7, /device:TPU:0, one launch (start us, length us, event | category | flops | bytes accessed | tf_op | source)
XLA Modules:
  0.0 900.0 jit_solution(4059531520604607052)
XLA Ops:
  20.5 2.3 reshape.835
  35.8 298.7 %forward.1 = (bf16[8,24,2048]{2,1,0:T(8,128)(2,1)}, bf16[8,8,24,2048]{3,2,1,0:T(8,128)(2,1)}, bf16[4,8,64,1536]{3,2,1,0:T(8,128)(2,1)}, bf16[8,64,2048]{2,1,0:T(...) custom-call(bf16[8,24,2048]{2,1,0:T(8,128)(2,1)} %copy.454.refs_0_, ...), custom_call_target="tpu_custom_call" | custom-call | tf_op jit(solution)/shard_map/forward/pallas_call | solution.py:434
  344.7 69.7 %experts_forward.1 = (bf16[1536,2048]{1,0:T(8,128)(2,1)}, bf16[1536,128]{1,0:T(8,128)(2,1)}, bf16[1536,2048]{1,0:T(8,128)(2,1)}, bf16[1536,2048]{1,0:T(8,128)(2,...) custom-call(bf16[1536,2048]{1,0:T(8,128)(2,1)} %bitcast.291, ...), custom_call_target="tpu_custom_call" | custom-call | flops 39862665216 | bytes 102236160 | tf_op jit(solution)/shard_map/experts_forward/pallas_call | solution.py:553
  414.5 64.9 %experts_backward.1 = (bf16[1536,2176]{1,0:T(8,128)(2,1)}, bf16[1536,1408]{1,0:T(8,128)(2,1)}, bf16[1536,1408]{1,0:T(8,128)(2,1)}, bf16[1536,704]{1,0:T(8,128)(2,1)}, bf16[1536,704]{1,0:T(8,128)(2,1)}) custom-call(bf16[1536,128]{1,0:T(8,128)(2,1)} %get-tuple-element.99.refs_0_, bf16[1536,2048]{1,0:T(8,128)(2,1)} %get-tuple-element.100.refs_1_, ...), custom_call_target="tpu_custom_call" | custom-call | flops 39862665216 | bytes 102236160 | tf_op jit(solution)/shard_map/experts_backward/pallas_call | solution.py:553
  479.5 3.7 fusion.43
  483.1 2.9 fusion.37
  488.8 2.9 slice-done.5
  494.0 2.5 convolution_convert_fusion.7
  499.7 2.5 convolution_convert_fusion.8
  502.3 2.4 pad_maximum_fusion
  512.5 3.1 bitcast_multiply_fusion.refs_18_
  515.6 5.7 fusion.16.refs_11_
  521.3 3.6 fusion.10.refs_8_
  524.9 3.6 fusion.13.refs_9_
  528.5 3.8 convolution_convert_fusion.5.refs_1_
  532.2 3.8 convolution_convert_fusion.3.refs_3_
  536.1 3.8 convolution_convert_fusion.4.refs_2_
  539.9 3.9 convolution_convert_fusion.6.refs_0_
  552.8 9.6 %convolution_convert_fusion.refs_10_ = bf16[1408,1024]{1,0:T(8,128)(2,1)} fusion(bf16[1536,1408]{1,0:T(8,128)(2,1)} %get-tuple-element.109, bf16[1536,2048]{1,0:T(8,128)(2,1)} %get-tuple-element.100.refs_1_), kind=kOutput, calls=%fused_computation.15 | convolution fusion | flops 4430626816 | bytes 10354688 | tf_op jit(solution)/shard_map/dot_general | solution.py:29
  562.3 9.1 %convolution_convert_fusion.1.refs_7_ = bf16[1024,1408]{1,0:T(8,128)(2,1)} fusion(bf16[1536,1408]{1,0:T(8,128)(2,1)} %get-tuple-element.115, bf16[1536,2048]{1,0:T(8,128)(2,1)} %bitcast.294), kind=kOutput, calls=%fused_computation.16 | convolution fusion | flops 4430626816 | bytes 10354688 | tf_op jit(solution)/shard_map/dot_general | solution.py:29
  571.4 9.5 %convolution_convert_fusion.2.refs_6_ = bf16[1024,1408]{1,0:T(8,128)(2,1)} fusion(bf16[1536,1408]{1,0:T(8,128)(2,1)} %get-tuple-element.114, bf16[1536,2048]{1,0:T(8,128)(2,1)} %bitcast.295), kind=kOutput, calls=%fused_computation.17 | convolution fusion | flops 4430626816 | bytes 10354688 | tf_op jit(solution)/shard_map/dot_general | solution.py:29
  581.0 2.1 copy.543
  583.0 2.6 gather_fusion.8
  594.9 3.2 gather_fusion.2
  602.5 1.9 multiply_reduce_fusion.1
  608.3 3.9 multiply_add_fusion
  612.2 236.8 %backward.1 = (bf16[8,24,2048]{2,1,0:T(8,128)(2,1)}, bf16[8,24,2048]{2,1,0:T(8,128)(2,1)}, bf16[4,64,1536]{2,1,0:T(8,128)(2,1)}, f32[64,2048]{1,0:T(8,128)}, f32...) custom-call(bf16[512,1408]{1,0:T(8,128)(2,1)} %convolution_convert_f, ...), custom_call_target="tpu_custom_call" | custom-call | tf_op jit(solution)/shard_map/backward/pallas_call | solution.py:902
  863.6 2.2 copy.499
  865.7 3.6 reshape.863
  869.3 2.3 convert_add_fusion.1
  871.7 1.9 maximum_bitcast_fusion.2
  875.3 2.4 convert_add_fusion.6
  (350 shorter events, 109.5 us)
Async XLA Ops:
  7.2 11.1 %copy-start.17 = (bf16[2,96,2048]{2,1,0:T(8,128)(2,1)S(1)}, bf16[2,96,2048]{2,1,0:T(8,128)(2,1)}, u32[]{:S(2)}) copy-start(bf16[2,96,2048]{2,1,0:T(8,128)(2,1)} %param.25) | copy-start | bytes 2359300
  7.2 573.8 %reduce-scatter.5.cloned.1.call-start = ((), (), s32[]{:S(2)}) async-start(), calls=%async_computation.3 | async-start | bytes 7077888 | tf_op jit(solution)/shard_map/reduce_scatter | solution.py:1037
  414.4 176.5 %reduce-scatter.3.cloned.1.call-start = ((), (), s32[]{:S(2)}) async-start(), calls=%async_computation.2 | async-start | bytes 7520256 | tf_op jit(solution)/shard_map/reduce_scatter | solution.py:1040
  479.4 13.6 %slice-start.12 = ((s8[4325376]{0:T(1024)(128)(4,1)}), s8[131072]{0:T(1024)(128)(4,1)S(1)}, s32[]{:S(2)}) async-start(s8[4325376]{0:T(1024)(128)(4,1)} %bitcast.335), calls=%async_computation.16 | async-start | bytes 262144
  479.4 3.7 copy-start.40
  479.4 6.6 slice-start
  486.1 6.9 slice-start.13
  487.4 4.3 slice-start.5
  487.4 4.2 copy-start.36
  487.4 5.6 slice-start.6
  502.2 5.3 copy-start.12
  504.7 6.2 copy-start.2
  504.7 86.2 %collective-permute-start = (bf16[3520,512]{1,0:T(8,128)(2,1)}, bf16[3520,512]{1,0:T(8,128)(2,1)}, u32[]{:S(2)}, u32[]{:S(2)}) collective-permute-start(bf16[3520,512]{1,0:T(8,128)(2,1)} %pad_maximum_fusion), channel_id=1, source_target_pairs={{0,8},{8,0},{16,24},{24,16},{1,9},{9,1},{17,25},{25,17},{2,10},{10... | collective-permute-start | bytes 10813448 | tf_op jit(solution)/shard_map/ppermute | solution.py:58
  506.2 84.7 %collective-permute-start.1 = (bf16[3520,512]{1,0:T(8,128)(2,1)}, bf16[3520,512]{1,0:T(8,128)(2,1)}, u32[]{:S(2)}, u32[]{:S(2)}) collective-permute-start(bf16[3520,512]{1,0:T(8,128)(2,1)} %pad_maximum_fusion.1), channel_id=1, source_target_pairs={{0,16},{8,24},{16,0},{24,8},{1,17},{9,25},{17,1},{25,9},{2,18},{10... | collective-permute-start | bytes 10813448 | tf_op jit(solution)/shard_map/ppermute | solution.py:58
  510.9 4.7 copy-start.37
  510.9 10.4 %slice-start.2 = ((s8[6291456]{0:T(1024)(128)(4,1)}), s8[4194304]{0:T(1024)(128)(4,1)S(1)}, s32[]{:S(2)}) async-start(s8[6291456]{0:T(1024)(128)(4,1)} %bitcast.300), calls=%async_computation.6 | async-start | bytes 8388608
  515.6 5.7 slice-start.3
  515.6 5.7 copy-start.41
  521.3 7.2 slice-start.10
  528.5 7.6 slice-start.8
  532.2 3.8 slice-start.9
  598.1 4.4 copy-start.13
  604.5 3.9 copy-start.7
  849.0 5.9 copy-start.35
  850.5 4.8 copy-start.18
  869.3 4.3 copy-start.33
  869.3 4.3 copy-start.34
  875.3 3.7 copy-start.22
  875.3 3.7 copy-start.23
  875.3 3.7 copy-start.27
  875.3 3.7 copy-start.28
  880.7 3.8 copy-start.25
  (28 other events, 79.9 us)
Sparse Core Ops, SparseCore 0:
  414.6 68.1 reduce-scatter.4
  485.0 71.8 reduce-scatter.2
